TPU v7x, 32 devices: a whole 2x2x4 slice. The times are simulated.
32 devices in a mesh: seq: 8 (over z, core), grp: 4 (over y, x).
Axes of the slice: x: 2, y: 2, z: 4, core: 2. Of those that a mesh axis runs over, the one named last changes fastest.
Arguments:
- tokens: bfloat16 [2, 2048, 2048], P(None, ('seq', 'grp')), may hold values from -6 to 6
- lengths: int32 [2], replicated, may hold values from 1 to 2048, as said below
- attn_gain: float32 [2048], P(('seq', 'grp')), may hold values from 0.5 to 1.5
- w_query: bfloat16 [2048, 2048], P('seq', 'grp'), may hold values from -0.125 to 0.125
- w_key: bfloat16 [2048, 1024], P('seq', 'grp'), may hold values from -0.125 to 0.125
- w_value: bfloat16 [2048, 1024], P('seq', 'grp'), may hold values from -0.125 to 0.125
- query_gain: float32 [128], replicated, may hold values from 1 to 2
- key_gain: float32 [128], replicated, may hold values from 1 to 2
- w_out: bfloat16 [2048, 2048], P('grp', 'seq'), may hold values from -0.75 to 0.75
- mlp_gain: float32 [2048], P(('seq', 'grp')), may hold values from 0.5 to 1.5
- w_gate: bfloat16 [2048, 6144], P('seq', 'grp'), may hold values from -0.125 to 0.125
- w_up: bfloat16 [2048, 6144], P('seq', 'grp'), may hold values from -0.125 to 0.125
- w_down: bfloat16 [6144, 2048], P('grp', 'seq'), may hold values from -0.078125 to 0.078125
- cotangent: bfloat16 [2, 2048, 2048], P(None, ('seq', 'grp')), may hold values from -6 to 6
Outputs:
- output: bfloat16 [2, 2048, 2048], P(None, ('seq', 'grp'))
- grad_tokens: float32 [2, 2048, 2048], P(None, ('seq', 'grp'))
- grad_attn_gain: float32 [2048], P(('seq', 'grp'))
- grad_w_query: float32 [2048, 2048], P('seq', 'grp')
- grad_w_key: float32 [2048, 1024], P('seq', 'grp')
- grad_w_value: float32 [2048, 1024], P('seq', 'grp')
- grad_query_gain: float32 [128], replicated
- grad_key_gain: float32 [128], replicated
- grad_w_out: float32 [2048, 2048], P('grp', 'seq')
- grad_mlp_gain: float32 [2048], P(('seq', 'grp'))
- grad_w_gate: float32 [2048, 6144], P('seq', 'grp')
- grad_w_up: float32 [2048, 6144], P('seq', 'grp')
- grad_w_down: float32 [6144, 2048], P('grp', 'seq')
Inputs may be any that keep to these rules, and one draw needn't show every extreme that they name: `lengths`: each row holds 1 to 2048 valid tokens followed by padding; one of the two rows, drawn from the seed, is full.
All inputs are finite; a program needn't handle non-finite values.
Results may differ from a plain program's by a relative error of at most 0.025.
Values may be sent and summed in bfloat16 or wider, within the bound.
A program may use at most 128 MiB of HBM per device.

v0:
```python
from functools import partial
import math

import jax
import jax.numpy as jnp
from jax import lax
from jax.sharding import PartitionSpec as P

EPSILON = 1e-06
ROPE_BASE = 1000000.0
NEGATIVE = -1e30


def from_behind(x, axis, by):
    size = lax.axis_size(axis)
    pairs = [(i, i + by) for i in range(size) if 0 <= i + by < size]
    return lax.ppermute(x, axis, pairs)


def from_behind_2(x, axis, by):
    size = lax.axis_size(axis)
    return lax.ppermute(x, axis, [(i, (i + by) % size) for i in range(size)])


def normalize(values):
    inverse = lax.rsqrt(jnp.mean(values * values, axis=-1, keepdims=True) + EPSILON)
    return (values * inverse, inverse)


def norm_back(gradient, unit_values, inverse):
    return inverse * (
        gradient - unit_values * jnp.mean(gradient * unit_values, axis=-1, keepdims=True)
    )


def turn_half(values):
    half_dim = values.shape[-1] // 2
    return jnp.concatenate([-values[..., half_dim:], values[..., :half_dim]], axis=-1)


def angle_tables(positions, head_dim):
    half_dim = head_dim // 2
    frequency = ROPE_BASE ** (-jnp.arange(half_dim, dtype=jnp.float32) * 2.0 / head_dim)
    angles = positions.astype(jnp.float32)[:, None] * frequency[None, :]
    cosine = jnp.concatenate([jnp.cos(angles), jnp.cos(angles)], axis=-1)
    sine_table = jnp.concatenate([jnp.sin(angles), jnp.sin(angles)], axis=-1)
    return (cosine[None, :, None, :], sine_table[None, :, None, :])


def keep_state(state):
    return state


def to_group(rows_local):
    return lax.all_gather(rows_local, "grp", axis=1, tiled=True)


def to_rows(partial_sums):
    return lax.psum_scatter(
        partial_sums.astype(jnp.bfloat16), "grp", scatter_dimension=1, tiled=True
    ).astype(jnp.float32)


def move_keys(key_block):
    return from_behind(key_block, "seq", 1)


def move_pair(kv_block):
    return from_behind(kv_block, "seq", 1)


def move_grads(grad_block):
    return from_behind_2(grad_block.astype(jnp.bfloat16), "seq", 1).astype(grad_block.dtype)


def shards(
    tokens,
    lengths,
    attn_gain,
    w_query,
    w_key,
    w_value,
    query_gain,
    key_gain,
    w_out,
    mlp_gain,
    w_gate,
    w_up,
    w_down,
    cotangent,
):
    cycle_size = lax.axis_size("seq")
    group_size = lax.axis_size("grp")
    seq_index = lax.axis_index("seq")
    grp_index = lax.axis_index("grp")
    local_rows = tokens.shape[1]
    block_rows = local_rows * group_size
    half_rows = block_rows // 2
    head_dim = query_gain.shape[0]
    score_scale = 1.0 / math.sqrt(head_dim)
    gain_attn, gain_mlp = (
        lax.all_gather(attn_gain, ("seq", "grp"), axis=0, tiled=True),
        lax.all_gather(mlp_gain, ("seq", "grp"), axis=0, tiled=True),
    )
    full_query, full_key, full_value, full_out = (
        lax.all_gather(w_query, "seq", axis=0, tiled=True),
        lax.all_gather(w_key, "seq", axis=0, tiled=True),
        lax.all_gather(w_value, "seq", axis=0, tiled=True),
        lax.all_gather(w_out, "seq", axis=1, tiled=True),
    )
    full_gate, full_up, full_down = (
        lax.all_gather(w_gate, "seq", axis=0, tiled=True),
        lax.all_gather(w_up, "seq", axis=0, tiled=True),
        lax.all_gather(w_down, "seq", axis=1, tiled=True),
    )
    query_heads = full_query.shape[1] // head_dim
    key_heads = full_key.shape[1] // head_dim
    repeat = query_heads // key_heads
    residual = tokens.astype(jnp.float32)
    attn_unit, attn_inverse = normalize(residual)
    attn_rows = to_group((attn_unit * gain_attn).astype(jnp.bfloat16))
    query_raw = jnp.einsum(
        "bsd,dc->bsc", attn_rows, full_query, preferred_element_type=jnp.float32
    ).reshape(2, block_rows, query_heads, head_dim)
    key_raw = jnp.einsum(
        "bsd,dc->bsc", attn_rows, full_key, preferred_element_type=jnp.float32
    ).reshape(2, block_rows, key_heads, head_dim)
    value_raw = jnp.einsum("bsd,dc->bsc", attn_rows, full_value, preferred_element_type=jnp.float32)
    positions = seq_index * block_rows + jnp.arange(block_rows, dtype=jnp.int32)
    cosine, sine_table = angle_tables(positions, head_dim)
    query_unit, query_inverse = normalize(query_raw)
    query_scaled = query_unit * query_gain
    query_home = (query_scaled * cosine + turn_half(query_scaled) * sine_table).astype(jnp.bfloat16)
    query_home = query_home.reshape(2, block_rows, key_heads, repeat, head_dim).transpose(
        0, 2, 3, 1, 4
    )
    key_unit, key_inverse = normalize(key_raw)
    key_scaled = key_unit * key_gain
    key_home = (
        (key_scaled * cosine + turn_half(key_scaled) * sine_table)
        .astype(jnp.bfloat16)
        .transpose(0, 2, 1, 3)
    )
    value_home = (
        value_raw.astype(jnp.bfloat16)
        .reshape(2, block_rows, key_heads, head_dim)
        .transpose(0, 2, 1, 3)
    )
    pair_home = jnp.stack([key_home, value_home], axis=1)
    query_halves = [query_home[:, :, :, :half_rows], query_home[:, :, :, half_rows:]]
    half_block = (seq_index, seq_index)
    local_half = jnp.arange(half_rows, dtype=jnp.int32)
    half_pos = (
        half_block[0] * block_rows + local_half,
        half_block[1] * block_rows + half_rows + local_half,
    )

    def scored(half, key_block, block_index):
        key_pos = block_index * block_rows + jnp.arange(block_rows, dtype=jnp.int32)
        scores = (
            jnp.einsum(
                "bgrqd,bgkd->bgrqk",
                query_halves[half],
                key_block,
                preferred_element_type=jnp.float32,
            )
            * score_scale
        )
        allowed = (key_pos[None, None, :] <= half_pos[half][None, :, None]) & (
            key_pos[None, None, :] < lengths[:, None, None]
        )
        return (scores, allowed[:, None, None])

    def stats_add(half, key_block, block_index, running):
        row_max, row_sum = running
        scores, allowed = scored(half, key_block, block_index)
        masked = jnp.where(allowed, scores, NEGATIVE)
        new_max = jnp.maximum(row_max, jnp.max(masked, axis=-1))
        weights = jnp.where(allowed, jnp.exp(masked - new_max[..., None]), 0.0)
        return (new_max, row_sum * jnp.exp(row_max - new_max) + jnp.sum(weights, axis=-1))

    def visit_stats(running, key_block, block_index):
        return tuple(
            (
                lax.cond(
                    block_index <= half_block[half],
                    partial(stats_add, half, key_block, block_index),
                    keep_state,
                    running[half],
                )
                for half in range(2)
            )
        )

    stats_shape = query_halves[0].shape[:4]
    one_start = (jnp.full(stats_shape, NEGATIVE, jnp.float32), jnp.zeros(stats_shape, jnp.float32))

    def stats_turn(turn_index, carried):
        running, key_block = carried
        block_index = (seq_index - turn_index) % cycle_size
        running = visit_stats(running, key_block, block_index)
        return (running, move_keys(key_block))

    running, key_block = lax.fori_loop(
        0, cycle_size - 1, stats_turn, ((one_start, one_start), key_home)
    )
    running = visit_stats(running, key_block, (seq_index + 1) % cycle_size)
    log_total = tuple((state[0] + jnp.log(state[1]) for state in running))

    def output_add(half, kv_block, block_index, partial_out):
        scores, allowed = scored(half, kv_block[:, 0], block_index)
        weights = jnp.where(allowed, jnp.exp(scores - log_total[half][..., None]), 0.0).astype(
            jnp.bfloat16
        )
        return partial_out + jnp.einsum(
            "bgrqk,bgkd->bgrqd", weights, kv_block[:, 1], preferred_element_type=jnp.float32
        )

    def visit_output(partial_out, kv_block, block_index):
        return tuple(
            (
                lax.cond(
                    block_index <= half_block[half],
                    partial(output_add, half, kv_block, block_index),
                    keep_state,
                    partial_out[half],
                )
                for half in range(2)
            )
        )

    half_zero = jnp.zeros(query_halves[0].shape, jnp.float32)

    def output_turn(turn_index, carried):
        partial_out, kv_block = carried
        block_index = (seq_index - turn_index) % cycle_size
        partial_out = visit_output(partial_out, kv_block, block_index)
        return (partial_out, move_pair(kv_block))

    mixed_sum, kv_block = lax.fori_loop(
        0, cycle_size - 1, output_turn, ((half_zero, half_zero), pair_home)
    )
    mixed_sum = visit_output(mixed_sum, kv_block, (seq_index + 1) % cycle_size)
    mixed_parts = [mixed_sum[0].astype(jnp.bfloat16), mixed_sum[1].astype(jnp.bfloat16)]
    mixed_low = (
        jnp.concatenate(mixed_parts, axis=3)
        .transpose(0, 3, 1, 2, 4)
        .reshape(2, block_rows, query_heads * head_dim)
    )
    hidden = residual + to_rows(
        jnp.einsum("bsc,cd->bsd", mixed_low, full_out, preferred_element_type=jnp.float32)
    )
    mlp_unit, mlp_inverse = normalize(hidden)
    mlp_rows = to_group((mlp_unit * gain_mlp).astype(jnp.bfloat16))
    gate_pre = jnp.einsum("bsd,df->bsf", mlp_rows, full_gate, preferred_element_type=jnp.float32)
    up_pre = jnp.einsum("bsd,df->bsf", mlp_rows, full_up, preferred_element_type=jnp.float32)
    inner_low = (jax.nn.silu(gate_pre) * up_pre).astype(jnp.bfloat16)
    layer_out = hidden + to_rows(
        jnp.einsum("bsf,fd->bsd", inner_low, full_down, preferred_element_type=jnp.float32)
    )
    output = layer_out.astype(jnp.bfloat16)
    token_pos = (seq_index * group_size + grp_index) * local_rows + jnp.arange(
        local_rows, dtype=jnp.int32
    )
    valid_rows = (token_pos[None, :] < lengths[:, None]).astype(jnp.float32)
    cot_rows = cotangent.astype(jnp.float32) * valid_rows[:, :, None]
    grad_out_rows = to_group(cot_rows.astype(jnp.bfloat16))
    grad_w_down = jnp.einsum(
        "bsf,bsd->fd", inner_low, grad_out_rows, preferred_element_type=jnp.float32
    )
    grad_inner = jnp.einsum(
        "bsd,fd->bsf", grad_out_rows, full_down, preferred_element_type=jnp.float32
    )
    sigmoid_gate = jax.nn.sigmoid(gate_pre)
    grad_gate = (
        grad_inner * up_pre * sigmoid_gate * (1.0 + gate_pre * (1.0 - sigmoid_gate))
    ).astype(jnp.bfloat16)
    grad_up = (grad_inner * gate_pre * sigmoid_gate).astype(jnp.bfloat16)
    grad_w_gate = jnp.einsum("bsd,bsf->df", mlp_rows, grad_gate, preferred_element_type=jnp.float32)
    grad_w_up = jnp.einsum("bsd,bsf->df", mlp_rows, grad_up, preferred_element_type=jnp.float32)
    grad_mlp_in = to_rows(
        jnp.einsum("bsf,df->bsd", grad_gate, full_gate, preferred_element_type=jnp.float32)
        + jnp.einsum("bsf,df->bsd", grad_up, full_up, preferred_element_type=jnp.float32)
    )
    grad_gain_mlp = jnp.sum(grad_mlp_in * mlp_unit, axis=(0, 1))
    grad_hidden = cot_rows + norm_back(grad_mlp_in * gain_mlp, mlp_unit, mlp_inverse)
    out_gate, out_up, out_down = (
        lax.psum_scatter(
            grad_w_gate.astype(jnp.bfloat16), "seq", scatter_dimension=0, tiled=True
        ).astype(jnp.float32),
        lax.psum_scatter(
            grad_w_up.astype(jnp.bfloat16), "seq", scatter_dimension=0, tiled=True
        ).astype(jnp.float32),
        lax.psum_scatter(
            grad_w_down.astype(jnp.bfloat16), "seq", scatter_dimension=1, tiled=True
        ).astype(jnp.float32),
    )
    grad_branch = to_group(grad_hidden.astype(jnp.bfloat16))
    grad_w_out = jnp.einsum(
        "bsc,bsd->cd", mixed_low, grad_branch, preferred_element_type=jnp.float32
    )
    grad_mixed = jnp.einsum(
        "bsd,cd->bsc", grad_branch, full_out, preferred_element_type=jnp.float32
    ).astype(jnp.bfloat16)
    grad_mixed = grad_mixed.reshape(2, block_rows, key_heads, repeat, head_dim).transpose(
        0, 2, 3, 1, 4
    )
    grad_halves = [grad_mixed[:, :, :, :half_rows], grad_mixed[:, :, :, half_rows:]]
    row_delta = [
        jnp.sum(grad_halves[half].astype(jnp.float32) * mixed_sum[half], axis=-1)
        for half in range(2)
    ]

    def grad_add(half, kv_block, block_index, state):
        grad_query, grad_pair = state
        scores, allowed = scored(half, kv_block[:, 0], block_index)
        weights = jnp.where(allowed, jnp.exp(scores - log_total[half][..., None]), 0.0)
        grad_weights = jnp.einsum(
            "bgrqd,bgkd->bgrqk",
            grad_halves[half],
            kv_block[:, 1],
            preferred_element_type=jnp.float32,
        )
        grad_scores = (weights * (grad_weights - row_delta[half][..., None])).astype(jnp.bfloat16)
        grad_query = grad_query + score_scale * jnp.einsum(
            "bgrqk,bgkd->bgrqd", grad_scores, kv_block[:, 0], preferred_element_type=jnp.float32
        )
        grad_keys = score_scale * jnp.einsum(
            "bgrqk,bgrqd->bgkd", grad_scores, query_halves[half], preferred_element_type=jnp.float32
        )
        grad_values = jnp.einsum(
            "bgrqk,bgrqd->bgkd",
            weights.astype(jnp.bfloat16),
            grad_halves[half],
            preferred_element_type=jnp.float32,
        )
        return (grad_query, grad_pair + jnp.stack([grad_keys, grad_values], axis=1))

    def visit_grads(carried, kv_block, block_index):
        grad_query, grad_pair = carried
        new_query = []
        for half in range(2):
            one_query, grad_pair = lax.cond(
                block_index <= half_block[half],
                partial(grad_add, half, kv_block, block_index),
                keep_state,
                (grad_query[half], grad_pair),
            )
            new_query.append(one_query)
        return (tuple(new_query), grad_pair)

    def grad_turn(turn_index, carried):
        running_grads, kv_block = carried
        block_index = (seq_index - turn_index) % cycle_size
        running_grads = visit_grads(running_grads, kv_block, block_index)
        return ((running_grads[0], move_grads(running_grads[1])), move_pair(kv_block))

    grad_start = ((half_zero, half_zero), jnp.zeros(pair_home.shape, jnp.float32))
    running_grads, kv_block = lax.fori_loop(0, cycle_size - 1, grad_turn, (grad_start, pair_home))
    running_grads = visit_grads(running_grads, kv_block, (seq_index + 1) % cycle_size)
    grad_pair = move_grads(running_grads[1])
    query_parts = [running_grads[0][0], running_grads[0][1]]
    grad_query = jnp.concatenate(query_parts, axis=3)

    def unturn(gradient):
        return gradient * cosine - turn_half(gradient * sine_table)

    grad_query_scaled = unturn(
        grad_query.transpose(0, 3, 1, 2, 4).reshape(2, block_rows, query_heads, head_dim)
    )
    grad_key_scaled = unturn(grad_pair[:, 0].transpose(0, 2, 1, 3))
    local_query_gain = jnp.sum(grad_query_scaled * query_unit, axis=(0, 1, 2))
    local_key_gain = jnp.sum(grad_key_scaled * key_unit, axis=(0, 1, 2))
    grad_query_raw = (
        norm_back(grad_query_scaled * query_gain, query_unit, query_inverse)
        .reshape(2, block_rows, query_heads * head_dim)
        .astype(jnp.bfloat16)
    )
    grad_key_raw = (
        norm_back(grad_key_scaled * key_gain, key_unit, key_inverse)
        .reshape(2, block_rows, key_heads * head_dim)
        .astype(jnp.bfloat16)
    )
    grad_value_raw = (
        grad_pair[:, 1]
        .transpose(0, 2, 1, 3)
        .reshape(2, block_rows, key_heads * head_dim)
        .astype(jnp.bfloat16)
    )
    grad_w_query = jnp.einsum(
        "bsd,bsc->dc", attn_rows, grad_query_raw, preferred_element_type=jnp.float32
    )
    grad_w_key = jnp.einsum(
        "bsd,bsc->dc", attn_rows, grad_key_raw, preferred_element_type=jnp.float32
    )
    grad_w_value = jnp.einsum(
        "bsd,bsc->dc", attn_rows, grad_value_raw, preferred_element_type=jnp.float32
    )
    grad_attn_part = jnp.einsum(
        "bsc,dc->bsd", grad_query_raw, full_query, preferred_element_type=jnp.float32
    )
    grad_attn_part = grad_attn_part + jnp.einsum(
        "bsc,dc->bsd", grad_key_raw, full_key, preferred_element_type=jnp.float32
    )
    grad_attn_part = grad_attn_part + jnp.einsum(
        "bsc,dc->bsd", grad_value_raw, full_value, preferred_element_type=jnp.float32
    )
    grad_attn_in = to_rows(grad_attn_part)
    grad_gain_attn = jnp.sum(grad_attn_in * attn_unit, axis=(0, 1))
    grad_tokens = grad_hidden + norm_back(grad_attn_in * gain_attn, attn_unit, attn_inverse)
    out_query, out_key, out_value, out_out = (
        lax.psum_scatter(
            grad_w_query.astype(jnp.bfloat16), "seq", scatter_dimension=0, tiled=True
        ).astype(jnp.float32),
        lax.psum_scatter(
            grad_w_key.astype(jnp.bfloat16), "seq", scatter_dimension=0, tiled=True
        ).astype(jnp.float32),
        lax.psum_scatter(
            grad_w_value.astype(jnp.bfloat16), "seq", scatter_dimension=0, tiled=True
        ).astype(jnp.float32),
        lax.psum_scatter(
            grad_w_out.astype(jnp.bfloat16), "seq", scatter_dimension=1, tiled=True
        ).astype(jnp.float32),
    )
    out_attn_gain, out_mlp_gain = (
        lax.psum_scatter(grad_gain_attn, ("seq", "grp"), scatter_dimension=0, tiled=True),
        lax.psum_scatter(grad_gain_mlp, ("seq", "grp"), scatter_dimension=0, tiled=True),
    )
    out_query_gain, out_key_gain = lax.psum((local_query_gain, local_key_gain), ("seq", "grp"))
    return (
        output,
        grad_tokens,
        out_attn_gain,
        out_query,
        out_key,
        out_value,
        out_query_gain,
        out_key_gain,
        out_out,
        out_mlp_gain,
        out_gate,
        out_up,
        out_down,
    )


def solution(mesh):
    placed = (
        P(None, ("seq", "grp"), None),
        P(),
        P(("seq", "grp")),
        P("seq", "grp"),
        P("seq", "grp"),
        P("seq", "grp"),
        P(),
        P(),
        P("grp", "seq"),
        P(("seq", "grp")),
        P("seq", "grp"),
        P("seq", "grp"),
        P("grp", "seq"),
        P(None, ("seq", "grp"), None),
    )
    return jax.shard_map(
        shards,
        mesh=mesh,
        in_specs=placed,
        out_specs=(
            P(None, ("seq", "grp"), None),
            P(None, ("seq", "grp"), None),
            P(("seq", "grp")),
            P("seq", "grp"),
            P("seq", "grp"),
            P("seq", "grp"),
            P(),
            P(),
            P("grp", "seq"),
            P(("seq", "grp")),
            P("seq", "grp"),
            P("seq", "grp"),
            P("grp", "seq"),
        ),
        check_vma=False,
    )
```

profile of v0, /device:TPU:9, one launch (start us, length us, event | category | flops | bytes accessed | tf_op | source)
XLA Modules:
  0.0 1334.9 jit_solution(1417192310628535065)
XLA Ops:
  10.7 39.9 %all-reduce.5 = (f32[2048]{0:T(1024)S(1)}, f32[2048]{0:T(1024)S(1)}) all-reduce(f32[2048]{0:T(1024)S(1)} %dynamic-update-slice, f32[2048]{0:T(1024)S(1)} %dynamic-update-slice.1), channel_id=1, replica_groups=mesh['seq'=8,'grp'=4] {'seq','grp'}, use_global_device_ids=true, to_apply=%add | all-reduce | flops 4096 | bytes 32768
  57.7 32.3 %all-gather.12.cloned.1.call-done = bf16[2,256,2048]{2,1,0:T(8,128)(2,1)} async-done(((bf16[2,64,2048]{2,1,0:T(8,128)(2,1)}), bf16[2,256,2048]{2,1,0:T(8,128)(2,1)}) %all-gather.12.cloned.1.call-update) | async-done | bytes 2097168 | tf_op jit(solution)/shard_map/all_gather | solution.py:55
  93.6 24.0 %all-gather.16.cloned.1.call-done = bf16[2048,256]{0,1:T(8,128)(2,1)} async-done(((bf16[256,256]{0,1:T(8,128)(2,1)}), bf16[2048,256]{0,1:T(8,128)(2,1)}) %all-gather.16.cloned.1.call-update) | async-done | bytes 1048592 | tf_op jit(solution)/shard_map/all_gather | solution.py:108
  120.6 25.3 %all-gather.18.cloned.1.call-done = bf16[2048,512]{1,0:T(8,128)(2,1)} async-done(((bf16[256,512]{1,0:T(8,128)(2,1)}), bf16[2048,512]{1,0:T(8,128)(2,1)}) %all-gather.18.cloned.1.call-update) | async-done | bytes 2097168 | tf_op jit(solution)/shard_map/all_gather | solution.py:106
  159.7 65.2 %while.78 = (s32[]{:T(128)}, f32[2,2,2,128]{3,2,1,0:T(2,128)S(1)}, f32[2,2,2,128]{3,2,1,0:T(2,128)S(1)}, f32[2,2,2,128]{3,2,1,0:T(2,128)S(1)}, f32[2,2,2,128]{3,...) while((s32[]{:T(128)}, f32[2,2,2,128]{3,2,1,0:T(2,128)S(1)}, ...), condition=%wide.region_12.13_spmd.clone, body=%wide.region_3.12_spmd.clone.sunk | while | flops 137565968 | bytes 7459404 | solution.py:204
  227.1 80.5 %while.79 = (s32[]{:T(128)}, f32[2,2,2,128,128]{4,3,2,1,0:T(8,128)S(1)}, f32[2,2,2,128,128]{4,3,2,1,0:T(8,128)S(1)}, bf16[2,2,2,256,128]{4,3,2,0,1:T(8,128)(2,1)...) while((s32[]{:T(128)}, ...), condition=%wide.region_26.27_spmd.clone, body=%wide.region_21.26_spmd.clone.sunk | while | flops 270993152 | bytes 7229964 | solution.py:240
  313.0 35.9 %reduce-scatter.12.cloned.1.call-done = bf16[2,64,2048]{2,1,0:T(8,128)(2,1)} async-done(((bf16[2,256,2048]{2,1,0:T(8,128)(2,1)}), bf16[2,64,2048]{2,1,0:T(8,128)(2,1)}) %reduce-scatter.12.cloned.1.call-update) | async-done | bytes 524304 | tf_op jit(solution)/shard_map/reduce_scatter | solution.py:59
  355.5 32.2 %all-gather.22.cloned.1.call-done = bf16[2,256,2048]{2,1,0:T(8,128)(2,1)} async-done(((bf16[2,64,2048]{2,1,0:T(8,128)(2,1)}), bf16[2,256,2048]{2,1,0:T(8,128)(2,1)}) %all-gather.22.cloned.1.call-update) | async-done | bytes 2097168 | tf_op jit(solution)/shard_map/all_gather | solution.py:55
  387.7 64.7 %all-gather.26.cloned.1.call-done = bf16[2048,1536]{1,0:T(8,128)(2,1)} async-done(((bf16[256,1536]{1,0:T(8,128)(2,1)}), bf16[2048,1536]{1,0:T(8,128)(2,1)}) %all-gather.26.cloned.1.call-update) | async-done | bytes 6291472 | tf_op jit(solution)/shard_map/all_gather | solution.py:113
  452.4 8.5 fusion.158
  461.0 29.8 %all-gather.30.cloned.1.call-done = bf16[2,256,2048]{2,1,0:T(8,128)(2,1)} async-done(((bf16[2,64,2048]{2,1,0:T(8,128)(2,1)}), bf16[2,256,2048]{2,1,0:T(8,128)(2,1)}) %all-gather.30.cloned.1.call-update) | async-done | bytes 2097168 | tf_op jit(solution)/shard_map/all_gather | solution.py:55
  490.8 64.2 %all-gather.28.cloned.1.call-done = bf16[1536,2048]{1,0:T(8,128)(2,1)} async-done(((bf16[1536,256]{1,0:T(8,128)(2,1)}), bf16[1536,2048]{1,0:T(8,128)(2,1)}) %all-gather.28.cloned.1.call-update) | async-done | bytes 6291472 | tf_op jit(solution)/shard_map/all_gather | solution.py:114
  555.0 8.6 fusion.152
  563.5 56.9 %all-gather.24.cloned.1.call-done = bf16[2048,1536]{1,0:T(8,128)(2,1)} async-done(((bf16[256,1536]{1,0:T(8,128)(2,1)}), bf16[2048,1536]{1,0:T(8,128)(2,1)}) %all-gather.24.cloned.1.call-update) | async-done | bytes 6291472 | tf_op jit(solution)/shard_map/all_gather | solution.py:112
  620.5 11.0 multiply_convert_fusion.1
  631.4 6.7 fusion.156
  643.0 35.8 %reduce-scatter.16.cloned.1.call-done = bf16[2,64,2048]{2,1,0:T(8,128)(2,1)} async-done(((bf16[2,256,2048]{2,1,0:T(8,128)(2,1)}), bf16[2,64,2048]{2,1,0:T(8,128)(2,1)}) %reduce-scatter.16.cloned.1.call-update) | async-done | bytes 524304 | tf_op jit(solution)/shard_map/reduce_scatter | solution.py:59
  683.5 35.2 %all-gather.32.cloned.1.call-done = bf16[2,256,2048]{2,1,0:T(8,128)(2,1)} async-done(((bf16[2,64,2048]{2,1,0:T(8,128)(2,1)}), bf16[2,256,2048]{2,1,0:T(8,128)(2,1)}) %all-gather.32.cloned.1.call-update) | async-done | bytes 2097168 | tf_op jit(solution)/shard_map/all_gather | solution.py:55
  727.2 145.7 %while.80 = (s32[]{:T(128)}, f32[2,2,2,128,128]{4,3,2,1,0:T(8,128)}, f32[2,2,2,128,128]{4,3,2,1,0:T(8,128)}, f32[2,2,2,256,128]{4,3,2,0,1:T(8,128)S(1)}, bf16[2,...) while((s32[]{:T(128)}, ...), condition=%wide.region_43.44_spmd.clone, body=%wide.region_38.0_spmd.clone.sunk | while | flops 677578496 | bytes 43938656 | solution.py:359
  817.7 10.7 collective-permute-start.2
  843.0 9.2 collective-permute-start.3
  932.9 7.3 fusion.166
  941.9 6.7 bitcast_convert_fusion.2
  948.7 6.9 bitcast_convert_fusion.1
  957.2 6.8 bitcast_convert_fusion
  967.5 29.0 %reduce-scatter.26.cloned.1.call-done = bf16[512,256]{1,0:T(8,128)(2,1)} async-done(((bf16[512,2048]{1,0:T(8,128)(2,1)}), bf16[512,256]{1,0:T(8,128)(2,1)}) %reduce-scatter.26.cloned.1.call-update) | async-done | bytes 262160 | tf_op jit(solution)/shard_map/reduce_scatter | solution.py:421
  998.2 34.8 %reduce-scatter.20.cloned.1.call-done = bf16[256,512]{1,0:T(8,128)(2,1)} async-done(((bf16[2048,512]{1,0:T(8,128)(2,1)}), bf16[256,512]{1,0:T(8,128)(2,1)}) %reduce-scatter.20.cloned.1.call-update) | async-done | bytes 262160 | tf_op jit(solution)/shard_map/reduce_scatter | solution.py:412
  1034.9 40.0 %reduce-scatter.18.cloned.1.call-done = bf16[2,64,2048]{2,1,0:T(8,128)(2,1)} async-done(((bf16[2,256,2048]{2,1,0:T(8,128)(2,1)}), bf16[2,64,2048]{2,1,0:T(8,128)(2,1)}) %reduce-scatter.18.cloned.1.call-update) | async-done | bytes 524304 | tf_op jit(solution)/shard_map/reduce_scatter | solution.py:59
  1076.4 39.2 %all-reduce.4 = (f32[2048]{0:T(1024)S(1)}, f32[128]{0:T(128)}, f32[128]{0:T(128)}, f32[2048]{0:T(1024)S(1)}) all-reduce(f32[2048]{0:T(1024)S(1)} %get-tuple-element.1724, f32[128]{0:T(128)S(1)} %get-tuple-element.1718, f32[128]{0:T(128)S(1)} %copy-done.70, f32[2048]{0:T(1024)S(1)} %copy-done.54), channel_id=6, replica_groups=mesh['seq'=8,'grp'=4] {'seq','grp'}, use_global_device_ids=true, to_apply=%region_53.54.clone | all-reduce | flops 4352 | bytes 34816
  1120.0 64.2 %reduce-scatter.28.cloned.1.call-done = bf16[256,1536]{1,0:T(8,128)(2,1)} async-done(((bf16[2048,1536]{1,0:T(8,128)(2,1)}), bf16[256,1536]{1,0:T(8,128)(2,1)}) %reduce-scatter.28.cloned.1.call-update) | async-done | bytes 786448 | tf_op jit(solution)/shard_map/reduce_scatter | solution.py:288
  1186.6 68.1 %reduce-scatter.30.cloned.1.call-done = bf16[256,1536]{1,0:T(8,128)(2,1)} async-done(((bf16[2048,1536]{1,0:T(8,128)(2,1)}), bf16[256,1536]{1,0:T(8,128)(2,1)}) %reduce-scatter.30.cloned.1.call-update) | async-done | bytes 786448 | tf_op jit(solution)/shard_map/reduce_scatter | solution.py:291
  1257.2 68.1 %reduce-scatter.32.cloned.1.call-done = bf16[1536,256]{1,0:T(8,128)(2,1)} async-done(((bf16[1536,2048]{1,0:T(8,128)(2,1)}), bf16[1536,256]{1,0:T(8,128)(2,1)}) %reduce-scatter.32.cloned.1.call-update) | async-done | bytes 786448 | tf_op jit(solution)/shard_map/reduce_scatter | solution.py:294
  (752 shorter events, 477.9 us)
Async XLA Ops:
  7.2 50.5 %all-gather.14.cloned.1.call-start = ((), (), s32[]{:S(2)}) async-start(), calls=%async_computation.12 | async-start | bytes 1179648 | tf_op jit(solution)/shard_map/all_gather | solution.py:107
  9.0 81.1 %all-gather.12.cloned.1.call-start = ((), (), s32[]{:S(2)}) async-start(), calls=%async_computation.11 | async-start | bytes 2621440 | tf_op jit(solution)/shard_map/all_gather | solution.py:55
  54.0 63.6 %all-gather.16.cloned.1.call-start = ((), (), s32[]{:S(2)}) async-start(), calls=%async_computation.13 | async-start | bytes 1179648 | tf_op jit(solution)/shard_map/all_gather | solution.py:108
  54.8 91.0 %all-gather.18.cloned.1.call-start = ((), (), s32[]{:S(2)}) async-start(), calls=%async_computation.14 | async-start | bytes 2359296 | tf_op jit(solution)/shard_map/all_gather | solution.py:106
  55.4 253.2 %all-gather.20.cloned.1.call-start = ((), (), s32[]{:S(2)}) async-start(), calls=%async_computation.15 | async-start | bytes 2359296 | tf_op jit(solution)/shard_map/all_gather | solution.py:109
  56.0 292.9 %reduce-scatter.12.cloned.1.call-start = ((), (), s32[]{:S(2)}) async-start(), calls=%async_computation.16 | async-start | bytes 2621440 | tf_op jit(solution)/shard_map/reduce_scatter | solution.py:59
  160.4 12.5 collective-permute-start
  312.9 74.8 %all-gather.22.cloned.1.call-start = ((), (), s32[]{:S(2)}) async-start(), calls=%async_computation.17 | async-start | bytes 2621440 | tf_op jit(solution)/shard_map/all_gather | solution.py:55
  352.2 100.2 %all-gather.26.cloned.1.call-start = ((), (), s32[]{:S(2)}) async-start(), calls=%async_computation.19 | async-start | bytes 7077888 | tf_op jit(solution)/shard_map/all_gather | solution.py:113
  353.0 137.8 %all-gather.30.cloned.1.call-start = ((), (), s32[]{:S(2)}) async-start(), calls=%async_computation.22 | async-start | bytes 2621440 | tf_op jit(solution)/shard_map/all_gather | solution.py:55
  354.1 200.9 %all-gather.28.cloned.1.call-start = ((), (), s32[]{:S(2)}) async-start(), calls=%async_computation.20 | async-start | bytes 7077888 | tf_op jit(solution)/shard_map/all_gather | solution.py:114
  354.7 265.8 %all-gather.24.cloned.1.call-start = ((), (), s32[]{:S(2)}) async-start(), calls=%async_computation.18 | async-start | bytes 7077888 | tf_op jit(solution)/shard_map/all_gather | solution.py:112
  355.4 323.4 %reduce-scatter.16.cloned.1.call-start = ((), (), s32[]{:S(2)}) async-start(), calls=%async_computation.23 | async-start | bytes 2621440 | tf_op jit(solution)/shard_map/reduce_scatter | solution.py:59
  643.0 75.8 %all-gather.32.cloned.1.call-start = ((), (), s32[]{:S(2)}) async-start(), calls=%async_computation.24 | async-start | bytes 2621440 | tf_op jit(solution)/shard_map/all_gather | solution.py:55
  683.3 280.8 %reduce-scatter.22.cloned.1.call-start = ((), (), s32[]{:S(2)}) async-start(), calls=%async_computation.27 | async-start | bytes 1179648 | tf_op jit(solution)/shard_map/reduce_scatter | solution.py:415
  737.4 11.7 collective-permute-start.3
  760.2 11.7 collective-permute-start.3
  782.9 11.7 collective-permute-start.3
  805.7 11.7 collective-permute-start.3
  817.7 16.8 %collective-permute-start.2 = (bf16[2,2,2,256,128]{4,3,2,0,1:T(8,128)(2,1)S(1)}, bf16[2,2,2,256,128]{4,3,2,0,1:T(8,128)(2,1)S(1)}, u32[]{:S(2)}, u32[]{:S(2)}) collective-permute-start(bf16[2,2,2,256,128]{4,3,2,0,1:T(8,128)(2,1)S(1)} %convert_element_type.497), channel_id=1, source_target_pairs={{0,4},{4,8},{8,12},{12,16},{16,20},{20,24},{24,28},{28,0},{1,5},{5... | collective-permute-start | bytes 1572872 | tf_op jit(solution)/shard_map/while/body/eval_jaxpr/ppermute | solution.py:22
  828.4 11.7 collective-permute-start.3
  840.4 11.8 collective-permute-start.2
  843.0 15.3 %collective-permute-start.3 = (bf16[2,2,2,256,128]{4,3,2,0,1:T(8,128)(2,1)S(1)}, bf16[2,2,2,256,128]{4,3,2,0,1:T(8,128)(2,1)S(1)}, u32[]{:S(2)}, u32[]{:S(2)}) collective-permute-start(bf16[2,2,2,256,128]{4,3,2,0,1:T(8,128)(2,1)S(1)} %copy.299), channel_id=1, source_target_pairs={{0,4},{4,8},{8,12},{12,16},{16,20},{20,24},{24,28},{1,5},{5,9},{9,... | collective-permute-start | bytes 1572872 | tf_op jit(solution)/shard_map/while/body/eval_jaxpr/ppermute | solution.py:17
  873.7 12.2 collective-permute-start.4
  890.3 75.6 %reduce-scatter.24.cloned.1.call-start = ((), (), s32[]{:S(2)}) async-start(), calls=%async_computation.28 | async-start | bytes 1179648 | tf_op jit(solution)/shard_map/reduce_scatter | solution.py:418
  894.1 102.4 %reduce-scatter.26.cloned.1.call-start = ((), (), s32[]{:S(2)}) async-start(), calls=%async_computation.29 | async-start | bytes 2359296 | tf_op jit(solution)/shard_map/reduce_scatter | solution.py:421
  896.8 136.3 %reduce-scatter.20.cloned.1.call-start = ((), (), s32[]{:S(2)}) async-start(), calls=%async_computation.26 | async-start | bytes 2359296 | tf_op jit(solution)/shard_map/reduce_scatter | solution.py:412
  924.2 150.7 %reduce-scatter.18.cloned.1.call-start = ((), (), s32[]{:S(2)}) async-start(), calls=%async_computation.25 | async-start | bytes 2621440 | tf_op jit(solution)/shard_map/reduce_scatter | solution.py:59
  931.6 185.2 %reduce-scatter.14.cloned.1.call-start = ((), (), s32[]{:S(2)}) async-start(), calls=%async_computation.21 | async-start | bytes 2621440 | tf_op jit(solution)/shard_map/reduce_scatter | solution.py:59
  940.3 243.9 %reduce-scatter.28.cloned.1.call-start = ((), (), s32[]{:S(2)}) async-start(), calls=%async_computation.30 | async-start | bytes 7077888 | tf_op jit(solution)/shard_map/reduce_scatter | solution.py:288
  948.6 306.1 %reduce-scatter.30.cloned.1.call-start = ((), (), s32[]{:S(2)}) async-start(), calls=%async_computation.31 | async-start | bytes 7077888 | tf_op jit(solution)/shard_map/reduce_scatter | solution.py:291
  955.6 369.6 %reduce-scatter.32.cloned.1.call-start = ((), (), s32[]{:S(2)}) async-start(), calls=%async_computation.32 | async-start | bytes 7077888 | tf_op jit(solution)/shard_map/reduce_scatter | solution.py:294
  (109 other events, 3824.1 us)
Sparse Core Ops, SparseCore 0:
  10.2 26.9 all-gather.13
  54.1 35.9 all-gather.11
  92.2 25.3 all-gather.15
  119.0 26.7 all-gather.17
  147.2 32.1 all-gather.19
  313.1 35.7 reduce-scatter.11
  352.3 35.3 all-gather.21
  389.4 62.9 all-gather.25
  455.0 35.7 all-gather.29
  492.3 62.5 all-gather.27
  556.7 63.7 all-gather.23
  643.1 35.6 reduce-scatter.15
  683.4 35.2 all-gather.31
  890.4 35.6 reduce-scatter.21
  928.3 30.5 reduce-scatter.23
  961.1 35.3 reduce-scatter.25
  998.6 34.4 reduce-scatter.19
  1035.9 38.9 reduce-scatter.17
  1078.1 35.4 reduce-scatter.13
  1115.7 68.3 reduce-scatter.27
  1186.5 68.1 reduce-scatter.29
  1257.0 68.1 reduce-scatter.31
where the time goes:
time: 1350 us; the launch traced here: 1330 us
  waiting for transfers between devices  857 us (63%)
  matrix products  143 us (11%)
  starting transfers between devices  114 us (8%)
  blocking collectives  79.1 us (6%)
  local copies, waits for them, and re-layouts  62.4 us (5%)
  other arithmetic  59.7 us (4%)
  between operations  15.9 us (1%)
    all_gather x4, waiting for transfers between devices, to_group(): return lax.all_gather(rows_local, 'grp', axis=1, tiled=True)  130 us
    reduce_scatter x4, waiting for transfers between devices, to_rows(): lax.psum_scatter(partial_sums.astype(jnp.bfloat16), 'grp', scatter_dimens...  112 us
    ppermute x21, waiting for transfers between devices, from_behind(): return lax.ppermute(x, axis, pairs)  85.3 us
    ppermute x21, starting transfers between devices, from_behind(): return lax.ppermute(x, axis, pairs)  81.3 us
    unnamed x2, blocking collectives  79.1 us
    reduce_scatter x1, waiting for transfers between devices, shards(): lax.psum_scatter(grad_w_up.astype(jnp.bfloat16), 'seq', scatter_dimension...  68.1 us
    reduce_scatter x1, waiting for transfers between devices, shards(): lax.psum_scatter(grad_w_down.astype(jnp.bfloat16), 'seq', scatter_dimensi...  68.1 us
    all_gather x1, waiting for transfers between devices, shards(): lax.all_gather(w_up, 'seq', axis=0, tiled=True)  64.7 us
  transfers between devices with their start and end apart: 51, of which 42 were waited for; matrix products, arithmetic and copies ran while one was open for 13% of the time, Pallas kernels for 0%

commit v1 on v0

v1 whole, which is shorter than its diff:
```python
from functools import partial
import math

import jax
import jax.numpy as jnp
from jax import lax
from jax.experimental import pallas as pl
from jax.experimental.pallas import tpu as pltpu
from jax.sharding import PartitionSpec as P

EPSILON = 1e-06
ROPE_BASE = 1000000.0
MESH = pl.DeviceIdType.MESH
ANY = pl.BlockSpec(memory_space=pl.ANY)
VMEM = pl.BlockSpec(memory_space=pltpu.VMEM)
DMA = pltpu.SemaphoreType.DMA
F32 = jnp.float32
BF16 = jnp.bfloat16


def normalize(values):
    inverse = lax.rsqrt(jnp.mean(values * values, axis=-1, keepdims=True) + EPSILON)
    return (values * inverse, inverse)


def norm_back(gradient, unit_values, inverse):
    return inverse * (
        gradient - unit_values * jnp.mean(gradient * unit_values, axis=-1, keepdims=True)
    )


def after(value, earlier):
    return lax.optimization_barrier((value, earlier))[0]


def nt(a, b):
    return lax.dot_general(a, b, (((1,), (1,)), ((), ())), preferred_element_type=F32)


def tn(a, b):
    return lax.dot_general(a, b, (((0,), (0,)), ((), ())), preferred_element_type=F32)


def nn(a, b):
    return jnp.dot(a, b, preferred_element_type=F32)


def comm_params(collective_id, mib=32):
    return pltpu.CompilerParams(
        collective_id=collective_id, has_side_effects=True, vmem_limit_bytes=mib * 2**20
    )


def greet(peers):
    barrier = pltpu.get_barrier_semaphore()
    for peer in peers:
        pl.semaphore_signal(barrier, inc=1, device_id=peer, device_id_type=MESH)
    pl.semaphore_wait(barrier, len(peers))


def send(src, dst, send_sem, recv_sem, peer):
    copy = pltpu.make_async_remote_copy(
        src_ref=src,
        dst_ref=dst,
        send_sem=send_sem,
        recv_sem=recv_sem,
        device_id=peer,
        device_id_type=MESH,
    )
    copy.start()
    return copy


def spread_kernel(seq, grp, x_ref, out_ref, send1, recv1, send2, recv2):
    s, g = lax.axis_index("seq"), lax.axis_index("grp")
    line = [(lax.rem(s + k, seq), g) for k in range(1, seq)]
    plane = [(s, lax.rem(g + k, grp)) for k in range(1, grp)]
    greet(line + plane)
    out_ref[pl.ds(g, 1), pl.ds(s, 1)] = x_ref[...][None, None]
    first = [
        send(x_ref, out_ref.at[g, s], send1.at[k], recv1.at[k], peer) for k, peer in enumerate(line)
    ]
    for copy in first:
        copy.wait()
    second = [
        send(out_ref.at[g], out_ref.at[g], send2.at[k], recv2.at[k], peer)
        for k, peer in enumerate(plane)
    ]
    for copy in second:
        copy.wait()


def spread(block, seq, grp, collective_id):
    return pl.pallas_call(
        partial(spread_kernel, seq, grp),
        name="gather_gains",
        out_shape=jax.ShapeDtypeStruct((grp, seq) + block.shape, block.dtype),
        in_specs=[VMEM],
        out_specs=VMEM,
        scratch_shapes=[DMA((seq - 1,)), DMA((seq - 1,)), DMA((grp - 1,)), DMA((grp - 1,))],
        compiler_params=comm_params(collective_id),
    )(block)


def total_kernel(seq, grp, x_ref, out_ref, line_buf, part, plane_buf, send1, recv1, send2, recv2):
    s, g = lax.axis_index("seq"), lax.axis_index("grp")
    line = [(lax.rem(s + k, seq), g) for k in range(1, seq)]
    plane = [(s, lax.rem(g + k, grp)) for k in range(1, grp)]
    greet(line + plane)
    line_buf[pl.ds(s, 1)] = x_ref[...][None]
    first = [
        send(x_ref, line_buf.at[s], send1.at[k], recv1.at[k], peer) for k, peer in enumerate(line)
    ]
    for copy in first:
        copy.wait()
    part[...] = jnp.sum(line_buf[...], axis=0)
    plane_buf[pl.ds(g, 1)] = part[...][None]
    second = [
        send(part, plane_buf.at[g], send2.at[k], recv2.at[k], peer) for k, peer in enumerate(plane)
    ]
    for copy in second:
        copy.wait()
    out_ref[...] = jnp.sum(plane_buf[...], axis=0)


def total(block, seq, grp, collective_id):
    return pl.pallas_call(
        partial(total_kernel, seq, grp),
        name="sum_gains",
        out_shape=jax.ShapeDtypeStruct(block.shape, block.dtype),
        in_specs=[VMEM],
        out_specs=VMEM,
        scratch_shapes=[
            pltpu.VMEM((seq,) + block.shape, block.dtype),
            pltpu.VMEM(block.shape, block.dtype),
            pltpu.VMEM((grp,) + block.shape, block.dtype),
            DMA((seq - 1,)),
            DMA((seq - 1,)),
            DMA((grp - 1,)),
            DMA((grp - 1,)),
        ],
        compiler_params=comm_params(collective_id),
    )(block)


def plane_peers(high):
    s, g = lax.axis_index("seq"), lax.axis_index("grp")
    a, b = g // 2, lax.rem(g, 2)
    across = (s, a * 2 + 1 - b)
    along = [(s, lax.rem(a + k, high) * 2 + b) for k in range(1, high)]
    return a, b, across, along


def gather_rows_kernel(count, high, *refs):
    sources, targets = refs[:count], refs[count : 2 * count]
    send_sems, recv_sems, local_sems = refs[2 * count :]
    a, b, across, along = plane_peers(high)
    greet([across] + along)
    def pusher(i):
        slots = iter(range(4 * high))

        def push(what, where, peer):
            k = next(slots)
            return send(what, where, send_sems.at[i, k], recv_sems.at[i, k], peer)

        return push

    started, local = [], []
    for i in range(count):
        src, dst, push = sources[i], targets[i], pusher(i)
        copy = pltpu.make_async_copy(src, dst.at[:, a, b], local_sems.at[i])
        copy.start()
        local.append(copy)
        over0 = push(src.at[0], dst.at[0, a, b], across)
        up1 = [push(src.at[1], dst.at[1, a, b], peer) for peer in along]
        over1 = push(src.at[1], dst.at[1, a, b], across)
        up0 = [push(src.at[0], dst.at[0, a, b], peer) for peer in along]
        started.append((over0, up1, over1, up0, push))
    for i in range(count):
        dst = targets[i]
        over0, up1, over1, up0, push = started[i]
        over0.wait_recv()
        later = [push(dst.at[0, a, 1 - b], dst.at[0, a, 1 - b], peer) for peer in along]
        for k in range(1, high):
            up1[k - 1].wait_recv()
            origin = lax.rem(a + high - k, high)
            later.append(push(dst.at[1, origin, b], dst.at[1, origin, b], across))
        over1.wait_recv()
        for copy in up0 + later:
            copy.wait_recv()
        for copy in [over0, over1] + up0 + up1 + later:
            copy.wait_send()
        local[i].wait()


def gather_rows(arrays, grp, collective_id, name):
    count, high = len(arrays), grp // 2
    rows, rest = arrays[0].shape[1:]
    result = pl.pallas_call(
        partial(gather_rows_kernel, count, high),
        name=name,
        out_shape=[jax.ShapeDtypeStruct((2, high, 2, rows, rest), x.dtype) for x in arrays],
        in_specs=[ANY] * count,
        out_specs=[ANY] * count,
        scratch_shapes=[DMA((count, 4 * high)), DMA((count, 4 * high)), DMA((count,))],
        compiler_params=comm_params(collective_id),
    )(*arrays)
    return [x.reshape(2 * grp * rows, rest) for x in result]


def sum_rows_kernel(high, src, out, recv0, mid0, last0, recv1, mid1, last1, own0, own1, send_sems, recv_sems, local_sems):
    a, b, across, along = plane_peers(high)
    greet([across] + along)
    slots = iter(range(2 * high))

    def push(what, where, peer):
        k = next(slots)
        return send(what, where, send_sems.at[k], recv_sems.at[k], peer)

    over0 = push(src.at[0, :, 1 - b], recv0, across)
    up1 = [
        push(src.at[1, lax.rem(a + k, high)], recv1.at[k - 1], along[k - 1]) for k in range(1, high)
    ]
    load0 = pltpu.make_async_copy(src.at[0, :, b], own0, local_sems.at[0])
    load1 = pltpu.make_async_copy(src.at[1, a], own1, local_sems.at[1])
    load0.start()
    load1.start()
    load0.wait()
    load1.wait()
    over0.wait_recv()
    mid0[...] = (own0[...].astype(F32) + recv0[...].astype(F32)).astype(BF16)
    up0 = [
        push(mid0.at[lax.rem(a + k, high)], last0.at[k - 1], along[k - 1]) for k in range(1, high)
    ]
    for copy in up1:
        copy.wait_recv()
    joined = own1[...].astype(F32)
    for k in range(1, high):
        joined = joined + recv1[k - 1].astype(F32)
    mid1[...] = joined.astype(BF16)
    over1 = push(mid1.at[1 - b], last1, across)
    for copy in up0:
        copy.wait_recv()
    result = own0[pl.ds(a, 1)][0].astype(F32) + recv0[pl.ds(a, 1)][0].astype(F32)
    for k in range(1, high):
        result = result + last0[k - 1].astype(F32)
    out[0] = result
    over1.wait_recv()
    result = own1[pl.ds(b, 1)][0].astype(F32)
    for k in range(1, high):
        result = result + recv1[k - 1, pl.ds(b, 1)][0].astype(F32)
    out[1] = result + last1[...].astype(F32)
    for copy in [over0, over1] + up0 + up1:
        copy.wait_send()


def sum_rows(partial_sums, grp, collective_id, name):
    high = grp // 2
    tokens, width = partial_sums.shape
    rows = tokens // (2 * grp)
    parts = partial_sums.astype(BF16).reshape(2, high, 2, rows, width)
    return pl.pallas_call(
        partial(sum_rows_kernel, high),
        name=name,
        out_shape=jax.ShapeDtypeStruct((2, rows, width), F32),
        in_specs=[ANY],
        out_specs=VMEM,
        scratch_shapes=[
            pltpu.VMEM((high, rows, width), BF16),
            pltpu.VMEM((high, rows, width), BF16),
            pltpu.VMEM((high - 1, rows, width), BF16),
            pltpu.VMEM((high - 1, 2, rows, width), BF16),
            pltpu.VMEM((2, rows, width), BF16),
            pltpu.VMEM((rows, width), BF16),
            pltpu.VMEM((high, rows, width), BF16),
            pltpu.VMEM((2, rows, width), BF16),
            DMA((2 * high,)),
            DMA((2 * high,)),
            DMA((2,)),
        ],
        compiler_params=comm_params(collective_id),
    )(parts)


def turn_half(values):
    half = values.shape[-1] // 2
    return jnp.concatenate([-values[:, half:], values[:, :half]], axis=-1)


def heads_kernel(queries, keys, raw, gains, cosine, sine, out):
    head = pl.program_id(0)

    @pl.when(head < queries + keys)
    def _():
        unit, _ = normalize(raw[...])
        scaled = unit * jnp.where(head < queries, gains[0:1], gains[1:2])
        out[...] = (scaled * cosine[...] + turn_half(scaled) * sine[...]).astype(BF16)

    @pl.when(head >= queries + keys)
    def _():
        out[...] = raw[...].astype(BF16)


def heads_forward(raw, gains, cosine, sine, queries, keys, dim):
    tokens, width = raw.shape
    column = pl.BlockSpec((tokens, dim), lambda h: (0, h))
    table = pl.BlockSpec((tokens, dim), lambda h: (0, 0))
    return pl.pallas_call(
        partial(heads_kernel, queries, keys),
        name="heads_forward",
        grid=(width // dim,),
        out_shape=jax.ShapeDtypeStruct((tokens, width), BF16),
        in_specs=[column, pl.BlockSpec((8, dim), lambda h: (0, 0)), table, table],
        out_specs=column,
    )(raw, gains, cosine, sine)


def heads_back_kernel(queries, keys, raw, grads, gains, cosine, sine, out, gain_out):
    head = pl.program_id(0)

    @pl.when(head < queries + keys)
    def _():
        unit, inverse = normalize(raw[...])
        given = grads[...]
        turned = given * cosine[...] - turn_half(given * sine[...])
        gain_out[...] = jnp.broadcast_to(
            jnp.sum(turned * unit, axis=0, keepdims=True)[None], gain_out.shape
        )
        scaled = turned * jnp.where(head < queries, gains[0:1], gains[1:2])
        out[...] = norm_back(scaled, unit, inverse).astype(BF16)

    @pl.when(head >= queries + keys)
    def _():
        gain_out[...] = jnp.zeros_like(gain_out)
        out[...] = grads[...].astype(BF16)


def heads_backward(raw, grads, gains, cosine, sine, queries, keys, dim):
    tokens, width = raw.shape
    column = pl.BlockSpec((tokens, dim), lambda h: (0, h))
    table = pl.BlockSpec((tokens, dim), lambda h: (0, 0))
    return pl.pallas_call(
        partial(heads_back_kernel, queries, keys),
        name="heads_backward",
        grid=(width // dim,),
        out_shape=[
            jax.ShapeDtypeStruct((tokens, width), BF16),
            jax.ShapeDtypeStruct((width // dim, 8, dim), F32),
        ],
        in_specs=[column, column, pl.BlockSpec((8, dim), lambda h: (0, 0)), table, table],
        out_specs=[column, pl.BlockSpec((1, 8, dim), lambda h: (h, 0, 0))],
    )(raw, grads, gains, cosine, sine)


def allowed_pairs(info, row, block, rows, repeat):
    key_pos = block * rows + lax.broadcasted_iota(jnp.int32, (rows, repeat * rows), 0)
    query_pos = lax.broadcasted_iota(jnp.int32, (rows, repeat * rows), 1)
    query_pos = info[0] * rows + lax.rem(query_pos, rows)
    return (key_pos <= query_pos) & (key_pos < info[1 + row])


def stacked(ref, row, rows, first, repeat, dim):
    return jnp.concatenate(
        [
            ref[row * rows : (row + 1) * rows, (first + r) * dim : (first + r + 1) * dim]
            for r in range(repeat)
        ],
        axis=0,
    )


def attend_kernel(shape, info, q, kv, mixed, mixed_low, log_total, acc, sums):
    rows, keys, repeat, dim = shape
    block = pl.program_id(0)
    scale = 1.0 / math.sqrt(dim)

    @pl.when(block == 0)
    def _():
        acc[...] = jnp.zeros_like(acc)
        sums[...] = jnp.zeros_like(sums)

    @pl.when(block <= info[0])
    def _():
        for row in range(2):
            allowed = allowed_pairs(info, row, block, rows, repeat)
            for k in range(keys):
                unit = row * keys + k
                kk = kv[0, row * rows : (row + 1) * rows, k * dim : (k + 1) * dim]
                vv = kv[0, row * rows : (row + 1) * rows, (keys + k) * dim : (keys + k + 1) * dim]
                scores = nt(kk, stacked(q, row, rows, k * repeat, repeat, dim)) * scale
                weights = jnp.where(allowed, jnp.exp(scores), 0.0)
                sums[unit] += jnp.sum(weights, axis=0, keepdims=True)
                acc[unit] += tn(vv, weights.astype(BF16))

    @pl.when(block == info[0])
    def _():
        for row in range(2):
            for k in range(keys):
                unit = row * keys + k
                log_total[unit] = jnp.log(sums[unit])
                result = (acc[unit] / sums[unit]).T
                for r in range(repeat):
                    piece = result[r * rows : (r + 1) * rows]
                    h = k * repeat + r
                    mixed[row * rows : (row + 1) * rows, h * dim : (h + 1) * dim] = piece
                    mixed_low[row * rows : (row + 1) * rows, h * dim : (h + 1) * dim] = piece.astype(BF16)


def attend(info, q, kv, keys, repeat, dim):
    blocks, tokens, kv_width = kv.shape
    rows, width = tokens // 2, keys * repeat * dim
    whole = lambda j, info: (0, 0)
    return pl.pallas_call(
        partial(attend_kernel, (rows, keys, repeat, dim)),
        name="attend",
        grid_spec=pltpu.PrefetchScalarGridSpec(
            num_scalar_prefetch=1,
            grid=(blocks,),
            in_specs=[
                pl.BlockSpec((tokens, width), whole),
                pl.BlockSpec((1, tokens, kv_width), lambda j, info: (jnp.minimum(j, info[0]), 0, 0)),
            ],
            out_specs=[
                pl.BlockSpec((tokens, width), whole),
                pl.BlockSpec((tokens, width), whole),
                pl.BlockSpec((2 * keys, 1, repeat * rows), lambda j, info: (0, 0, 0)),
            ],
            scratch_shapes=[
                pltpu.VMEM((2 * keys, dim, repeat * rows), F32),
                pltpu.VMEM((2 * keys, 1, repeat * rows), F32),
            ],
        ),
        out_shape=[
            jax.ShapeDtypeStruct((tokens, width), F32),
            jax.ShapeDtypeStruct((tokens, width), BF16),
            jax.ShapeDtypeStruct((2 * keys, 1, repeat * rows), F32),
        ],
        compiler_params=pltpu.CompilerParams(vmem_limit_bytes=32 * 2**20),
    )(info, q, kv)


def attend_back_kernel(shape, info, q, kv, mixed, grad_mixed, log_total, grad_q, grad_kv, acc, delta):
    rows, keys, repeat, dim = shape
    block = pl.program_id(0)
    scale = 1.0 / math.sqrt(dim)

    @pl.when(block == 0)
    def _():
        acc[...] = jnp.zeros_like(acc)
        for row in range(2):
            for k in range(keys):
                product = stacked(mixed, row, rows, k * repeat, repeat, dim) * stacked(
                    grad_mixed, row, rows, k * repeat, repeat, dim
                ).astype(F32)
                delta[row * keys + k] = jnp.sum(product.T, axis=0, keepdims=True)

    @pl.when(block <= info[0])
    def _():
        for row in range(2):
            allowed = allowed_pairs(info, row, block, rows, repeat)
            here = slice(row * rows, (row + 1) * rows)
            for k in range(keys):
                unit = row * keys + k
                kk = kv[0, here, k * dim : (k + 1) * dim]
                vv = kv[0, here, (keys + k) * dim : (keys + k + 1) * dim]
                qq = stacked(q, row, rows, k * repeat, repeat, dim)
                gg = stacked(grad_mixed, row, rows, k * repeat, repeat, dim)
                weights = jnp.where(allowed, jnp.exp(nt(kk, qq) * scale - log_total[unit]), 0.0)
                grad_scores = (weights * (nt(vv, gg) - delta[unit])).astype(BF16)
                grad_kv[0, here, k * dim : (k + 1) * dim] = (nn(grad_scores, qq) * scale).astype(BF16)
                grad_kv[0, here, (keys + k) * dim : (keys + k + 1) * dim] = nn(
                    weights.astype(BF16), gg
                ).astype(BF16)
                acc[unit] += tn(grad_scores, kk)

    @pl.when(block > info[0])
    def _():
        grad_kv[...] = jnp.zeros_like(grad_kv)

    @pl.when(block == info[0])
    def _():
        for row in range(2):
            for k in range(keys):
                for r in range(repeat):
                    h = k * repeat + r
                    grad_q[row * rows : (row + 1) * rows, h * dim : (h + 1) * dim] = (
                        acc[row * keys + k, r * rows : (r + 1) * rows] * scale
                    )


def attend_back(info, q, kv, mixed, grad_mixed, log_total, keys, repeat, dim):
    blocks, tokens, kv_width = kv.shape
    rows, width = tokens // 2, keys * repeat * dim
    whole = lambda j, info: (0, 0)
    full = pl.BlockSpec((tokens, width), whole)
    return pl.pallas_call(
        partial(attend_back_kernel, (rows, keys, repeat, dim)),
        name="attend_back",
        grid_spec=pltpu.PrefetchScalarGridSpec(
            num_scalar_prefetch=1,
            grid=(blocks,),
            in_specs=[
                full,
                pl.BlockSpec((1, tokens, kv_width), lambda j, info: (jnp.minimum(j, info[0]), 0, 0)),
                full,
                full,
                pl.BlockSpec((2 * keys, 1, repeat * rows), lambda j, info: (0, 0, 0)),
            ],
            out_specs=[full, pl.BlockSpec((1, tokens, kv_width), lambda j, info: (j, 0, 0))],
            scratch_shapes=[
                pltpu.VMEM((2 * keys, repeat * rows, dim), F32),
                pltpu.VMEM((2 * keys, 1, repeat * rows), F32),
            ],
        ),
        out_shape=[
            jax.ShapeDtypeStruct((tokens, width), F32),
            jax.ShapeDtypeStruct((blocks, tokens, kv_width), BF16),
        ],
        compiler_params=pltpu.CompilerParams(vmem_limit_bytes=32 * 2**20),
    )(info, q, kv, mixed, grad_mixed, log_total)


def shards(
    tokens,
    lengths,
    attn_gain,
    w_query,
    w_key,
    w_value,
    query_gain,
    key_gain,
    w_out,
    mlp_gain,
    w_gate,
    w_up,
    w_down,
    cotangent,
):
    seq, grp = lax.axis_size("seq"), lax.axis_size("grp")
    seq_index, grp_index = lax.axis_index("seq"), lax.axis_index("grp")
    local_rows, width = tokens.shape[1:]
    rows = local_rows * grp
    dim = query_gain.shape[0]
    queries, keys = w_query.shape[1] // dim, w_key.shape[1] // dim
    repeat = queries // keys
    hidden_units = w_gate.shape[1]

    projections = jnp.concatenate([w_query, w_key, w_value], axis=1)
    full_qkv = lax.all_gather(projections, "seq", axis=0, tiled=True)
    full_out = lax.all_gather(after(w_out.T, full_qkv), "seq", axis=0, tiled=True)
    gate_up = jnp.concatenate([w_gate, w_up], axis=1)

    chunk = attn_gain.shape[0]
    lane = max(128, chunk)
    packed = jnp.zeros((8, lane), F32).at[0, :chunk].set(attn_gain).at[1, :chunk].set(mlp_gain)
    spread_gains = spread(packed, seq, grp, 1)[:, :, :, :chunk].transpose(2, 1, 0, 3)
    gain_attn = spread_gains[0].reshape(-1)
    gain_mlp = spread_gains[1].reshape(-1)
    residual = tokens.astype(F32)
    attn_unit, attn_inverse = normalize(residual)
    token_pos = (seq_index * grp + grp_index) * local_rows + jnp.arange(local_rows, dtype=jnp.int32)
    valid_rows = (token_pos[None, :] < lengths[:, None]).astype(F32)
    cot_rows = cotangent.astype(F32) * valid_rows[:, :, None]
    attn_rows, grad_out_rows = gather_rows(
        [(attn_unit * gain_attn).astype(BF16), cot_rows.astype(BF16)], grp, 2, "gather_inputs"
    )

    raw = nn(attn_rows, full_qkv)
    positions = seq_index * rows + jnp.arange(rows, dtype=jnp.int32)
    half = dim // 2
    frequency = ROPE_BASE ** (-jnp.arange(half, dtype=F32) * 2.0 / dim)
    angles = positions.astype(F32)[:, None] * frequency[None, :]
    cosine = jnp.tile(jnp.cos(angles), (2, 2))
    sine = jnp.tile(jnp.sin(angles), (2, 2))
    head_gains = jnp.zeros((8, dim), F32).at[0].set(query_gain).at[1].set(key_gain)
    heads = heads_forward(raw, head_gains, cosine, sine, queries, keys, dim)
    q, kv_home = heads[:, : queries * dim], heads[:, queries * dim :]
    kv = lax.all_gather(kv_home, "seq", axis=0, tiled=False)
    full_gate_up = lax.all_gather(after(gate_up, kv), "seq", axis=0, tiled=True)
    full_down = lax.all_gather(after(w_down.T, full_gate_up), "seq", axis=0, tiled=True)

    info = jnp.concatenate([seq_index.astype(jnp.int32)[None], lengths])
    mixed, mixed_low, log_total = attend(info, q, kv, keys, repeat, dim)
    hidden = residual + sum_rows(nt(mixed_low, full_out), grp, 3, "sum_attention")

    mlp_unit, mlp_inverse = normalize(hidden)
    (mlp_rows,) = gather_rows([(mlp_unit * gain_mlp).astype(BF16)], grp, 4, "gather_mlp")
    pre = nn(mlp_rows, full_gate_up)
    gate_pre, up_pre = pre[:, :hidden_units], pre[:, hidden_units:]
    inner_low = (jax.nn.silu(gate_pre) * up_pre).astype(BF16)
    grad_w_down = tn(grad_out_rows, inner_low).astype(BF16)
    sum_down = lax.psum_scatter(grad_w_down, "seq", scatter_dimension=0, tiled=True)
    grad_inner = nn(grad_out_rows, full_down)
    sigmoid_gate = jax.nn.sigmoid(gate_pre)
    grad_gate = grad_inner * up_pre * sigmoid_gate * (1.0 + gate_pre * (1.0 - sigmoid_gate))
    grad_up = grad_inner * gate_pre * sigmoid_gate
    grad_pre = jnp.concatenate([grad_gate.astype(BF16), grad_up.astype(BF16)], axis=1)
    grad_w_pre = tn(mlp_rows, grad_pre).astype(BF16)
    sum_pre = lax.psum_scatter(after(grad_w_pre, sum_down), "seq", scatter_dimension=0, tiled=True)
    grad_mlp_in = sum_rows(nt(grad_pre, full_gate_up), grp, 5, "sum_mlp_back")
    grad_gain_mlp = jnp.sum(grad_mlp_in * mlp_unit, axis=(0, 1))
    grad_hidden = cot_rows + norm_back(grad_mlp_in * gain_mlp, mlp_unit, mlp_inverse)
    (grad_branch,) = gather_rows([grad_hidden.astype(BF16)], grp, 6, "gather_branch")

    grad_mixed = nn(grad_branch, full_out).astype(BF16)
    grad_q, grad_kv = attend_back(info, q, kv, mixed, grad_mixed, log_total, keys, repeat, dim)
    sum_kv = lax.psum_scatter(grad_kv, "seq", scatter_dimension=0, tiled=False)
    layer_out = hidden + sum_rows(
        after(nt(inner_low, full_down), grad_kv), grp, 7, "sum_output"
    )
    output = layer_out.astype(BF16)
    grad_heads = jnp.concatenate([grad_q, sum_kv.astype(F32)], axis=1)
    grad_raw, head_gain_parts = heads_backward(
        raw, grad_heads, head_gains, cosine, sine, queries, keys, dim
    )
    grad_w_attn = jnp.concatenate(
        [tn(attn_rows, grad_raw).astype(BF16), tn(grad_branch, mixed_low).astype(BF16)], axis=1
    )
    sum_attn = lax.psum_scatter(after(grad_w_attn, sum_pre), "seq", scatter_dimension=0, tiled=True)
    grad_attn_in = sum_rows(nt(grad_raw, full_qkv), grp, 8, "sum_attention_back")
    grad_gain_attn = jnp.sum(grad_attn_in * attn_unit, axis=(0, 1))
    grad_tokens = grad_hidden + norm_back(grad_attn_in * gain_attn, attn_unit, attn_inverse)

    head_gain_grads = jnp.stack(
        [
            jnp.sum(head_gain_parts[:queries, 0], axis=0),
            jnp.sum(head_gain_parts[queries : queries + keys, 0], axis=0),
        ]
    )
    vector = jnp.concatenate([grad_gain_attn, grad_gain_mlp, head_gain_grads.reshape(-1)])
    padded = -(-vector.shape[0] // 1024) * 1024
    vector = jnp.pad(vector, (0, padded - vector.shape[0])).reshape(-1, 128)
    sums = total(vector, seq, grp, 9).reshape(-1)
    place = (seq_index * grp + grp_index) * chunk
    out_attn_gain = lax.dynamic_slice(sums, (place,), (chunk,))
    out_mlp_gain = lax.dynamic_slice(sums, (width + place,), (chunk,))
    out_query_gain = sums[2 * width : 2 * width + dim]
    out_key_gain = sums[2 * width + dim : 2 * width + 2 * dim]

    sum_attn = sum_attn.astype(F32)
    cuts = (queries * dim, (queries + keys) * dim, (queries + 2 * keys) * dim)
    sum_pre = sum_pre.astype(F32)
    return (
        output,
        grad_tokens,
        out_attn_gain,
        sum_attn[:, : cuts[0]],
        sum_attn[:, cuts[0] : cuts[1]],
        sum_attn[:, cuts[1] : cuts[2]],
        out_query_gain,
        out_key_gain,
        sum_attn[:, cuts[2] :].T,
        out_mlp_gain,
        sum_pre[:, :hidden_units],
        sum_pre[:, hidden_units:],
        sum_down.astype(F32).T,
    )


def solution(mesh):
    rows = P(None, ("seq", "grp"), None)
    vector = P(("seq", "grp"))
    wide, tall = P("seq", "grp"), P("grp", "seq")
    return jax.shard_map(
        shards,
        mesh=mesh,
        in_specs=(
            rows,
            P(),
            vector,
            wide,
            wide,
            wide,
            P(),
            P(),
            tall,
            vector,
            wide,
            wide,
            tall,
            rows,
        ),
        out_specs=(
            rows,
            rows,
            vector,
            wide,
            wide,
            wide,
            P(),
            P(),
            tall,
            vector,
            wide,
            wide,
            tall,
        ),
        check_vma=False,
    )
```

time: 1350 us -> 698 us (0.52)
  waiting for transfers between devices: 857 us -> 345 us
  Pallas kernels: 0 us -> 209 us
  starting transfers between devices: 114 us -> 1 us
  blocking collectives: 79.1 us -> 0 us
  matrix products: 143 us -> 79.3 us
  other arithmetic: 59.7 us -> 15.5 us
  local copies, waits for them, and re-layouts: 62.4 us -> 26.9 us
    reduce_scatter x11 -> x4, waiting for transfers between devices: 376 us -> 151 us  [the longest x1 112 us: shards(): lax.psum_scatter(after(grad_w_pre, sum_down), 'seq', scatter_dimension=0,...]
    pallas_call x0 -> x13, Pallas kernels: none -> 209 us  [the longest x4 83.6 us: sum_rows(): pl.pallas_call(partial(sum_rows_kernel, high), name=name, out_shape=jax.S...]
    all_gather x11 -> x5, waiting for transfers between devices: 365 us -> 193 us  [the longest x1 116 us: shards(): full_gate_up = lax.all_gather(after(gate_up, kv), 'seq', axis=0, tiled=True)]
    ppermute x29 -> x0, waiting for transfers between devices: 113 us -> none  [the longest x21 85.3 us: from_behind(): return lax.ppermute(x, axis, pairs)]
    ppermute x29 -> x0, starting transfers between devices: 113 us -> none  [the longest x21 81.3 us: from_behind(): return lax.ppermute(x, axis, pairs)]
    unnamed x2 -> x0, blocking collectives: 79.1 us -> none
    dot_general x77 -> x12, matrix products: 143 us -> 79.3 us  [the longest x4 30.8 us: nn(): return jnp.dot(a, b, preferred_element_type=F32)]
    convert_element_type x31 -> x7, other arithmetic: 25.7 us -> 2.18 us  [the longest x1 1.16 us: shards(): grad_heads = jnp.concatenate([grad_q, sum_kv.astype(F32)], axis=1)]
  transfers between devices with their start and end apart: 51 -> 9, of which waited for: 42 -> 7; matrix products, arithmetic and copies ran while one was open for 13% -> 11% of each run, Pallas kernels for 0% -> 29%
where the time goes in v1:
time: 698 us; the launch traced here: 691 us
  waiting for transfers between devices  345 us (49%)
  Pallas kernels  209 us (30%)
  matrix products  79.3 us (11%)
  local copies, waits for them, and re-layouts  26.9 us (4%)
  other arithmetic  15.5 us (2%)
  between operations  14.8 us (2%)
    all_gather x1, waiting for transfers between devices, shards(): full_gate_up = lax.all_gather(after(gate_up, kv), 'seq', axis=0, tiled=True)  116 us
    reduce_scatter x1, waiting for transfers between devices, shards(): lax.psum_scatter(after(grad_w_pre, sum_down), 'seq', scatter_dimension=0,...  112 us
    pallas_call x4, Pallas kernels, sum_rows(): pl.pallas_call(partial(sum_rows_kernel, high), name=name, out_shape=jax.S...  83.6 us
    pallas_call x3, Pallas kernels, gather_rows(): pl.pallas_call(partial(gather_rows_kernel, count, high), name=name, out_s...  72.8 us
    all_gather x1, waiting for transfers between devices, shards(): kv = lax.all_gather(kv_home, 'seq', axis=0, tiled=False)  45.7 us
    reduce_scatter x1, waiting for transfers between devices, shards(): sum_kv = lax.psum_scatter(grad_kv, 'seq', scatter_dimension=0, tiled=False)  38.9 us
    dot_general x4, matrix products, nn(): return jnp.dot(a, b, preferred_element_type=F32)  30.8 us
    all_gather x1, waiting for transfers between devices, shards(): lax.all_gather(after(w_out.T, full_qkv), 'seq', axis=0, tiled=True)  26.1 us
  transfers between devices with their start and end apart: 9, of which 7 were waited for; matrix products, arithmetic and copies ran while one was open for 11% of the time, Pallas kernels for 29%

profile of v1, /device:TPU:9, one launch (start us, length us, event | category | flops | bytes accessed | tf_op | source)
XLA Modules:
  0.0 691.3 jit_solution(16979929629061694039)
XLA Ops:
  10.8 9.7 %gather_gains.1 = f32[4,8,8,128]{3,2,1,0:T(8,128)S(1)} custom-call(f32[8,128]{1,0:T(8,128)S(1)} %scatter.15.x_ref), custom_call_target="tpu_custom_call" | custom-call | tf_op jit(solution)/shard_map/gather_gains/pallas_call | solution.py:94
  23.5 36.6 %gather_inputs.1 = (bf16[2,2,2,64,2048]{4,3,2,1,0:T(8,128)(2,1)S(1)}, bf16[2,2,2,64,2048]{4,3,2,1,0:T(8,128)(2,1)S(1)}) custom-call(bf16[2,64,2048]{2,1,0:T(8,128)(2,1)S(1)} %get-tuple-element.142.refs_0_, bf16[2,64,2048]{2,1,0:T(8,128)(2,1)S(1)} %get-tuple-element.143.refs_1_), custom_call_target="tpu_custom_call" | custom-call | tf_op jit(solution)/shard_map/gather_inputs/pallas_call | solution.py:199
  61.5 6.6 fusion.21.raw
  68.1 6.4 heads_forward.1
  78.1 45.7 %all-gather.15.cloned.1.call-done = bf16[4096,512]{1,0:T(8,128)(2,1)} async-done(((bf16[512,512]{1,0:T(8,128)(2,1)}), bf16[4096,512]{1,0:T(8,128)(2,1)}) %all-gather.15.cloned.1.call-update) | async-done | bytes 4194320 | tf_op jit(solution)/shard_map/all_gather | solution.py:578
  124.5 115.6 %all-gather.11.cloned.1.call-done = bf16[2048,3072]{1,0:T(8,128)(2,1)} async-done(((bf16[256,3072]{1,0:T(8,128)(2,1)}), bf16[2048,3072]{1,0:T(8,128)(2,1)}) %all-gather.11.cloned.1.call-update) | async-done | bytes 12582928 | tf_op jit(solution)/shard_map/all_gather | solution.py:579
  240.5 2.2 copy-done
  242.7 6.6 attend.1
  249.4 26.1 %all-gather.9.cloned.1.call-done = bf16[2048,512]{0,1:T(8,128)(2,1)} async-done(((bf16[256,512]{0,1:T(8,128)(2,1)}), bf16[2048,512]{0,1:T(8,128)(2,1)}) %all-gather.9.cloned.1.call-update) | async-done | bytes 2097168 | tf_op jit(solution)/shard_map/all_gather | solution.py:550
  275.4 2.9 convolution_convert_fusion.6
  278.4 20.3 %sum_attention.1 = f32[2,64,2048]{2,1,0:T(8,128)S(1)} custom-call(bf16[2,2,2,64,2048]{4,3,2,1,0:T(8,128)(2,1)S(1)} %bitcast.77), custom_call_target="tpu_custom_call" | custom-call | tf_op jit(solution)/shard_map/sum_attention/pallas_call | solution.py:262
  300.1 18.2 %gather_mlp.1 = bf16[2,2,2,64,2048]{4,3,2,1,0:T(8,128)(2,1)S(1)} custom-call(bf16[2,64,2048]{2,1,0:T(8,128)(2,1)S(1)} %multiply_convert_fusion.3.refs_0_), custom_call_target="tpu_custom_call" | custom-call | tf_op jit(solution)/shard_map/gather_mlp/pallas_call | solution.py:199
  319.6 11.5 %fusion.22 = f32[512,3072]{1,0:T(8,128)} fusion(bf16[512,2048]{1,0:T(8,128)(2,1)S(1)} %bitcast.70, bf16[2048,3072]{1,0:T(8,128)(2,1)} %all-gather.11.cloned.1.call-done), kind=kOutput, calls=%fused_computation.72 | convolution fusion | flops 6442450944 | bytes 20971520 | tf_op jit(solution)/shard_map/dot_general | solution.py:45
  331.0 5.4 all-gather.13.cloned.1.call-done
  336.4 11.5 %multiply_convert_fusion.1 = (bf16[512,1536]{1,0:T(8,128)(2,1)}, bf16[512,1536]{1,0:T(8,128)(2,1)}, bf16[512,1536]{1,0:T(8,128)(2,1)S(1)}) fusion(f32[512,3072]{1,0:T(8,128)} %fusion.22, bf16[512,2048]{1,0:T(8,128)(2,1)} %bitcast.81, bf16[2048,1536]{0,1:T(8,128)(2,1)} %all-gather.13.cloned.1.call-done), kind=kOutput, calls=%fused_computation.6 | convolution fusion | flops 3233808384 | bytes 19398656 | tf_op jit(solution)/shard_map/dot_general | solution.py:45
  349.0 5.4 convolution_convert_fusion.1
  354.7 10.6 %convolution_convert_fusion.3 = bf16[512,2048]{1,0:T(8,128)(2,1)S(1)} fusion(bf16[2048,3072]{1,0:T(8,128)(2,1)} %all-gather.11.cloned.1.call-done, bf16[512,1536]{1,0:T(8,128)(2,1)} %get-tuple-element.124, bf16[512,1536]{1,0:T(8,128)(2,1)} %get-tuple-element.123), kind=kOutput, calls=%fused_computation.9 | convolution fusion | flops 6449790976 | bytes 17825792 | tf_op jit(solution)/shard_map/dot_general | solution.py:37
  365.4 21.1 %sum_mlp_back.1 = f32[2,64,2048]{2,1,0:T(8,128)S(1)} custom-call(bf16[2,2,2,64,2048]{4,3,2,1,0:T(8,128)(2,1)S(1)} %bitcast.76), custom_call_target="tpu_custom_call" | custom-call | tf_op jit(solution)/shard_map/sum_mlp_back/pallas_call | solution.py:262
  387.3 17.9 %gather_branch.1 = bf16[2,2,2,64,2048]{4,3,2,1,0:T(8,128)(2,1)S(1)} custom-call(bf16[2,64,2048]{2,1,0:T(8,128)(2,1)S(1)} %fusion.12.refs_0_), custom_call_target="tpu_custom_call" | custom-call | tf_op jit(solution)/shard_map/gather_branch/pallas_call | solution.py:199
  408.3 8.8 %attend_back.1 = (f32[512,512]{1,0:T(8,128)S(1)}, bf16[8,512,512]{2,1,0:T(8,128)(2,1)S(1)}) custom-call(s32[3]{0:T(128)S(1)} %pad_add_fusion.info, bf16[512,512]{1,0:T(8,128)(2,1)S(1)} %get-tuple-element.131.q, bf16[8,512,512]{2,1,0:T(8,128)(2,1)S(1)} %bitcast.69, f32[512,512]{1,0:T(8,128)S(1)} %get-tuple-element.81.mixed, ...), custom_call_target="tpu_custom_call" | custom-call | tf_op jit(solution)/shard_map/attend_back/pallas_call | solution.py:496
  420.1 11.9 %convolution_convert_fusion = bf16[2048,3072]{1,0:T(8,128)(2,1)} fusion(bf16[512,2048]{1,0:T(8,128)(2,1)} %bitcast.71, bf16[512,1536]{1,0:T(8,128)(2,1)} %get-tuple-element.124, bf16[512,1536]{1,0:T(8,128)(2,1)} %get-tuple-element.123), kind=kOutput, calls=%fused_computation | convolution fusion | flops 6455033856 | bytes 17825792 | tf_op jit(solution)/shard_map/dot_general | solution.py:41
  432.3 4.3 convolution_convert_fusion.5
  436.7 38.9 %reduce-scatter.5.cloned.1.call-done = bf16[1,512,512]{2,1,0:T(8,128)(2,1)} async-done(((bf16[8,512,512]{2,1,0:T(8,128)(2,1)}), bf16[1,512,512]{2,1,0:T(8,128)(2,1)}) %reduce-scatter.5.cloned.1.call-update) | async-done | bytes 524304 | tf_op jit(solution)/shard_map/reduce_scatter | solution.py:607
  478.2 7.2 %heads_backward.1 = (bf16[512,1024]{1,0:T(8,128)(2,1)}, f32[8,8,128]{2,1,0:T(8,128)}) custom-call(f32[512,1024]{1,0:T(8,128)} %fusion.21.raw, f32[512,1024]{1,0:T(8,128)} %pad_maximum_fusion.2.grads, f32[8,128]{1,0:T(8,128)} %copy-done.25, f32[512,128]{1,0:T(8,128)} %copy.32.cosine, f32[512,128]{1,0:T(8,128)} %copy.33.sine), custom_call_target="tpu_custom_call" | custom-call | tf_op jit(solution)/shard_map/heads_backward/pallas_call | solution.py:342
  485.4 4.4 convolution_convert_fusion.2
  489.9 3.5 pad_maximum_fusion
  493.4 111.9 %reduce-scatter.9.cloned.1.call-done = bf16[256,3072]{1,0:T(8,128)(2,1)} async-done(((bf16[2048,3072]{1,0:T(8,128)(2,1)}), bf16[256,3072]{1,0:T(8,128)(2,1)}) %reduce-scatter.9.cloned.1.call-update) | async-done | bytes 1572880 | tf_op jit(solution)/shard_map/reduce_scatter | solution.py:599
  605.3 6.6 fusion.23
  611.9 22.2 %sum_output.1 = f32[2,64,2048]{2,1,0:T(8,128)S(1)} custom-call(bf16[2,2,2,64,2048]{4,3,2,1,0:T(8,128)(2,1)S(1)} %bitcast.74), custom_call_target="tpu_custom_call" | custom-call | tf_op jit(solution)/shard_map/sum_output/pallas_call | solution.py:262
  634.2 2.4 convolution_convert_fusion.4
  636.6 20.0 %sum_attention_back.1 = f32[2,64,2048]{2,1,0:T(8,128)S(1)} custom-call(bf16[2,2,2,64,2048]{4,3,2,1,0:T(8,128)(2,1)S(1)} %bitcast.75), custom_call_target="tpu_custom_call" | custom-call | tf_op jit(solution)/shard_map/sum_attention_back/pallas_call | solution.py:262
  658.4 14.0 %sum_gains.1 = f32[40,128]{1,0:T(8,128)S(1)} custom-call(f32[40,128]{1,0:T(8,128)S(1)} %fusion.13.x_ref), custom_call_target="tpu_custom_call" | custom-call | tf_op jit(solution)/shard_map/sum_gains/pallas_call | solution.py:127
  (144 shorter events, 39.9 us)
Async XLA Ops:
  7.2 13.5 %copy-start.26 = (f32[128]{0:T(128)S(1)}, f32[128]{0:T(128)}, u32[]{:S(2)}) copy-start(f32[128]{0:T(128)} %param.28) | copy-start | bytes 1540
  7.2 54.3 %all-gather.7.cloned.1.call-start = ((), (), s32[]{:S(2)}) async-start(), calls=%async_computation.4 | async-start | bytes 4718592 | tf_op jit(solution)/shard_map/all_gather | solution.py:549
  9.2 13.7 %copy-start.13 = (bf16[2,64,2048]{2,1,0:T(8,128)(2,1)S(1)}, bf16[2,64,2048]{2,1,0:T(8,128)(2,1)}, u32[]{:S(2)}) copy-start(bf16[2,64,2048]{2,1,0:T(8,128)(2,1)} %param.22) | copy-start | bytes 1572868
  9.2 13.9 %copy-start.28 = (s32[2]{0:T(128)S(1)}, s32[2]{0:T(128)}, u32[]{:S(2)}) copy-start(s32[2]{0:T(128)} %param.23) | copy-start | bytes 28
  9.2 13.9 %copy-start.17 = (bf16[2,64,2048]{2,1,0:T(8,128)(2,1)S(1)}, bf16[2,64,2048]{2,1,0:T(8,128)(2,1)}, u32[]{:S(2)}) copy-start(bf16[2,64,2048]{2,1,0:T(8,128)(2,1)} %param.35) | copy-start | bytes 1572868
  9.2 114.6 %all-gather.15.cloned.1.call-start = ((), (), s32[]{:S(2)}) async-start(), calls=%async_computation.12 | async-start | bytes 4718592 | tf_op jit(solution)/shard_map/all_gather | solution.py:578
  22.0 39.5 %copy-start.27 = (f32[128]{0:T(128)S(1)}, f32[128]{0:T(128)}, u32[]{:S(2)}) copy-start(f32[128]{0:T(128)} %param.29) | copy-start | bytes 1540
  61.5 6.6 copy-start.7
  61.5 6.6 copy-start.25
  74.5 2.3 copy-start.22
  74.5 2.3 copy-start.23
  76.7 163.4 %all-gather.11.cloned.1.call-start = ((), (), s32[]{:S(2)}) async-start(), calls=%async_computation.6 | async-start | bytes 14155776 | tf_op jit(solution)/shard_map/all_gather | solution.py:579
  123.9 151.6 %all-gather.9.cloned.1.call-start = ((), (), s32[]{:S(2)}) async-start(), calls=%async_computation.5 | async-start | bytes 2359296 | tf_op jit(solution)/shard_map/all_gather | solution.py:550
  124.4 211.9 %all-gather.13.cloned.1.call-start = ((), (), s32[]{:S(2)}) async-start(), calls=%async_computation.7 | async-start | bytes 7077888 | tf_op jit(solution)/shard_map/all_gather | solution.py:580
  240.1 191.9 %reduce-scatter.7.cloned.1.call-start = ((), (), s32[]{:S(2)}) async-start(), calls=%async_computation.9 | async-start | bytes 7077888 | tf_op jit(solution)/shard_map/reduce_scatter | solution.py:592
  278.3 20.3 %copy-start.14 = (bf16[2,64,2048]{2,1,0:T(8,128)(2,1)S(1)}, bf16[2,64,2048]{2,1,0:T(8,128)(2,1)}, u32[]{:S(2)}) copy-start(bf16[2,64,2048]{2,1,0:T(8,128)(2,1)} %param.22) | copy-start | bytes 1572868
  336.4 12.6 %copy-start.9 = (bf16[2,2,2,64,2048]{4,3,2,1,0:T(8,128)(2,1)S(1)}, bf16[2,2,2,64,2048]{4,3,2,1,0:T(8,128)(2,1)}, u32[]{:S(2)}) copy-start(bf16[2,2,2,64,2048]{4,3,2,1,0:T(8,128)(2,1)} %copy-done.8) | copy-start | bytes 6291460
  354.4 121.1 %reduce-scatter.5.cloned.1.call-start = ((), (), s32[]{:S(2)}) async-start(), calls=%async_computation.8 | async-start | bytes 4718592 | tf_op jit(solution)/shard_map/reduce_scatter | solution.py:607
  365.3 21.1 %copy-start.11 = (f32[2,64,2048]{2,1,0:T(8,128)S(1)}, f32[2,64,2048]{2,1,0:T(8,128)}, u32[]{:S(2)}) copy-start(f32[2,64,2048]{2,1,0:T(8,128)} %copy-done.10) | copy-start | bytes 3145732
  365.3 21.5 %copy-start.18 = (bf16[2,64,2048]{2,1,0:T(8,128)(2,1)S(1)}, bf16[2,64,2048]{2,1,0:T(8,128)(2,1)}, u32[]{:S(2)}) copy-start(bf16[2,64,2048]{2,1,0:T(8,128)(2,1)} %param.35) | copy-start | bytes 1572868
  387.3 18.0 %copy-start.30 = (bf16[2048,512]{0,1:T(8,128)(2,1)S(1)}, bf16[2048,512]{0,1:T(8,128)(2,1)}, u32[]{:S(2)}) copy-start(bf16[2048,512]{0,1:T(8,128)(2,1)} %all-gather.9.cloned.1.call-done) | copy-start | bytes 6291460
  405.2 3.0 copy-start.1
  420.1 185.2 %reduce-scatter.9.cloned.1.call-start = ((), (), s32[]{:S(2)}) async-start(), calls=%async_computation.10 | async-start | bytes 14155776 | tf_op jit(solution)/shard_map/reduce_scatter | solution.py:599
  432.0 247.5 %reduce-scatter.11.cloned.1.call-start = ((), (), s32[]{:S(2)}) async-start(), calls=%async_computation.11 | async-start | bytes 7077888 | tf_op jit(solution)/shard_map/reduce_scatter | solution.py:619
  436.7 40.1 %copy-start.6 = (f32[512,512]{1,0:T(8,128)S(1)}, f32[512,512]{1,0:T(8,128)}, u32[]{:S(2)}) copy-start(f32[512,512]{1,0:T(8,128)} %copy-done.5) | copy-start | bytes 3145732
  485.4 4.4 copy-start.21
  493.4 112.0 %copy-start.33 = (bf16[512,1536]{1,0:T(8,128)(2,1)S(1)}, bf16[512,1536]{1,0:T(8,128)(2,1)}, u32[]{:S(2)}) copy-start(bf16[512,1536]{1,0:T(8,128)(2,1)} %copy-done.32) | copy-start | bytes 4718596
  605.3 28.8 %copy-start.29 = (bf16[2048,1024]{1,0:T(8,128)(2,1)S(1)}, bf16[2048,1024]{1,0:T(8,128)(2,1)}, u32[]{:S(2)}) copy-start(bf16[2048,1024]{1,0:T(8,128)(2,1)} %all-gather.7.cloned.1.call-done) | copy-start | bytes 12582916
  611.9 22.3 %copy-start.31 = (bf16[512,1024]{1,0:T(8,128)(2,1)S(1)}, bf16[512,1024]{1,0:T(8,128)(2,1)}, u32[]{:S(2)}) copy-start(bf16[512,1024]{1,0:T(8,128)(2,1)} %get-tuple-element.87) | copy-start | bytes 3145732
  636.6 21.5 %copy-start.15 = (bf16[2,64,2048]{2,1,0:T(8,128)(2,1)S(1)}, bf16[2,64,2048]{2,1,0:T(8,128)(2,1)}, u32[]{:S(2)}) copy-start(bf16[2,64,2048]{2,1,0:T(8,128)(2,1)} %param.22) | copy-start | bytes 1572868
  636.6 37.0 %copy-start.12 = (f32[2,64,2048]{2,1,0:T(8,128)S(1)}, f32[2,64,2048]{2,1,0:T(8,128)}, u32[]{:S(2)}) copy-start(f32[2,64,2048]{2,1,0:T(8,128)} %copy-done.10) | copy-start | bytes 3145732
  636.6 37.0 %copy-start.19 = (bf16[2,64,2048]{2,1,0:T(8,128)(2,1)S(1)}, bf16[2,64,2048]{2,1,0:T(8,128)(2,1)}, u32[]{:S(2)}) copy-start(bf16[2,64,2048]{2,1,0:T(8,128)(2,1)} %param.35) | copy-start | bytes 1572868
  (11 other events, 16.9 us)
Sparse Core Ops, SparseCore 0:
  10.2 47.1 all-gather.6
  76.8 46.9 all-gather.14
  126.1 113.9 all-gather.10
  241.6 33.8 all-gather.8
  276.9 59.4 all-gather.12
  354.6 69.0 reduce-scatter.6
  425.9 49.6 reduce-scatter.4
  477.9 127.3 reduce-scatter.8
  607.6 71.9 reduce-scatter.10

commit v2 on v1

v2 whole, which is shorter than its diff:
```python
from functools import partial
import math

import jax
import jax.numpy as jnp
from jax import lax
from jax.experimental import pallas as pl
from jax.experimental.pallas import tpu as pltpu
from jax.sharding import PartitionSpec as P

EPSILON = 1e-06
ROPE_BASE = 1000000.0
MESH = pl.DeviceIdType.MESH
ANY = pl.BlockSpec(memory_space=pl.ANY)
VMEM = pl.BlockSpec(memory_space=pltpu.VMEM)
DMA = pltpu.SemaphoreType.DMA
F32 = jnp.float32
BF16 = jnp.bfloat16


def normalize(values):
    inverse = lax.rsqrt(jnp.mean(values * values, axis=-1, keepdims=True) + EPSILON)
    return (values * inverse, inverse)


def norm_back(gradient, unit_values, inverse):
    return inverse * (
        gradient - unit_values * jnp.mean(gradient * unit_values, axis=-1, keepdims=True)
    )


def after(value, earlier):
    return lax.optimization_barrier((value, earlier))[0]


def nt(a, b):
    return lax.dot_general(a, b, (((1,), (1,)), ((), ())), preferred_element_type=F32)


def tn(a, b):
    return lax.dot_general(a, b, (((0,), (0,)), ((), ())), preferred_element_type=F32)


def nn(a, b):
    return jnp.dot(a, b, preferred_element_type=F32)


def comm_params(collective_id, mib=32):
    return pltpu.CompilerParams(
        collective_id=collective_id, has_side_effects=True, vmem_limit_bytes=mib * 2**20
    )


def greet(peers):
    barrier = pltpu.get_barrier_semaphore()
    for peer in peers:
        pl.semaphore_signal(barrier, inc=1, device_id=peer, device_id_type=MESH)
    pl.semaphore_wait(barrier, len(peers))


def send(src, dst, send_sem, recv_sem, peer):
    copy = pltpu.make_async_remote_copy(
        src_ref=src,
        dst_ref=dst,
        send_sem=send_sem,
        recv_sem=recv_sem,
        device_id=peer,
        device_id_type=MESH,
    )
    copy.start()
    return copy


class Riders:
    def __init__(self, kinds, sources, targets, send_sems, recv_sems):
        self.kinds, self.sources, self.targets = kinds, sources, targets
        self.send_sems, self.recv_sems = send_sems, recv_sems
        self.copies = []

    def peers(self):
        s, g = lax.axis_index("seq"), lax.axis_index("grp")
        seq = lax.axis_size("seq")
        where = {"opposite": lax.rem(s + seq // 2, seq), "pair": s + 2 - 4 * lax.rem(s // 2, 2)}
        return [(where[kind], g) for kind in self.kinds]

    def start(self):
        for i, peer in enumerate(self.peers()):
            self.copies.append(
                send(self.sources[i], self.targets[i], self.send_sems.at[i], self.recv_sems.at[i], peer)
            )

    def finish(self):
        for copy in self.copies:
            copy.wait()


def carried_call(kernel, operands, out_shape, in_specs, out_specs, scratch, params, name, riders=()):
    kinds = [kind for kind, _ in riders]
    arrays = [array for _, array in riders]
    count, ins, outs = len(riders), len(in_specs), len(out_specs)

    def body(*refs):
        sources, refs = refs[:count], refs[count:]
        own_in, refs = refs[:ins], refs[ins:]
        targets, refs = refs[:count], refs[count:]
        own_out, refs = refs[:outs], refs[outs:]
        sems, refs = (refs[:2], refs[2:]) if count else ((None, None), refs)
        kernel(Riders(kinds, sources, targets, *sems), *own_in, *own_out, *refs)

    results = pl.pallas_call(
        body,
        name=name,
        out_shape=[jax.ShapeDtypeStruct(x.shape, x.dtype) for x in arrays] + list(out_shape),
        in_specs=[ANY] * count + list(in_specs),
        out_specs=[ANY] * count + list(out_specs),
        scratch_shapes=([DMA((count,)), DMA((count,))] if count else []) + list(scratch),
        compiler_params=params,
    )(*arrays, *operands)
    return list(results[count:]), list(results[:count])


def spread_kernel(seq, grp, riders, x_ref, out_ref, send1, recv1, send2, recv2):
    s, g = lax.axis_index("seq"), lax.axis_index("grp")
    line = [(lax.rem(s + k, seq), g) for k in range(1, seq)]
    plane = [(s, lax.rem(g + k, grp)) for k in range(1, grp)]
    greet(line + plane + riders.peers())
    out_ref[pl.ds(g, 1), pl.ds(s, 1)] = x_ref[...][None, None]
    first = [
        send(x_ref, out_ref.at[g, s], send1.at[k], recv1.at[k], peer) for k, peer in enumerate(line)
    ]
    riders.start()
    for copy in first:
        copy.wait()
    second = [
        send(out_ref.at[g], out_ref.at[g], send2.at[k], recv2.at[k], peer)
        for k, peer in enumerate(plane)
    ]
    for copy in second:
        copy.wait()
    riders.finish()


def spread(block, seq, grp, collective_id, riders=()):
    (result,), arrived = carried_call(
        partial(spread_kernel, seq, grp),
        [block],
        [jax.ShapeDtypeStruct((grp, seq) + block.shape, block.dtype)],
        [VMEM],
        [VMEM],
        [DMA((seq - 1,)), DMA((seq - 1,)), DMA((grp - 1,)), DMA((grp - 1,))],
        comm_params(collective_id),
        "gather_gains",
        riders,
    )
    return result, arrived


def total_kernel(
    seq, grp, riders, x_ref, out_ref, line_buf, part, plane_buf, send1, recv1, send2, recv2
):
    s, g = lax.axis_index("seq"), lax.axis_index("grp")
    line = [(lax.rem(s + k, seq), g) for k in range(1, seq)]
    plane = [(s, lax.rem(g + k, grp)) for k in range(1, grp)]
    greet(line + plane + riders.peers())
    riders.start()
    line_buf[pl.ds(s, 1)] = x_ref[...][None]
    first = [
        send(x_ref, line_buf.at[s], send1.at[k], recv1.at[k], peer) for k, peer in enumerate(line)
    ]
    for copy in first:
        copy.wait()
    part[...] = jnp.sum(line_buf[...], axis=0)
    plane_buf[pl.ds(g, 1)] = part[...][None]
    second = [
        send(part, plane_buf.at[g], send2.at[k], recv2.at[k], peer) for k, peer in enumerate(plane)
    ]
    for copy in second:
        copy.wait()
    out_ref[...] = jnp.sum(plane_buf[...], axis=0)
    riders.finish()


def total(block, seq, grp, collective_id, riders=()):
    (result,), arrived = carried_call(
        partial(total_kernel, seq, grp),
        [block],
        [jax.ShapeDtypeStruct(block.shape, block.dtype)],
        [VMEM],
        [VMEM],
        [
            pltpu.VMEM((seq,) + block.shape, block.dtype),
            pltpu.VMEM(block.shape, block.dtype),
            pltpu.VMEM((grp,) + block.shape, block.dtype),
            DMA((seq - 1,)),
            DMA((seq - 1,)),
            DMA((grp - 1,)),
            DMA((grp - 1,)),
        ],
        comm_params(collective_id),
        "sum_gains",
        riders,
    )
    return result, arrived


def plane_peers(high):
    s, g = lax.axis_index("seq"), lax.axis_index("grp")
    a, b = g // 2, lax.rem(g, 2)
    across = (s, a * 2 + 1 - b)
    along = [(s, lax.rem(a + k, high) * 2 + b) for k in range(1, high)]
    return a, b, across, along


def gather_rows_kernel(count, high, riders, *refs):
    sources, targets = refs[:count], refs[count : 2 * count]
    send_sems, recv_sems, local_sems = refs[2 * count :]
    a, b, across, along = plane_peers(high)
    greet([across] + along + riders.peers())
    riders.start()
    def pusher(i):
        slots = iter(range(4 * high))

        def push(what, where, peer):
            k = next(slots)
            return send(what, where, send_sems.at[i, k], recv_sems.at[i, k], peer)

        return push

    started, local = [], []
    for i in range(count):
        src, dst, push = sources[i], targets[i], pusher(i)
        copy = pltpu.make_async_copy(src, dst.at[:, a, b], local_sems.at[i])
        copy.start()
        local.append(copy)
        over0 = push(src.at[0], dst.at[0, a, b], across)
        up1 = [push(src.at[1], dst.at[1, a, b], peer) for peer in along]
        over1 = push(src.at[1], dst.at[1, a, b], across)
        up0 = [push(src.at[0], dst.at[0, a, b], peer) for peer in along]
        started.append((over0, up1, over1, up0, push))
    for i in range(count):
        dst = targets[i]
        over0, up1, over1, up0, push = started[i]
        over0.wait_recv()
        later = [push(dst.at[0, a, 1 - b], dst.at[0, a, 1 - b], peer) for peer in along]
        for k in range(1, high):
            up1[k - 1].wait_recv()
            origin = lax.rem(a + high - k, high)
            later.append(push(dst.at[1, origin, b], dst.at[1, origin, b], across))
        over1.wait_recv()
        for copy in up0 + later:
            copy.wait_recv()
        for copy in [over0, over1] + up0 + up1 + later:
            copy.wait_send()
        local[i].wait()
    riders.finish()


def gather_rows(arrays, grp, collective_id, name, riders=()):
    count, high = len(arrays), grp // 2
    rows, rest = arrays[0].shape[1:]
    result, arrived = carried_call(
        partial(gather_rows_kernel, count, high),
        arrays,
        [jax.ShapeDtypeStruct((2, high, 2, rows, rest), x.dtype) for x in arrays],
        [ANY] * count,
        [ANY] * count,
        [DMA((count, 4 * high)), DMA((count, 4 * high)), DMA((count,))],
        comm_params(collective_id),
        name,
        riders,
    )
    return [x.reshape(2 * grp * rows, rest) for x in result], arrived


def sum_rows_kernel(high, riders, src, out, recv0, mid0, last0, recv1, mid1, last1, own0, own1, send_sems, recv_sems, local_sems):
    a, b, across, along = plane_peers(high)
    greet([across] + along + riders.peers())
    riders.start()
    slots = iter(range(2 * high))

    def push(what, where, peer):
        k = next(slots)
        return send(what, where, send_sems.at[k], recv_sems.at[k], peer)

    over0 = push(src.at[0, :, 1 - b], recv0, across)
    up1 = [
        push(src.at[1, lax.rem(a + k, high)], recv1.at[k - 1], along[k - 1]) for k in range(1, high)
    ]
    load0 = pltpu.make_async_copy(src.at[0, :, b], own0, local_sems.at[0])
    load1 = pltpu.make_async_copy(src.at[1, a], own1, local_sems.at[1])
    load0.start()
    load1.start()
    load0.wait()
    load1.wait()
    over0.wait_recv()
    mid0[...] = (own0[...].astype(F32) + recv0[...].astype(F32)).astype(BF16)
    up0 = [
        push(mid0.at[lax.rem(a + k, high)], last0.at[k - 1], along[k - 1]) for k in range(1, high)
    ]
    for copy in up1:
        copy.wait_recv()
    joined = own1[...].astype(F32)
    for k in range(1, high):
        joined = joined + recv1[k - 1].astype(F32)
    mid1[...] = joined.astype(BF16)
    over1 = push(mid1.at[1 - b], last1, across)
    for copy in up0:
        copy.wait_recv()
    result = own0[pl.ds(a, 1)][0].astype(F32) + recv0[pl.ds(a, 1)][0].astype(F32)
    for k in range(1, high):
        result = result + last0[k - 1].astype(F32)
    out[0] = result
    over1.wait_recv()
    result = own1[pl.ds(b, 1)][0].astype(F32)
    for k in range(1, high):
        result = result + recv1[k - 1, pl.ds(b, 1)][0].astype(F32)
    out[1] = result + last1[...].astype(F32)
    for copy in [over0, over1] + up0 + up1:
        copy.wait_send()
    riders.finish()


def sum_rows(partial_sums, grp, collective_id, name, riders=()):
    high = grp // 2
    tokens, width = partial_sums.shape
    rows = tokens // (2 * grp)
    parts = partial_sums.astype(BF16).reshape(2, high, 2, rows, width)
    (result,), arrived = carried_call(
        partial(sum_rows_kernel, high),
        [parts],
        [jax.ShapeDtypeStruct((2, rows, width), F32)],
        [ANY],
        [VMEM],
        [
            pltpu.VMEM((high, rows, width), BF16),
            pltpu.VMEM((high, rows, width), BF16),
            pltpu.VMEM((high - 1, rows, width), BF16),
            pltpu.VMEM((high - 1, 2, rows, width), BF16),
            pltpu.VMEM((2, rows, width), BF16),
            pltpu.VMEM((rows, width), BF16),
            pltpu.VMEM((high, rows, width), BF16),
            pltpu.VMEM((2, rows, width), BF16),
            DMA((2 * high,)),
            DMA((2 * high,)),
            DMA((2,)),
        ],
        comm_params(collective_id),
        name,
        riders,
    )
    return result, arrived


def pair_peer():
    s, g = lax.axis_index("seq"), lax.axis_index("grp")
    side = lax.rem(s // 2, 2)
    return side, (s + 2 - 4 * side, g)


def gather_pair_kernel(high, src, dst, send_sems, recv_sems, pair_sems, local_sem):
    a, b, across, along = plane_peers(high)
    side, pair = pair_peer()
    greet([across, pair] + along)
    over_pair = send(src, dst.at[side, :, a, b], pair_sems.at[0], pair_sems.at[1], pair)
    local = pltpu.make_async_copy(src, dst.at[side, :, a, b], local_sem)
    local.start()

    def spread_plane(i, side, first, second):
        slots = iter(range(4 * high))

        def push(what, where, peer):
            k = next(slots)
            return send(what, where, send_sems.at[i, k], recv_sems.at[i, k], peer)

        over0 = push(first, dst.at[side, 0, a, b], across)
        up1 = [push(second, dst.at[side, 1, a, b], peer) for peer in along]
        over1 = push(second, dst.at[side, 1, a, b], across)
        up0 = [push(first, dst.at[side, 0, a, b], peer) for peer in along]
        over0.wait_recv()
        passed = dst.at[side, 0, a, 1 - b]
        later = [push(passed, passed, peer) for peer in along]
        for k in range(1, high):
            up1[k - 1].wait_recv()
            passed = dst.at[side, 1, lax.rem(a + high - k, high), b]
            later.append(push(passed, passed, across))
        return [over1] + up0 + later, [over0] + up1

    late0, early0 = spread_plane(0, side, src.at[0], src.at[1])
    over_pair.wait_recv()
    other = 1 - side
    late1, early1 = spread_plane(1, other, dst.at[other, 0, a, b], dst.at[other, 1, a, b])
    for copy in late0 + late1:
        copy.wait_recv()
    for copy in early0 + early1 + late0 + late1 + [over_pair]:
        copy.wait_send()
    local.wait()


def gather_pair(array, grp, collective_id, name):
    high = grp // 2
    rows, width = array.shape[1:]
    result = pl.pallas_call(
        partial(gather_pair_kernel, high),
        name=name,
        out_shape=jax.ShapeDtypeStruct((2, 2, high, 2, rows, width), array.dtype),
        in_specs=[ANY],
        out_specs=ANY,
        scratch_shapes=[DMA((2, 4 * high)), DMA((2, 4 * high)), DMA((2,)), DMA],
        compiler_params=comm_params(collective_id),
    )(array)
    return result.reshape(4 * grp * rows, width)


def sum_pair_kernel(
    high, riders, src, out, recv0, mid0, last0, recv1, mid1, last1, own0, own1, given, taken, send_sems, recv_sems, pair_sems, local_sems
):
    a, b, across, along = plane_peers(high)
    side, pair = pair_peer()
    greet([across, pair] + along + riders.peers())
    riders.start()

    def pusher(i):
        slots = iter(range(2 * high))

        def push(what, where, peer):
            k = next(slots)
            return send(what, where, send_sems.at[i, k], recv_sems.at[i, k], peer)

        return push

    parts = []
    for i, part in ((0, 1 - side), (1, side)):
        push = pusher(i)
        over0 = push(src.at[part, 0, :, 1 - b], recv0.at[i], across)
        up1 = [
            push(src.at[part, 1, lax.rem(a + k, high)], recv1.at[i, k - 1], along[k - 1])
            for k in range(1, high)
        ]
        load0 = pltpu.make_async_copy(src.at[part, 0, :, b], own0.at[i], local_sems.at[i, 0])
        load1 = pltpu.make_async_copy(src.at[part, 1, a], own1.at[i], local_sems.at[i, 1])
        load0.start()
        load1.start()
        parts.append((push, over0, up1, load0, load1))
    started = []
    for i in range(2):
        push, over0, up1, load0, load1 = parts[i]
        load0.wait()
        load1.wait()
        over0.wait_recv()
        mid0[i] = (own0[i].astype(F32) + recv0[i].astype(F32)).astype(BF16)
        up0 = [
            push(mid0.at[i, lax.rem(a + k, high)], last0.at[i, k - 1], along[k - 1])
            for k in range(1, high)
        ]
        for copy in up1:
            copy.wait_recv()
        joined = own1[i].astype(F32)
        for k in range(1, high):
            joined = joined + recv1[i, k - 1].astype(F32)
        mid1[i] = joined.astype(BF16)
        over1 = push(mid1.at[i, 1 - b], last1.at[i], across)
        started.append((up0, over1))
    over_pair = None
    for i in range(2):
        up0, over1 = started[i]
        for copy in up0:
            copy.wait_recv()
        result0 = own0[i, pl.ds(a, 1)][0].astype(F32) + recv0[i, pl.ds(a, 1)][0].astype(F32)
        for k in range(1, high):
            result0 = result0 + last0[i, k - 1].astype(F32)
        over1.wait_recv()
        result1 = own1[i, pl.ds(b, 1)][0].astype(F32) + last1[i].astype(F32)
        for k in range(1, high):
            result1 = result1 + recv1[i, k - 1, pl.ds(b, 1)][0].astype(F32)
        if i == 0:
            given[0] = result0.astype(BF16)
            given[1] = result1.astype(BF16)
            over_pair = send(given, taken, pair_sems.at[0], pair_sems.at[1], pair)
        else:
            out[0] = result0
            out[1] = result1
    over_pair.wait_recv()
    out[...] += taken[...].astype(F32)
    over_pair.wait_send()
    for i in range(2):
        push, over0, up1, load0, load1 = parts[i]
        up0, over1 = started[i]
        for copy in [over0, over1] + up0 + up1:
            copy.wait_send()
    riders.finish()


def sum_pair(partial_sums, grp, collective_id, name, riders=()):
    high = grp // 2
    tokens, width = partial_sums.shape
    rows = tokens // (4 * grp)
    parts = partial_sums.astype(BF16).reshape(2, 2, high, 2, rows, width)
    (result,), arrived = carried_call(
        partial(sum_pair_kernel, high),
        [parts],
        [jax.ShapeDtypeStruct((2, rows, width), F32)],
        [ANY],
        [VMEM],
        [
            pltpu.VMEM((2, high, rows, width), BF16),
            pltpu.VMEM((2, high, rows, width), BF16),
            pltpu.VMEM((2, high - 1, rows, width), BF16),
            pltpu.VMEM((2, high - 1, 2, rows, width), BF16),
            pltpu.VMEM((2, 2, rows, width), BF16),
            pltpu.VMEM((2, rows, width), BF16),
            pltpu.VMEM((2, high, rows, width), BF16),
            pltpu.VMEM((2, 2, rows, width), BF16),
            pltpu.VMEM((2, rows, width), BF16),
            pltpu.VMEM((2, rows, width), BF16),
            DMA((2, 2 * high)),
            DMA((2, 2 * high)),
            DMA((2,)),
            DMA((2, 2)),
        ],
        comm_params(collective_id),
        name,
        riders,
    )
    return result, arrived


def turn_half(values):
    half = values.shape[-1] // 2
    return jnp.concatenate([-values[:, half:], values[:, :half]], axis=-1)


def heads_kernel(queries, keys, raw, gains, cosine, sine, out):
    head = pl.program_id(0)

    @pl.when(head < queries + keys)
    def _():
        unit, _ = normalize(raw[...])
        scaled = unit * jnp.where(head < queries, gains[0:1], gains[1:2])
        out[...] = (scaled * cosine[...] + turn_half(scaled) * sine[...]).astype(BF16)

    @pl.when(head >= queries + keys)
    def _():
        out[...] = raw[...].astype(BF16)


def heads_forward(raw, gains, cosine, sine, queries, keys, dim):
    tokens, width = raw.shape
    column = pl.BlockSpec((tokens, dim), lambda h: (0, h))
    table = pl.BlockSpec((tokens, dim), lambda h: (0, 0))
    return pl.pallas_call(
        partial(heads_kernel, queries, keys),
        name="heads_forward",
        grid=(width // dim,),
        out_shape=jax.ShapeDtypeStruct((tokens, width), BF16),
        in_specs=[column, pl.BlockSpec((8, dim), lambda h: (0, 0)), table, table],
        out_specs=column,
    )(raw, gains, cosine, sine)


def heads_back_kernel(queries, keys, raw, grads, gains, cosine, sine, out, gain_out):
    head = pl.program_id(0)

    @pl.when(head < queries + keys)
    def _():
        unit, inverse = normalize(raw[...])
        given = grads[...]
        turned = given * cosine[...] - turn_half(given * sine[...])
        gain_out[...] = jnp.broadcast_to(
            jnp.sum(turned * unit, axis=0, keepdims=True)[None], gain_out.shape
        )
        scaled = turned * jnp.where(head < queries, gains[0:1], gains[1:2])
        out[...] = norm_back(scaled, unit, inverse).astype(BF16)

    @pl.when(head >= queries + keys)
    def _():
        gain_out[...] = jnp.zeros_like(gain_out)
        out[...] = grads[...].astype(BF16)


def heads_backward(raw, grads, gains, cosine, sine, queries, keys, dim):
    tokens, width = raw.shape
    column = pl.BlockSpec((tokens, dim), lambda h: (0, h))
    table = pl.BlockSpec((tokens, dim), lambda h: (0, 0))
    return pl.pallas_call(
        partial(heads_back_kernel, queries, keys),
        name="heads_backward",
        grid=(width // dim,),
        out_shape=[
            jax.ShapeDtypeStruct((tokens, width), BF16),
            jax.ShapeDtypeStruct((width // dim, 8, dim), F32),
        ],
        in_specs=[column, column, pl.BlockSpec((8, dim), lambda h: (0, 0)), table, table],
        out_specs=[column, pl.BlockSpec((1, 8, dim), lambda h: (h, 0, 0))],
    )(raw, grads, gains, cosine, sine)


def half_line_peers(chips):
    s, g = lax.axis_index("seq"), lax.axis_index("grp")
    chip, core = s // 2, lax.rem(s, 2)
    place = lax.rem(chip, chips)
    others = [((chip - place + lax.rem(place + k, chips)) * 2 + core, g) for k in range(1, chips)]
    return place, core, (s + 1 - 2 * core, g), others


def remote(src, dst, send_sem, recv_sem, peer):
    return pltpu.make_async_remote_copy(
        src_ref=src,
        dst_ref=dst,
        send_sem=send_sem,
        recv_sem=recv_sem,
        device_id=peer,
        device_id_type=MESH,
    )


def allowed_pairs(query_block, key_block, length, rows, repeat, diagonal):
    key_pos = key_block * rows + lax.broadcasted_iota(jnp.int32, (rows, repeat * rows), 0)
    allowed = key_pos < length
    if diagonal:
        query_pos = lax.broadcasted_iota(jnp.int32, (rows, repeat * rows), 1)
        allowed = allowed & (key_pos <= query_block * rows + lax.rem(query_pos, rows))
    return allowed


def stacked(ref, part, rows, first, repeat, dim):
    return jnp.concatenate(
        [
            ref[part * rows : (part + 1) * rows, (first + r) * dim : (first + r + 1) * dim]
            for r in range(repeat)
        ],
        axis=0,
    )


def attend_kernel(
    shape,
    chips,
    riders,
    length,
    q,
    kv_home,
    mixed,
    mixed_low,
    log_total,
    kv_all,
    kv_buf,
    acc,
    sums,
    lane_send,
    lane_recv,
    cross_send,
    cross_recv,
    local_sems,
):
    rows, keys, repeat, dim = shape
    scale = 1.0 / math.sqrt(dim)
    place, core, cross, others = half_line_peers(chips)
    me = place * 2 + core
    greet([cross] + others + riders.peers())
    home = pltpu.make_async_copy(kv_home, kv_all.at[me], local_sems.at[0])
    home.start()

    def over(i, src, owner):
        return remote(src, kv_all.at[owner], cross_send.at[i], cross_recv.at[i], cross)

    lanes = [
        remote(kv_home, kv_all.at[me], lane_send.at[k], lane_recv.at[k], peer)
        for k, peer in enumerate(others)
    ]
    crossed = [over(0, kv_home, me)]
    for copy in lanes + crossed:
        copy.start()
    riders.start()
    acc[...] = jnp.zeros_like(acc)
    sums[...] = jnp.zeros_like(sums)

    def piece(owner, query_part, key_part, diagonal):
        query_block, key_block = me + query_part * 2 * chips, owner + key_part * 2 * chips
        allowed = allowed_pairs(query_block, key_block, length[0], rows, repeat, diagonal)
        here = slice(key_part * rows, (key_part + 1) * rows)
        for k in range(keys):
            unit = query_part * keys + k
            kk = kv_buf[here, k * dim : (k + 1) * dim]
            vv = kv_buf[here, (keys + k) * dim : (keys + k + 1) * dim]
            scores = nt(kk, stacked(q, query_part, rows, k * repeat, repeat, dim)) * scale
            weights = jnp.where(allowed, jnp.exp(scores), 0.0)
            sums[unit] += jnp.sum(weights, axis=0, keepdims=True)
            acc[unit] += tn(vv, weights.astype(BF16))

    def work(src, owner, own):
        load = pltpu.make_async_copy(src, kv_buf, local_sems.at[1])
        load.start()
        load.wait()
        piece(owner, 1, 0, False)
        if own:
            piece(owner, 0, 0, True)
            piece(owner, 1, 1, True)
        else:

            @pl.when(owner < me)
            def _():
                piece(owner, 0, 0, False)
                piece(owner, 1, 1, False)

    work(kv_home, me, True)
    for k in range(chips):
        near = lax.rem(place + chips - k, chips) * 2
        if k:
            owner = near + core
            lanes[k - 1].wait_recv()
            crossed.append(over(k, kv_all.at[owner], owner))
            crossed[k].start()
            work(kv_all.at[owner], owner, False)
        owner = near + 1 - core
        crossed[k].wait_recv()
        work(kv_all.at[owner], owner, False)
    for part in range(2):
        for k in range(keys):
            unit = part * keys + k
            log_total[unit] = jnp.log(sums[unit])
            result = (acc[unit] / sums[unit]).T
            for r in range(repeat):
                cut = result[r * rows : (r + 1) * rows]
                h = k * repeat + r
                mixed[part * rows : (part + 1) * rows, h * dim : (h + 1) * dim] = cut
                mixed_low[part * rows : (part + 1) * rows, h * dim : (h + 1) * dim] = cut.astype(BF16)
    home.wait()
    for copy in lanes + crossed:
        copy.wait_send()
    riders.finish()


def attend(length, q, kv_home, seq, keys, repeat, dim, collective_id, riders=()):
    tokens, kv_width = kv_home.shape
    rows, width = tokens // 2, keys * repeat * dim
    chips = seq // 4
    return carried_call(
        partial(attend_kernel, (rows, keys, repeat, dim), chips),
        [length, q, kv_home],
        [
            jax.ShapeDtypeStruct((tokens, width), F32),
            jax.ShapeDtypeStruct((tokens, width), BF16),
            jax.ShapeDtypeStruct((2 * keys, 1, repeat * rows), F32),
            jax.ShapeDtypeStruct((2 * chips, tokens, kv_width), BF16),
        ],
        [pl.BlockSpec(memory_space=pltpu.SMEM), VMEM, ANY],
        [VMEM, VMEM, VMEM, ANY],
        [
            pltpu.VMEM((tokens, kv_width), BF16),
            pltpu.VMEM((2 * keys, dim, repeat * rows), F32),
            pltpu.VMEM((2 * keys, 1, repeat * rows), F32),
            DMA((chips,)),
            DMA((chips,)),
            DMA((chips,)),
            DMA((chips,)),
            DMA((2,)),
        ],
        comm_params(collective_id),
        "attend",
        riders,
    )


def attend_back_kernel(
    shape,
    chips,
    length,
    q,
    mixed,
    grad_mixed,
    log_total,
    kv_all,
    grad_q,
    grad_kv,
    kv_buf,
    acc,
    delta,
    mine,
    lane_out,
    lane_in,
    cross_out,
    cross_in,
    lane_send,
    lane_recv,
    cross_send,
    cross_recv,
    local_sem,
):
    rows, keys, repeat, dim = shape
    scale = 1.0 / math.sqrt(dim)
    place, core, cross, others = half_line_peers(chips)
    me = place * 2 + core
    greet([cross] + others)
    acc[...] = jnp.zeros_like(acc)
    for part in range(2):
        for k in range(keys):
            product = stacked(mixed, part, rows, k * repeat, repeat, dim) * stacked(
                grad_mixed, part, rows, k * repeat, repeat, dim
            ).astype(F32)
            delta[part * keys + k] = jnp.sum(product.T, axis=0, keepdims=True)

    def piece(owner, query_part, key_part, diagonal, first):
        query_block, key_block = me + query_part * 2 * chips, owner + key_part * 2 * chips
        allowed = allowed_pairs(query_block, key_block, length[0], rows, repeat, diagonal)
        here = slice(key_part * rows, (key_part + 1) * rows)
        for k in range(keys):
            unit = query_part * keys + k
            key_cut, value_cut = slice(k * dim, (k + 1) * dim), slice((keys + k) * dim, (keys + k + 1) * dim)
            kk, vv = kv_buf[here, key_cut], kv_buf[here, value_cut]
            qq = stacked(q, query_part, rows, k * repeat, repeat, dim)
            gg = stacked(grad_mixed, query_part, rows, k * repeat, repeat, dim)
            weights = jnp.where(allowed, jnp.exp(nt(kk, qq) * scale - log_total[unit]), 0.0)
            grad_scores = (weights * (nt(vv, gg) - delta[unit])).astype(BF16)
            grad_k, grad_v = nn(grad_scores, qq) * scale, nn(weights.astype(BF16), gg)
            if first:
                mine[here, key_cut] = grad_k
                mine[here, value_cut] = grad_v
            else:
                mine[here, key_cut] += grad_k
                mine[here, value_cut] += grad_v
            acc[unit] += tn(grad_scores, kk)

    def work(owner, own):
        load = pltpu.make_async_copy(kv_all.at[owner], kv_buf, local_sem)
        load.start()
        load.wait()
        piece(owner, 1, 0, False, True)
        if own:
            piece(owner, 0, 0, True, False)
            piece(owner, 1, 1, True, True)
        else:

            @pl.when(owner < me)
            def _():
                piece(owner, 0, 0, False, False)
                piece(owner, 1, 1, False, True)

            @pl.when(owner > me)
            def _():
                mine[rows:, :] = jnp.zeros_like(mine[rows:, :])

    lanes, crossed = [], []
    for k in list(range(1, chips)) + [0]:
        near = lax.rem(place + k, chips) * 2
        work(near + 1 - core, False)
        cross_out[k] = mine[...].astype(BF16)
        copy = remote(cross_out.at[k], cross_in.at[k], cross_send.at[k], cross_recv.at[k], cross)
        copy.start()
        crossed.append(copy)
        work(near + core, k == 0)
        copy.wait_recv()
        mine[...] += cross_in[k].astype(F32)
        if k:
            lane_out[k - 1] = mine[...].astype(BF16)
            copy = remote(
                lane_out.at[k - 1], lane_in.at[k - 1], lane_send.at[k - 1], lane_recv.at[k - 1], others[k - 1]
            )
            copy.start()
            lanes.append(copy)
    for k, copy in enumerate(lanes):
        copy.wait_recv()
        mine[...] += lane_in[k].astype(F32)
    grad_kv[...] = mine[...]
    for part in range(2):
        for k in range(keys):
            for r in range(repeat):
                h = k * repeat + r
                grad_q[part * rows : (part + 1) * rows, h * dim : (h + 1) * dim] = (
                    acc[part * keys + k, r * rows : (r + 1) * rows] * scale
                )
    for copy in lanes + crossed:
        copy.wait_send()


def attend_back(length, q, kv_all, mixed, grad_mixed, log_total, keys, repeat, dim, collective_id):
    owners, tokens, kv_width = kv_all.shape
    rows, width = tokens // 2, keys * repeat * dim
    chips = owners // 2
    slots = pltpu.VMEM((chips, tokens, kv_width), BF16)
    return pl.pallas_call(
        partial(attend_back_kernel, (rows, keys, repeat, dim), chips),
        name="attend_back",
        in_specs=[pl.BlockSpec(memory_space=pltpu.SMEM), VMEM, VMEM, VMEM, VMEM, ANY],
        out_specs=[VMEM, VMEM],
        scratch_shapes=[
            pltpu.VMEM((tokens, kv_width), BF16),
            pltpu.VMEM((2 * keys, repeat * rows, dim), F32),
            pltpu.VMEM((2 * keys, 1, repeat * rows), F32),
            pltpu.VMEM((tokens, kv_width), F32),
            slots,
            slots,
            slots,
            slots,
            DMA((chips,)),
            DMA((chips,)),
            DMA((chips,)),
            DMA((chips,)),
            DMA,
        ],
        out_shape=[
            jax.ShapeDtypeStruct((tokens, width), F32),
            jax.ShapeDtypeStruct((tokens, kv_width), F32),
        ],
        compiler_params=comm_params(collective_id, 48),
    )(length, q, mixed, grad_mixed, log_total, kv_all)


def load_weights(own, other, first, weights, sems):
    side = lax.rem(lax.axis_index("seq") // 2, 2)
    members = sems.shape[1]
    depth, width = own.shape[0] // members, weights.shape[1]
    copies = []
    for i in range(members):
        for k, (src, which) in enumerate(((own, side), (other, 1 - side))):
            block = ((i // 2) * 2 + which) * 2 + i % 2
            copy = pltpu.make_async_copy(
                src.at[pl.ds(i * depth, depth), pl.ds(first, width)],
                weights.at[pl.ds(block * depth, depth)],
                sems.at[k, i],
            )
            copy.start()
            copies.append(copy)
    for copy in copies:
        copy.wait()
    return depth


def member_place(block):
    return (block // 4) * 4 + lax.rem(block, 2) * 2 + lax.rem(block // 2, 2)


def mlp_kernel(own, other, rows, cot, inner, grad_pre, grad_down, weights, sems):
    depth = load_weights(own, other, 0, weights, sems)
    units = inner.shape[1]
    step = 256 if units % 256 == 0 else 128
    tile = 256
    tiles = rows.shape[0] // tile

    def one(t, carry):
        here = pl.ds(pl.multiple_of(lax.rem(t, tiles) * tile, tile), tile)
        first = pl.multiple_of((t // tiles) * step, step)
        cols = pl.ds(first, step)
        x = rows[here, :]
        gate = nn(x, weights[:, cols])
        up = nn(x, weights[:, pl.ds(units + first, step)])
        grad = nn(cot[here, :], weights[:, pl.ds(2 * units + first, step)])
        sigmoid = jax.nn.sigmoid(gate)
        silu = gate * sigmoid
        inner[here, cols] = (silu * up).astype(BF16)
        grad_pre[here, cols] = (grad * up * sigmoid * (1.0 + gate * (1.0 - sigmoid))).astype(BF16)
        grad_pre[here, pl.ds(units + first, step)] = (grad * silu).astype(BF16)
        return carry

    lax.fori_loop(0, tiles * (units // step), one, 0)

    def down(j, carry):
        x = cot[:, pl.ds(pl.multiple_of(j * depth, depth), depth)]
        place = pl.multiple_of(member_place(j) * depth, depth)
        grad_down[pl.ds(place, depth), :] = tn(x, inner[...]).astype(BF16)
        return carry

    lax.fori_loop(0, rows.shape[1] // depth, down, 0)


def mlp(own, other, rows, cot):
    (tokens, width), columns = rows.shape, own.shape[1]
    units, members = columns // 3, lax.axis_size("seq") // 2
    return pl.pallas_call(
        mlp_kernel,
        name="mlp",
        in_specs=[ANY, ANY, VMEM, VMEM],
        out_specs=[VMEM, VMEM, VMEM],
        out_shape=[
            jax.ShapeDtypeStruct((tokens, units), BF16),
            jax.ShapeDtypeStruct((tokens, 2 * units), BF16),
            jax.ShapeDtypeStruct((width, units), BF16),
        ],
        scratch_shapes=[pltpu.VMEM((width, columns), BF16), DMA((2, members))],
        compiler_params=pltpu.CompilerParams(vmem_limit_bytes=52 * 2**20),
    )(own, other, rows, cot)


def mlp_back_kernel(own, other, rows, grad_pre, grad_w, grad_rows, weights, sems):
    depth = load_weights(own, other, 0, weights, sems)
    tile = 256

    def one(j, carry):
        x = rows[:, pl.ds(pl.multiple_of(j * depth, depth), depth)]
        place = pl.multiple_of(member_place(j) * depth, depth)
        grad_w[pl.ds(place, depth), :] = tn(x, grad_pre[...]).astype(BF16)
        return carry

    lax.fori_loop(0, rows.shape[1] // depth, one, 0)

    def two(t, carry):
        here = pl.ds(pl.multiple_of(t * tile, tile), tile)
        grad_rows[here, :] = nt(grad_pre[here, :], weights[...]).astype(BF16)
        return carry

    lax.fori_loop(0, rows.shape[0] // tile, two, 0)


def mlp_back(own, other, rows, grad_pre):
    (tokens, width), columns = rows.shape, grad_pre.shape[1]
    return pl.pallas_call(
        mlp_back_kernel,
        name="mlp_back",
        in_specs=[ANY, ANY, VMEM, VMEM],
        out_specs=[VMEM, VMEM],
        out_shape=[
            jax.ShapeDtypeStruct((width, columns), BF16),
            jax.ShapeDtypeStruct((tokens, width), BF16),
        ],
        scratch_shapes=[pltpu.VMEM((width, columns), BF16), DMA((2, lax.axis_size("seq") // 2))],
        compiler_params=pltpu.CompilerParams(vmem_limit_bytes=52 * 2**20),
    )(own, other, rows, grad_pre)


def mlp_out_kernel(own, other, inner, out, weights, sems):
    load_weights(own, other, 2 * inner.shape[1], weights, sems)
    tile = 256

    def one(t, carry):
        here = pl.ds(pl.multiple_of(t * tile, tile), tile)
        out[here, :] = nt(inner[here, :], weights[...]).astype(BF16)
        return carry

    lax.fori_loop(0, inner.shape[0] // tile, one, 0)


def mlp_out(own, other, inner, width):
    tokens, units = inner.shape
    return pl.pallas_call(
        mlp_out_kernel,
        name="mlp_out",
        in_specs=[ANY, ANY, VMEM],
        out_specs=VMEM,
        out_shape=jax.ShapeDtypeStruct((tokens, width), BF16),
        scratch_shapes=[pltpu.VMEM((width, units), BF16), DMA((2, lax.axis_size("seq") // 2))],
        compiler_params=pltpu.CompilerParams(vmem_limit_bytes=52 * 2**20),
    )(own, other, inner)


def shards(
    tokens,
    lengths,
    attn_gain,
    w_query,
    w_key,
    w_value,
    query_gain,
    key_gain,
    w_out,
    mlp_gain,
    w_gate,
    w_up,
    w_down,
    cotangent,
):
    seq, grp = lax.axis_size("seq"), lax.axis_size("grp")
    seq_index, grp_index = lax.axis_index("seq"), lax.axis_index("grp")
    local_rows, width = tokens.shape[1:]
    rows = local_rows * grp
    dim = query_gain.shape[0]
    queries, keys = w_query.shape[1] // dim, w_key.shape[1] // dim
    repeat = queries // keys
    hidden_units = w_gate.shape[1]
    chunk = attn_gain.shape[0]
    depth = width // seq

    line = seq // 2
    row = seq_index // line

    def to_give(values):
        return lax.dynamic_index_in_dim(values, 1 - row, 0, keepdims=False)

    def both_rows(values, taken):
        kept = lax.dynamic_index_in_dim(values, row, 0, keepdims=False)
        return jnp.stack([jnp.where(row == 0, kept, taken), jnp.where(row == 0, taken, kept)])

    blocks = lax.rem(seq_index, line) + jnp.arange(2, dtype=jnp.int32) * line
    length = lax.dynamic_slice(lengths, (row,), (1,))

    side = lax.rem(seq_index // 2, 2)
    half_units = hidden_units // 2
    pairs = [(s, s ^ 2) for s in range(seq)]
    same_side = [[s for s in range(seq) if s // 2 % 2 == k] for k in range(2)]

    def half(which):
        cut = [
            lax.dynamic_slice_in_dim(w, which * half_units, half_units, 1)
            for w in (w_gate, w_up, w_down.T)
        ]
        return jnp.concatenate(cut, axis=1)

    def gather_side(weights):
        return lax.all_gather(weights, "seq", axis=0, tiled=True, axis_index_groups=same_side)

    def sum_side(grads):
        return lax.psum_scatter(
            grads, "seq", scatter_dimension=0, tiled=True, axis_index_groups=same_side
        )

    def half_to_give(sums):
        return lax.dynamic_slice_in_dim(sums, (1 - side) * depth, depth, 0)

    def from_halves(sums, taken, count):
        kept = lax.dynamic_slice_in_dim(sums, side * depth, depth, 0)
        low = jnp.where(side == 0, kept, taken).astype(F32).reshape(depth, count, half_units)
        high = jnp.where(side == 0, taken, kept).astype(F32).reshape(depth, count, half_units)
        return [jnp.concatenate([low[:, i], high[:, i]], axis=1) for i in range(count)]

    projections = jnp.concatenate([w_query, w_key, w_value], axis=1)
    full_qkv = lax.all_gather(projections, "seq", axis=0, tiled=True)
    lane = max(128, chunk)
    packed = jnp.zeros((8, lane), F32).at[0, :chunk].set(attn_gain).at[1, :chunk].set(mlp_gain)
    spread_gains, (taken_tokens,) = spread(packed, seq, grp, 1, [("opposite", to_give(tokens))])
    spread_gains = spread_gains[:, :, :, :chunk].transpose(2, 1, 0, 3)
    gain_attn = spread_gains[0].reshape(-1)
    gain_mlp = spread_gains[1].reshape(-1)
    full_out = lax.all_gather(after(w_out.T, taken_tokens), "seq", axis=0, tiled=True)
    residual = both_rows(tokens, taken_tokens).astype(F32)
    attn_unit, attn_inverse = normalize(residual)
    (attn_rows,), _ = gather_rows([(attn_unit * gain_attn).astype(BF16)], grp, 2, "gather_inputs")
    token_pos = (blocks[:, None] * grp + grp_index) * local_rows
    token_pos = token_pos + jnp.arange(local_rows, dtype=jnp.int32)[None, :]
    valid_rows = (token_pos < length).astype(F32)
    kept_half, given_half = after((half(side), half(1 - side)), attn_rows)

    raw = nn(attn_rows, full_qkv)
    positions = (blocks[:, None] * rows + jnp.arange(rows, dtype=jnp.int32)[None, :]).reshape(-1)
    frequency = ROPE_BASE ** (-jnp.arange(dim // 2, dtype=F32) * 2.0 / dim)
    angles = positions.astype(F32)[:, None] * frequency[None, :]
    cosine = jnp.tile(jnp.cos(angles), (1, 2))
    sine = jnp.tile(jnp.sin(angles), (1, 2))
    head_gains = jnp.zeros((8, dim), F32).at[0].set(query_gain).at[1].set(key_gain)
    heads = heads_forward(raw, head_gains, cosine, sine, queries, keys, dim)
    q, kv_home = heads[:, : queries * dim], heads[:, queries * dim :]

    (mixed, mixed_low, log_total, kv_all), (taken_cotangent,) = attend(
        length, q, kv_home, seq, keys, repeat, dim, 3, [("opposite", to_give(cotangent))]
    )
    own_side = gather_side(after(kept_half, mixed))
    taken_half = lax.ppermute(after(given_half, mixed), "seq", pairs)
    cot_rows = both_rows(cotangent, taken_cotangent).astype(F32) * valid_rows[:, :, None]
    summed, _ = sum_rows(nt(mixed_low, full_out), grp, 4, "sum_attention")
    hidden = residual + summed

    mlp_unit, mlp_inverse = normalize(hidden)
    taken_half, hidden_in = after((taken_half, (mlp_unit * gain_mlp).astype(BF16)), summed)
    other_side = gather_side(taken_half)
    mlp_rows = gather_pair(hidden_in, grp, 5, "gather_mlp")
    grad_out_rows = gather_pair(after(cot_rows.astype(BF16), mlp_rows), grp, 6, "gather_cotangent")
    inner_low, grad_pre, grad_w_down = mlp(own_side, other_side, mlp_rows, grad_out_rows)
    sum_down = sum_side(grad_w_down)
    grad_w_pre, grad_mlp_part = mlp_back(own_side, other_side, mlp_rows, grad_pre)
    sum_pre = sum_side(grad_w_pre)
    grad_mlp_in, _ = sum_pair(grad_mlp_part, grp, 7, "sum_mlp_back")
    grad_gain_mlp = jnp.sum(grad_mlp_in * mlp_unit, axis=(0, 1))
    grad_hidden = cot_rows + norm_back(grad_mlp_in * gain_mlp, mlp_unit, mlp_inverse)
    (grad_branch,), _ = gather_rows([grad_hidden.astype(BF16)], grp, 8, "gather_branch")

    grad_w_out = tn(grad_branch, mixed_low).astype(BF16)
    sum_out = lax.psum_scatter(grad_w_out, "seq", scatter_dimension=0, tiled=True)
    grad_mixed = nn(after(grad_branch, grad_w_out), full_out).astype(BF16)
    grad_q, grad_kv = attend_back(
        length, q, kv_all, mixed, grad_mixed, log_total, keys, repeat, dim, 9
    )
    grad_heads = jnp.concatenate([grad_q, grad_kv], axis=1)
    grad_raw, head_gain_parts = heads_backward(
        raw, grad_heads, head_gains, cosine, sine, queries, keys, dim
    )
    grad_w_qkv = tn(attn_rows, grad_raw).astype(BF16)
    sum_qkv = lax.psum_scatter(grad_w_qkv, "seq", scatter_dimension=0, tiled=True)
    grad_attn_part = nt(after(grad_raw, grad_w_qkv), full_qkv)
    grad_attn_in, _ = sum_rows(grad_attn_part, grp, 10, "sum_attention_back")
    grad_gain_attn = jnp.sum(grad_attn_in * attn_unit, axis=(0, 1))
    grad_tokens = grad_hidden + norm_back(grad_attn_in * gain_attn, attn_unit, attn_inverse)

    out_part = mlp_out(own_side, other_side, after(inner_low, grad_attn_in), width)
    summed, (taken_grads,) = sum_pair(
        out_part, grp, 11, "sum_output", [("opposite", to_give(grad_tokens).astype(BF16))]
    )
    grad_tokens = both_rows(grad_tokens, taken_grads.astype(F32))
    taken_down = lax.ppermute(half_to_give(sum_down), "seq", pairs)
    taken_pre = lax.ppermute(half_to_give(sum_pre), "seq", pairs)
    (out_down,) = from_halves(sum_down, taken_down, 1)
    out_gate, out_up = from_halves(sum_pre, taken_pre, 2)
    output = (hidden + summed).astype(BF16)

    head_gain_grads = jnp.stack(
        [
            jnp.sum(head_gain_parts[:queries, 0], axis=0),
            jnp.sum(head_gain_parts[queries : queries + keys, 0], axis=0),
        ]
    )
    vector = jnp.concatenate([grad_gain_attn, grad_gain_mlp, head_gain_grads.reshape(-1)])
    padded = -(-vector.shape[0] // 1024) * 1024
    vector = jnp.pad(vector, (0, padded - vector.shape[0])).reshape(-1, 128)
    sums, (taken_output,) = total(after(vector, (taken_down, taken_pre)), seq, grp, 12, [("opposite", to_give(output))])
    sums = sums.reshape(-1)
    output = both_rows(output, taken_output)
    place = (seq_index * grp + grp_index) * chunk
    out_attn_gain = lax.dynamic_slice(sums, (place,), (chunk,))
    out_mlp_gain = lax.dynamic_slice(sums, (width + place,), (chunk,))
    out_query_gain = sums[2 * width : 2 * width + dim]
    out_key_gain = sums[2 * width + dim : 2 * width + 2 * dim]

    sum_qkv = sum_qkv.astype(F32)
    cuts = (queries * dim, (queries + keys) * dim)
    return (
        output,
        grad_tokens,
        out_attn_gain,
        sum_qkv[:, : cuts[0]],
        sum_qkv[:, cuts[0] : cuts[1]],
        sum_qkv[:, cuts[1] :],
        out_query_gain,
        out_key_gain,
        sum_out.astype(F32).T,
        out_mlp_gain,
        out_gate,
        out_up,
        out_down.T,
    )


def solution(mesh):
    rows = P(None, ("seq", "grp"), None)
    vector = P(("seq", "grp"))
    wide, tall = P("seq", "grp"), P("grp", "seq")
    return jax.shard_map(
        shards,
        mesh=mesh,
        in_specs=(
            rows,
            P(),
            vector,
            wide,
            wide,
            wide,
            P(),
            P(),
            tall,
            vector,
            wide,
            wide,
            tall,
            rows,
        ),
        out_specs=(
            rows,
            rows,
            vector,
            wide,
            wide,
            wide,
            P(),
            P(),
            tall,
            vector,
            wide,
            wide,
            tall,
        ),
        check_vma=False,
    )
```

time: 698 us -> 625 us (0.90)
  waiting for transfers between devices: 345 us -> 30 us
  Pallas kernels: 209 us -> 470 us
  matrix products: 79.3 us -> 26.6 us
  local copies, waits for them, and re-layouts: 26.9 us -> 43.8 us
  starting transfers between devices: 1 us -> 8.01 us
    pallas_call x11 -> x15, Pallas kernels: 196 us -> 457 us  [the longest x9 288 us: carried_call(): pl.pallas_call(body, name=name, out_shape=[jax.ShapeDtypeStruct(x.shape,...]
    all_gather x4 -> x3, waiting for transfers between devices: 193 us -> 0.01 us  [the longest x2 0.01 us: gather_side(): lax.all_gather(weights, 'seq', axis=0, tiled=True, axis_index_groups=same...]
    reduce_scatter x4, waiting for transfers between devices: 151 us -> 0.01 us  [the longest x2 0.01 us: sum_side(): lax.psum_scatter(grads, 'seq', scatter_dimension=0, tiled=True, axis_inde...]
    ppermute x0 -> x3, waiting for transfers between devices: none -> 29.9 us  [the longest x1 18.6 us: shards(): taken_half = lax.ppermute(after(given_half, mixed), 'seq', pairs)]
    dot_general x4 -> x2, matrix products: 30.8 us -> 9.46 us  [nn(): return jnp.dot(a, b, preferred_element_type=F32)]
    dot_general x4 -> x2, matrix products: 26.1 us -> 9.77 us  [tn(): lax.dot_general(a, b, (((0,), (0,)), ((), ())), preferred_element_type=F32)]
    dot_general x4 -> x2, matrix products: 22.4 us -> 7.4 us  [nt(): lax.dot_general(a, b, (((1,), (1,)), ((), ())), preferred_element_type=F32)]
    ppermute x0 -> x3, starting transfers between devices: none -> 7.04 us  [the longest x1 3.86 us: shards(): taken_half = lax.ppermute(after(given_half, mixed), 'seq', pairs)]
  transfers between devices with their start and end apart: 9 -> 11, of which waited for: 7 -> 3; matrix products, arithmetic and copies ran while one was open for 11% -> 9% of each run, Pallas kernels for 29% -> 67%
where the time goes in v2:
time: 625 us; the launch traced here: 614 us
  Pallas kernels  470 us (75%)
  local copies, waits for them, and re-layouts  43.8 us (7%)
  waiting for transfers between devices  30 us (5%)
  matrix products  26.6 us (4%)
  other arithmetic  20.3 us (3%)
  between operations  15.4 us (2%)
  starting transfers between devices  8.01 us (1%)
    pallas_call x9, Pallas kernels, carried_call(): pl.pallas_call(body, name=name, out_shape=[jax.ShapeDtypeStruct(x.shape,...  288 us
    pallas_call x2, Pallas kernels, gather_pair(): pl.pallas_call(partial(gather_pair_kernel, high), name=name, out_shape=ja...  78.8 us
    pallas_call x1, Pallas kernels, attend_back(): pl.pallas_call(partial(attend_back_kernel, (rows, keys, repeat, dim), chi...  31.3 us
    pallas_call x1, Pallas kernels, mlp(): pl.pallas_call(mlp_kernel, name='mlp', in_specs=[ANY, ANY, VMEM, VMEM], o...  27.2 us
    pallas_call x1, Pallas kernels, mlp_back(): pl.pallas_call(mlp_back_kernel, name='mlp_back', in_specs=[ANY, ANY, VMEM...  23.7 us
    unnamed x85, local copies, waits for them, and re-layouts  22.5 us
    ppermute x1, waiting for transfers between devices, shards(): taken_half = lax.ppermute(after(given_half, mixed), 'seq', pairs)  18.6 us
  transfers between devices with their start and end apart: 11, of which 3 were waited for; matrix products, arithmetic and copies ran while one was open for 9% of the time, Pallas kernels for 67%

profile of v2, /device:TPU:9, one launch (start us, length us, event | category | flops | bytes accessed | tf_op | source)
XLA Modules:
  0.0 614.5 jit_solution(14617473892537118831)
XLA Ops:
  11.8 28.0 %gather_gains.1 = (bf16[64,2048]{1,0:T(8,128)(2,1)S(1)}, f32[4,8,8,128]{3,2,1,0:T(8,128)S(1)}) custom-call(bf16[64,2048]{1,0:T(8,128)(2,1)S(1)} %get-tuple-element.192.refs_0_, f32[8,128]{1,0:T(8,128)S(1)} %scatter.15.refs_1_), custom_call_target="tpu_custom_call" | custom-call | tf_op jit(solution)/shard_map/gather_gains/pallas_call | solution.py:110
  45.3 16.7 %gather_inputs.1 = bf16[2,2,2,64,2048]{4,3,2,1,0:T(8,128)(2,1)S(1)} custom-call(bf16[2,64,2048]{2,1,0:T(8,128)(2,1)S(1)} %fusion.4.refs_0_), custom_call_target="tpu_custom_call" | custom-call | tf_op jit(solution)/shard_map/gather_inputs/pallas_call | solution.py:110
  65.5 5.8 fusion.30.raw
  71.4 6.4 %heads_forward.1 = bf16[512,1024]{1,0:T(8,128)(2,1)} custom-call(f32[512,1024]{1,0:T(8,128)} %fusion.30.raw, f32[8,128]{1,0:T(8,128)} %copy-done.33, f32[512,128]{1,0:T(8,128)} %copy.36.cosine, f32[512,128]{1,0:T(8,128)} %copy.37.sine), custom_call_target="tpu_custom_call" | custom-call | tf_op jit(solution)/shard_map/heads_forward/pallas_call | solution.py:550
  79.0 32.5 %attend.1 = (bf16[64,2048]{1,0:T(8,128)(2,1)S(1)}, f32[512,512]{1,0:T(8,128)S(1)}, bf16[512,512]{1,0:T(8,128)(2,1)S(1)}, f32[4,1,512]{2,1,0:T(1,128)S(1)}, bf16[4,512,512]{2,1,0:T(8,128)(2,1)S(1)}) custom-call(bf16[64,2048]{1,0:T(8,128)(2,1)S(1)} %get-tuple-element.191.refs_0_, s32[1]{0:T(128)} %dynamic_slice.68.refs_1_.length, ...), custom_call_target="tpu_custom_call" | custom-call | tf_op jit(solution)/shard_map/attend/pallas_call | solution.py:110
  113.5 3.9 collective-permute-start
  117.4 2.8 convolution_convert_fusion.3
  120.2 21.5 %sum_attention.1 = f32[2,64,2048]{2,1,0:T(8,128)S(1)} custom-call(bf16[2,2,2,64,2048]{4,3,2,1,0:T(8,128)(2,1)S(1)} %bitcast.118), custom_call_target="tpu_custom_call" | custom-call | tf_op jit(solution)/shard_map/sum_attention/pallas_call | solution.py:110
  143.1 18.6 %collective-permute-done = bf16[256,2304]{1,0:T(8,128)(2,1)} collective-permute-done((bf16[256,2304]{1,0:T(8,128)(2,1)}, bf16[256,2304]{1,0:T(8,128)(2,1)}, u32[]{:S(2)}, u32[]{:S(2)}) %collective-permute-start) | collective-permute-done | bytes 1179680 | tf_op jit(solution)/shard_map/ppermute | solution.py:1144
  164.4 36.7 %gather_mlp.1 = bf16[2,2,2,2,64,2048]{5,4,3,2,1,0:T(8,128)(2,1)S(1)} custom-call(bf16[2,64,2048]{2,1,0:T(8,128)(2,1)S(1)} %multiply_convert_fusion.src), custom_call_target="tpu_custom_call" | custom-call | tf_op jit(solution)/shard_map/gather_mlp/pallas_call | solution.py:402
  201.1 2.0 copy-done
  203.1 42.1 %gather_cotangent.1 = bf16[2,2,2,2,64,2048]{5,4,3,2,1,0:T(8,128)(2,1)S(1)} custom-call(bf16[2,64,2048]{2,1,0:T(8,128)(2,1)S(1)} %fusion.11.src), custom_call_target="tpu_custom_call" | custom-call | tf_op jit(solution)/shard_map/gather_cotangent/pallas_call | solution.py:402
  245.2 2.0 copy-done.1
  247.2 27.2 %mlp.1 = (bf16[1024,768]{1,0:T(8,128)(2,1)S(1)}, bf16[1024,1536]{1,0:T(8,128)(2,1)}, bf16[2048,768]{1,0:T(8,128)(2,1)}) custom-call(bf16[1024,2304]{1,0:T(8,128)(2,1)} %all-gather.9.cloned.1.call-done.own, bf16[1024,2304]{1,0:T(8,128)(2,1)} %all-gather.11.cloned.1.call-done.other, bf16[1024,2048]{1,0:T(8,128)(2,1)} %bitcast.110, bf16[1024,2048]{1,0:T(8,128)(2,1)} %bitcast.112), custom_call_target="tpu_custom_call" | custom-call | tf_op jit(solution)/shard_map/mlp/pallas_call | solution.py:968
  275.6 23.7 %mlp_back.1 = (bf16[2048,1536]{1,0:T(8,128)(2,1)}, bf16[1024,2048]{1,0:T(8,128)(2,1)}) custom-call(bf16[1024,2304]{1,0:T(8,128)(2,1)} %all-gather.9.cloned.1.call-done.own, bf16[1024,2304]{1,0:T(8,128)(2,1)} %all-gather.11.cloned.1.call-done.other, bf16[1024,2048]{1,0:T(8,128)(2,1)} %bitcast.111, bf16[1024,1536]{1,0:T(8,128)(2,1)} %get-tuple-element.106.grad_pre), custom_call_target="tpu_custom_call" | custom-call | tf_op jit(solution)/shard_map/mlp_back/pallas_call | solution.py:1005
  299.4 2.2 copy-done.3
  301.6 45.2 %sum_mlp_back.1 = f32[2,64,2048]{2,1,0:T(8,128)S(1)} custom-call(bf16[2,2,2,2,64,2048]{5,4,3,2,1,0:T(8,128)(2,1)S(1)} %bitcast.114), custom_call_target="tpu_custom_call" | custom-call | tf_op jit(solution)/shard_map/sum_mlp_back/pallas_call | solution.py:110
  348.2 20.4 %gather_branch.1 = bf16[2,2,2,64,2048]{4,3,2,1,0:T(8,128)(2,1)} custom-call(bf16[2,64,2048]{2,1,0:T(8,128)(2,1)S(1)} %fusion.23.refs_0_), custom_call_target="tpu_custom_call" | custom-call | tf_op jit(solution)/shard_map/gather_branch/pallas_call | solution.py:110
  368.6 4.2 convolution_convert_fusion.2
  373.0 3.6 convolution_convert_fusion.4.grad_mixed
  376.7 31.3 %attend_back.1 = (f32[512,512]{1,0:T(8,128)S(1)}, f32[512,512]{1,0:T(8,128)S(1)}) custom-call(s32[1]{0:T(128)} %dynamic_slice.68.refs_1_.length, bf16[512,512]{1,0:T(8,128)(2,1)S(1)} %get-tuple-element.168.refs_2_.q, f32[512,512]{1,0:T(8,128)S(1)} %get-tuple-element.99.mixed, bf16[512,512]{1,0:T(8,128)(2,1)S(1)} %convolution_convert_fusion.4.grad_mixed, ...), custom_call_target="tpu_custom_call" | custom-call | tf_op jit(solution)/shard_map/attend_back/pallas_call | solution.py:880
  409.6 7.2 %heads_backward.1 = (bf16[512,1024]{1,0:T(8,128)(2,1)}, f32[8,8,128]{2,1,0:T(8,128)}) custom-call(f32[512,1024]{1,0:T(8,128)} %fusion.30.raw, f32[512,1024]{1,0:T(8,128)} %pad_maximum_fusion.grads, f32[8,128]{1,0:T(8,128)} %copy-done.33, f32[512,128]{1,0:T(8,128)} %copy.36.cosine, f32[512,128]{1,0:T(8,128)} %copy.37.sine), custom_call_target="tpu_custom_call" | custom-call | tf_op jit(solution)/shard_map/heads_backward/pallas_call | solution.py:584
  416.7 5.6 convolution_convert_fusion
  423.5 4.6 convolution_convert_fusion.1
  428.1 14.2 %sum_attention_back.1 = f32[2,64,2048]{2,1,0:T(8,128)S(1)} custom-call(bf16[2,2,2,64,2048]{4,3,2,1,0:T(8,128)(2,1)S(1)} %bitcast.117), custom_call_target="tpu_custom_call" | custom-call | tf_op jit(solution)/shard_map/sum_attention_back/pallas_call | solution.py:110
  442.3 8.0 %mlp_out.1 = bf16[1024,2048]{1,0:T(8,128)(2,1)} custom-call(bf16[1024,2304]{1,0:T(8,128)(2,1)} %all-gather.9.cloned.1.call-done.own, bf16[1024,2304]{1,0:T(8,128)(2,1)} %all-gather.11.cloned.1.call-done.other, bf16[1024,768]{1,0:T(8,128)(2,1)S(1)} %copy-done.8), custom_call_target="tpu_custom_call" | custom-call | tf_op jit(solution)/shard_map/mlp_out/pallas_call | solution.py:1033
  453.8 78.6 %sum_output.1 = (bf16[64,2048]{1,0:T(8,128)(2,1)S(1)}, f32[2,64,2048]{2,1,0:T(8,128)S(1)}) custom-call(bf16[64,2048]{1,0:T(8,128)(2,1)S(1)} %fusion.14.refs_0_, bf16[2,2,2,2,64,2048]{5,4,3,2,1,0:T(8,128)(2,1)S(1)} %bitcast.113), custom_call_target="tpu_custom_call" | custom-call | tf_op jit(solution)/shard_map/sum_output/pallas_call | solution.py:110
  537.1 3.1 collective-permute-start.1
  550.9 9.4 %collective-permute-done.2 = bf16[256,1536]{1,0:T(8,128)(2,1)} collective-permute-done((bf16[256,1536]{1,0:T(8,128)(2,1)S(1)}, bf16[256,1536]{1,0:T(8,128)(2,1)}, u32[]{:S(2)}, u32[]{:S(2)}) %collective-permute-start.2) | collective-permute-done | bytes 786464 | tf_op jit(solution)/shard_map/ppermute | solution.py:1186
  562.1 2.2 reshape.346
  564.3 3.3 fusion.24
  571.9 30.7 %sum_gains.1 = (bf16[64,2048]{1,0:T(8,128)(2,1)S(1)}, f32[40,128]{1,0:T(8,128)S(1)}) custom-call(bf16[64,2048]{1,0:T(8,128)(2,1)S(1)} %dynamic-slice_bitcast_fusion.refs_0_, f32[40,128]{1,0:T(8,128)S(1)} %fusion.21.refs_1_), custom_call_target="tpu_custom_call" | custom-call | tf_op jit(solution)/shard_map/sum_gains/pallas_call | solution.py:110
  (177 shorter events, 55.5 us)
Async XLA Ops:
  7.2 33.4 %copy-start.34 = (f32[128]{0:T(128)S(1)}, f32[128]{0:T(128)}, u32[]{:S(2)}) copy-start(f32[128]{0:T(128)} %param.28) | copy-start | bytes 1540
  7.2 58.3 %all-gather.5.cloned.1.call-start = ((), (), s32[]{:S(2)}) async-start(), calls=%async_computation.4 | async-start | bytes 4718592 | tf_op jit(solution)/shard_map/all_gather | solution.py:1114
  9.2 108.1 %all-gather.7.cloned.1.call-start = ((), (), s32[]{:S(2)}) async-start(), calls=%async_computation.5 | async-start | bytes 2359296 | tf_op jit(solution)/shard_map/all_gather | solution.py:1121
  9.3 33.2 %copy-start.28 = (bf16[1536,256]{1,0:T(8,128)(2,1)S(1)}, bf16[1536,256]{1,0:T(8,128)(2,1)}, u32[]{:S(2)}) copy-start(bf16[1536,256]{1,0:T(8,128)(2,1)} %param.34) | copy-start | bytes 2359300
  39.8 207.3 %all-gather.9.cloned.1.call-start = ((), (), s32[]{:S(2)}) async-start(), calls=%async_computation.6 | async-start | bytes 5898240 | tf_op jit(solution)/shard_map/all_gather | solution.py:1097
  41.5 2.7 copy-start.32
  44.3 17.7 %copy-start.29 = (bf16[256,1536]{1,0:T(8,128)(2,1)S(1)}, bf16[256,1536]{1,0:T(8,128)(2,1)}, u32[]{:S(2)}) copy-start(bf16[256,1536]{1,0:T(8,128)(2,1)} %param.33) | copy-start | bytes 2359300
  44.3 17.7 %copy-start.30 = (bf16[256,1536]{1,0:T(8,128)(2,1)S(1)}, bf16[256,1536]{1,0:T(8,128)(2,1)}, u32[]{:S(2)}) copy-start(bf16[256,1536]{1,0:T(8,128)(2,1)} %param.32) | copy-start | bytes 2359300
  62.0 3.5 copy-start.4
  65.5 5.9 copy-start.33
  112.9 134.3 %all-gather.11.cloned.1.call-start = ((), (), s32[]{:S(2)}) async-start(), calls=%async_computation.7 | async-start | bytes 5898240 | tf_op jit(solution)/shard_map/all_gather | solution.py:1097
  113.5 48.3 %collective-permute-start = (bf16[256,2304]{1,0:T(8,128)(2,1)}, bf16[256,2304]{1,0:T(8,128)(2,1)}, u32[]{:S(2)}, u32[]{:S(2)}) collective-permute-start(bf16[256,2304]{1,0:T(8,128)(2,1)} %pad_maximum_fusion.4), channel_id=1, source_target_pairs={{0,8},{4,12},{8,0},{12,4},{16,24},{20,28},{24,16},{28,20},{1,9},{5... | collective-permute-start | bytes 3538952 | tf_op jit(solution)/shard_map/ppermute | solution.py:1144
  120.2 21.6 %copy-start.13 = (bf16[1,64,2048]{2,1,0:T(8,128)(2,1)S(1)}, bf16[1,64,2048]{2,1,0:T(8,128)(2,1)}, u32[]{:S(2)}) copy-start(bf16[1,64,2048]{2,1,0:T(8,128)(2,1)} %copy-done.12) | copy-start | bytes 786436
  120.2 21.6 %copy-start.16 = (bf16[1,64,2048]{2,1,0:T(8,128)(2,1)S(1)}, bf16[1,64,2048]{2,1,0:T(8,128)(2,1)}, u32[]{:S(2)}) copy-start(bf16[1,64,2048]{2,1,0:T(8,128)(2,1)} %copy-done.15) | copy-start | bytes 786436
  161.8 374.2 %reduce-scatter.5.cloned.1.call-start = ((), (), s32[]{:S(2)}) async-start(), calls=%async_computation.8 | async-start | bytes 3932160 | tf_op jit(solution)/shard_map/reduce_scatter | solution.py:1100
  163.6 183.6 %copy-start.18 = (bf16[1,64,2048]{2,1,0:T(8,128)(2,1)}, bf16[1,64,2048]{2,1,0:T(8,128)(2,1)S(1)}, u32[]{:S(2)}) copy-start(bf16[1,64,2048]{2,1,0:T(8,128)(2,1)S(1)} %get-tuple-element.171) | copy-start | bytes 786436
  275.5 264.6 %reduce-scatter.7.cloned.1.call-start = ((), (), s32[]{:S(2)}) async-start(), calls=%async_computation.9 | async-start | bytes 7864320 | tf_op jit(solution)/shard_map/reduce_scatter | solution.py:1100
  299.3 242.1 %reduce-scatter.11.cloned.1.call-start = ((), (), s32[]{:S(2)}) async-start(), calls=%async_computation.11 | async-start | bytes 2359296 | tf_op jit(solution)/shard_map/reduce_scatter | solution.py:1164
  301.6 45.2 %copy-start.10 = (f32[2,64,2048]{2,1,0:T(8,128)S(1)}, f32[2,64,2048]{2,1,0:T(8,128)}, u32[]{:S(2)}) copy-start(f32[2,64,2048]{2,1,0:T(8,128)} %copy-done.9) | copy-start | bytes 3145732
  372.8 174.5 %reduce-scatter.9.cloned.1.call-start = ((), (), s32[]{:S(2)}) async-start(), calls=%async_computation.10 | async-start | bytes 4718592 | tf_op jit(solution)/shard_map/reduce_scatter | solution.py:1174
  409.5 7.2 %copy-start.5 = (bf16[2,2,2,64,2048]{4,3,2,1,0:T(8,128)(2,1)S(1)}, bf16[2,2,2,64,2048]{4,3,2,1,0:T(8,128)(2,1)}, u32[]{:S(2)}) copy-start(bf16[2,2,2,64,2048]{4,3,2,1,0:T(8,128)(2,1)} %copy-done.4) | copy-start | bytes 6291460
  428.1 14.2 %copy-start.8 = (bf16[1024,768]{1,0:T(8,128)(2,1)S(1)}, bf16[1024,768]{1,0:T(8,128)(2,1)}, u32[]{:S(2)}) copy-start(bf16[1024,768]{1,0:T(8,128)(2,1)} %copy-done.7) | copy-start | bytes 4718596
  442.3 8.0 %copy-start.14 = (bf16[1,64,2048]{2,1,0:T(8,128)(2,1)S(1)}, bf16[1,64,2048]{2,1,0:T(8,128)(2,1)}, u32[]{:S(2)}) copy-start(bf16[1,64,2048]{2,1,0:T(8,128)(2,1)} %copy-done.12) | copy-start | bytes 786436
  442.3 8.0 %copy-start.17 = (bf16[1,64,2048]{2,1,0:T(8,128)(2,1)S(1)}, bf16[1,64,2048]{2,1,0:T(8,128)(2,1)}, u32[]{:S(2)}) copy-start(bf16[1,64,2048]{2,1,0:T(8,128)(2,1)} %copy-done.15) | copy-start | bytes 786436
  442.3 8.4 %copy-start.19 = (bf16[1,64,2048]{2,1,0:T(8,128)(2,1)S(1)}, bf16[1,64,2048]{2,1,0:T(8,128)(2,1)}, u32[]{:S(2)}) copy-start(bf16[1,64,2048]{2,1,0:T(8,128)(2,1)} %copy-done.18) | copy-start | bytes 786436
  442.3 8.4 %copy-start.22 = (bf16[1,64,2048]{2,1,0:T(8,128)(2,1)S(1)}, bf16[1,64,2048]{2,1,0:T(8,128)(2,1)}, u32[]{:S(2)}) copy-start(bf16[1,64,2048]{2,1,0:T(8,128)(2,1)} %copy-done.20) | copy-start | bytes 786436
  451.6 2.2 copy-start.2
  536.0 9.3 %copy-start.31 = (bf16[512,768]{1,0:T(8,128)(2,1)S(1)}, bf16[512,768]{1,0:T(8,128)(2,1)}, u32[]{:S(2)}) copy-start(bf16[512,768]{1,0:T(8,128)(2,1)} %reduce-scatter.5.cloned.1.call-done) | copy-start | bytes 2359300
  537.1 8.2 %collective-permute-start.1 = (bf16[256,768]{1,0:T(8,128)(2,1)S(1)}, bf16[256,768]{1,0:T(8,128)(2,1)S(1)}, u32[]{:S(2)}, u32[]{:S(2)}) collective-permute-start(bf16[256,768]{1,0:T(8,128)(2,1)S(1)} %constant_dynamic-slice_fusion.1), channel_id=1, source_target_pairs={{0,8},{4,12},{8,0},{12,4},{16,24},{20,28},{24,16},{28,20},{1,9},{5... | collective-permute-start | bytes 1179656 | tf_op jit(solution)/shard_map/ppermute | solution.py:1185
  541.3 19.0 %collective-permute-start.2 = (bf16[256,1536]{1,0:T(8,128)(2,1)S(1)}, bf16[256,1536]{1,0:T(8,128)(2,1)}, u32[]{:S(2)}, u32[]{:S(2)}) collective-permute-start(bf16[256,1536]{1,0:T(8,128)(2,1)S(1)} %constant_dynamic-slice_fusion), channel_id=1, source_target_pairs={{0,8},{4,12},{8,0},{12,4},{16,24},{20,28},{24,16},{28,20},{1,9},{5... | collective-permute-start | bytes 2359304 | tf_op jit(solution)/shard_map/ppermute | solution.py:1186
  571.7 30.8 %copy-start.26 = (bf16[2,64,2048]{2,1,0:T(8,128)(2,1)S(1)}, bf16[2,64,2048]{2,1,0:T(8,128)(2,1)}, u32[]{:S(2)}) copy-start(bf16[2,64,2048]{2,1,0:T(8,128)(2,1)} %copy-done.25) | copy-start | bytes 1572868
  571.7 31.4 %copy-start.23 = (f32[256,1,768]{2,0,1:T(8,128)S(1)}, f32[256,1,768]{2,0,1:T(8,128)}, u32[]{:S(2)}) copy-start(f32[256,1,768]{2,0,1:T(8,128)} %copy.61) | copy-start | bytes 2359300
  (17 other events, 23.6 us)
Sparse Core Ops, SparseCore 0:
  10.2 51.2 all-gather.4
  63.1 38.5 all-gather.6
  113.0 63.0 all-gather.8
  177.5 62.5 all-gather.10
  275.7 59.2 reduce-scatter.4
  337.5 91.6 reduce-scatter.6
  431.5 35.1 reduce-scatter.10
  469.0 65.7 reduce-scatter.8

commit v3 on v2

v3 whole, which is shorter than its diff:
```python
from functools import partial
import math

import jax
import jax.numpy as jnp
from jax import lax
from jax.experimental import pallas as pl
from jax.experimental.pallas import tpu as pltpu
from jax.sharding import PartitionSpec as P

EPSILON = 1e-06
ROPE_BASE = 1000000.0
MESH = pl.DeviceIdType.MESH
ANY = pl.BlockSpec(memory_space=pltpu.HBM)
VMEM = pl.BlockSpec(memory_space=pltpu.VMEM)
DMA = pltpu.SemaphoreType.DMA
F32 = jnp.float32
BF16 = jnp.bfloat16


def normalize(values):
    inverse = lax.rsqrt(jnp.mean(values * values, axis=-1, keepdims=True) + EPSILON)
    return (values * inverse, inverse)


def norm_back(gradient, unit_values, inverse):
    return inverse * (
        gradient - unit_values * jnp.mean(gradient * unit_values, axis=-1, keepdims=True)
    )


def after(value, earlier):
    return lax.optimization_barrier((value, earlier))[0]


def nt(a, b):
    return lax.dot_general(a, b, (((1,), (1,)), ((), ())), preferred_element_type=F32)


def tn(a, b):
    return lax.dot_general(a, b, (((0,), (0,)), ((), ())), preferred_element_type=F32)


def nn(a, b):
    return jnp.dot(a, b, preferred_element_type=F32)


NO_COST = pl.CostEstimate(flops=1, bytes_accessed=1, transcendentals=0)


def comm_params(collective_id, mib=32):
    return pltpu.CompilerParams(
        collective_id=collective_id, has_side_effects=True, vmem_limit_bytes=mib * 2**20
    )


def greet(peers):
    barrier = pltpu.get_barrier_semaphore()
    for peer in peers:
        pl.semaphore_signal(barrier, inc=1, device_id=peer, device_id_type=MESH)
    pl.semaphore_wait(barrier, len(peers))


def send(src, dst, send_sem, recv_sem, peer):
    copy = pltpu.make_async_remote_copy(
        src_ref=src,
        dst_ref=dst,
        send_sem=send_sem,
        recv_sem=recv_sem,
        device_id=peer,
        device_id_type=MESH,
    )
    copy.start()
    return copy


def peer_of(kind):
    s, g = lax.axis_index("seq"), lax.axis_index("grp")
    line = lax.axis_size("seq") // 2
    if kind == "opposite":
        return lax.rem(s + line, 2 * line), g
    if kind == "core":
        return s + 1 - 2 * lax.rem(s, 2), g
    place = lax.rem(s, line)
    return s - place + lax.rem(place + 2 * kind, line), g


def part_of(kind, part):
    s = lax.axis_index("seq")
    line = lax.axis_size("seq") // 2
    if part == "row":
        return 1 - s // line
    return lax.rem(lax.rem(s, line) + 2 * kind, line) // 2


class Riders:
    def __init__(self, kinds, parts, sources, targets, send_sems, recv_sems):
        self.kinds, self.parts, self.sources, self.targets = kinds, parts, sources, targets
        self.send_sems, self.recv_sems = send_sems, recv_sems
        self.copies = []

    def peers(self):
        return [peer_of(kind) for kind in dict.fromkeys(self.kinds)]

    def start(self):
        for i, (kind, part) in enumerate(zip(self.kinds, self.parts)):
            src = self.sources[i] if part is None else self.sources[i].at[part_of(kind, part)]
            self.copies.append(
                send(src, self.targets[i], self.send_sems.at[i], self.recv_sems.at[i], peer_of(kind))
            )

    def finish(self):
        for copy in self.copies:
            copy.wait()


def carried_call(kernel, operands, out_shape, in_specs, out_specs, scratch, params, name, riders=()):
    riders = [rider if len(rider) == 3 else rider + (None,) for rider in riders]
    kinds, parts = [rider[0] for rider in riders], [rider[2] for rider in riders]
    arrays = [rider[1] for rider in riders]
    carried = [x.shape if part is None else x.shape[1:] for x, part in zip(arrays, parts)]
    count, ins, outs = len(arrays), len(in_specs), len(out_specs)

    def body(*refs):
        sources, refs = refs[:count], refs[count:]
        own_in, refs = refs[:ins], refs[ins:]
        targets, refs = refs[:count], refs[count:]
        own_out, refs = refs[:outs], refs[outs:]
        sems, refs = (refs[:2], refs[2:]) if count else ((None, None), refs)
        kernel(Riders(kinds, parts, sources, targets, *sems), *own_in, *own_out, *refs)

    results = pl.pallas_call(
        body,
        name=name,
        cost_estimate=NO_COST,
        out_shape=[jax.ShapeDtypeStruct(shape, x.dtype) for shape, x in zip(carried, arrays)]
        + list(out_shape),
        in_specs=[ANY] * count + list(in_specs),
        out_specs=[ANY] * count + list(out_specs),
        scratch_shapes=([DMA((count,)), DMA((count,))] if count else []) + list(scratch),
        compiler_params=params,
    )(*arrays, *operands)
    return list(results[count:]), list(results[:count])


def spread_kernel(seq, grp, riders, x_ref, out_ref, send1, recv1, send2, recv2):
    s, g = lax.axis_index("seq"), lax.axis_index("grp")
    line = [(lax.rem(s + k, seq), g) for k in range(1, seq)]
    plane = [(s, lax.rem(g + k, grp)) for k in range(1, grp)]
    greet(line + plane + riders.peers())
    out_ref[pl.ds(g, 1), pl.ds(s, 1)] = x_ref[...][None, None]
    first = [
        send(x_ref, out_ref.at[g, s], send1.at[k], recv1.at[k], peer) for k, peer in enumerate(line)
    ]
    riders.start()
    for copy in first:
        copy.wait()
    second = [
        send(out_ref.at[g], out_ref.at[g], send2.at[k], recv2.at[k], peer)
        for k, peer in enumerate(plane)
    ]
    for copy in second:
        copy.wait()
    riders.finish()


def spread(block, seq, grp, collective_id, riders=()):
    (result,), arrived = carried_call(
        partial(spread_kernel, seq, grp),
        [block],
        [jax.ShapeDtypeStruct((grp, seq) + block.shape, block.dtype)],
        [VMEM],
        [VMEM],
        [DMA((seq - 1,)), DMA((seq - 1,)), DMA((grp - 1,)), DMA((grp - 1,))],
        comm_params(collective_id),
        "gather_gains",
        riders,
    )
    return result, arrived


def total_kernel(
    seq, grp, riders, x_ref, out_ref, line_buf, part, plane_buf, send1, recv1, send2, recv2
):
    s, g = lax.axis_index("seq"), lax.axis_index("grp")
    line = [(lax.rem(s + k, seq), g) for k in range(1, seq)]
    plane = [(s, lax.rem(g + k, grp)) for k in range(1, grp)]
    greet(line + plane + riders.peers())
    riders.start()
    line_buf[pl.ds(s, 1)] = x_ref[...][None]
    first = [
        send(x_ref, line_buf.at[s], send1.at[k], recv1.at[k], peer) for k, peer in enumerate(line)
    ]
    for copy in first:
        copy.wait()
    part[...] = jnp.sum(line_buf[...], axis=0)
    plane_buf[pl.ds(g, 1)] = part[...][None]
    second = [
        send(part, plane_buf.at[g], send2.at[k], recv2.at[k], peer) for k, peer in enumerate(plane)
    ]
    for copy in second:
        copy.wait()
    out_ref[...] = jnp.sum(plane_buf[...], axis=0)
    riders.finish()


def total(block, seq, grp, collective_id, riders=()):
    (result,), arrived = carried_call(
        partial(total_kernel, seq, grp),
        [block],
        [jax.ShapeDtypeStruct(block.shape, block.dtype)],
        [VMEM],
        [VMEM],
        [
            pltpu.VMEM((seq,) + block.shape, block.dtype),
            pltpu.VMEM(block.shape, block.dtype),
            pltpu.VMEM((grp,) + block.shape, block.dtype),
            DMA((seq - 1,)),
            DMA((seq - 1,)),
            DMA((grp - 1,)),
            DMA((grp - 1,)),
        ],
        comm_params(collective_id),
        "sum_gains",
        riders,
    )
    return result, arrived


def plane_peers(high):
    s, g = lax.axis_index("seq"), lax.axis_index("grp")
    a, b = g // 2, lax.rem(g, 2)
    across = (s, a * 2 + 1 - b)
    along = [(s, lax.rem(a + k, high) * 2 + b) for k in range(1, high)]
    return a, b, across, along


class PlaneGather:
    def __init__(self, high, first, second, target, send_sems, recv_sems):
        self.high, self.first, self.second, self.target = high, first, second, target
        self.send_sems, self.recv_sems = send_sems, recv_sems
        self.slots = iter(range(4 * high))
        self.place = plane_peers(high)

    def push(self, what, where, peer):
        k = next(self.slots)
        return send(what, where, self.send_sems.at[k], self.recv_sems.at[k], peer)

    def start(self):
        a, b, across, along = self.place
        here0, here1 = self.target.at[0, a, b], self.target.at[1, a, b]
        self.early = [self.push(self.first, here0, across)]
        self.early += [self.push(self.second, here1, peer) for peer in along]
        self.late = [self.push(self.second, here1, across)]
        self.late += [self.push(self.first, here0, peer) for peer in along]

    def forward(self):
        a, b, across, along = self.place
        self.early[0].wait_recv()
        passed = self.target.at[0, a, 1 - b]
        self.late += [self.push(passed, passed, peer) for peer in along]
        for k in range(1, self.high):
            self.early[k].wait_recv()
            passed = self.target.at[1, lax.rem(a + self.high - k, self.high), b]
            self.late.append(self.push(passed, passed, across))

    def finish(self):
        for copy in self.late:
            copy.wait_recv()
        for copy in self.early + self.late:
            copy.wait_send()


def gather_rows_kernel(high, riders, src, dst, send_sems, recv_sems, local_sem):
    a, b, across, along = plane_peers(high)
    greet([across] + along + riders.peers())
    riders.start()
    home = pltpu.make_async_copy(src, dst.at[:, a, b], local_sem)
    home.start()
    plane = PlaneGather(high, src.at[0], src.at[1], dst, send_sems, recv_sems)
    plane.start()
    plane.forward()
    plane.finish()
    home.wait()
    riders.finish()


def plane_shape(array, grp):
    rows, width = array.shape[1:]
    return jax.ShapeDtypeStruct((2, grp // 2, 2, rows, width), array.dtype)


def gather_rows(array, grp, collective_id, name, riders=()):
    high = grp // 2
    (result,), arrived = carried_call(
        partial(gather_rows_kernel, high),
        [array],
        [plane_shape(array, grp)],
        [ANY],
        [ANY],
        [DMA((4 * high,)), DMA((4 * high,)), DMA],
        comm_params(collective_id),
        name,
        riders,
    )
    return result.reshape(2 * grp * array.shape[1], array.shape[2]), arrived


def sum_rows_kernel(high, riders, src, out, recv0, mid0, last0, recv1, mid1, last1, own0, own1, send_sems, recv_sems, local_sems):
    a, b, across, along = plane_peers(high)
    greet([across] + along + riders.peers())
    riders.start()
    slots = iter(range(2 * high))

    def push(what, where, peer):
        k = next(slots)
        return send(what, where, send_sems.at[k], recv_sems.at[k], peer)

    over0 = push(src.at[0, :, 1 - b], recv0, across)
    up1 = [
        push(src.at[1, lax.rem(a + k, high)], recv1.at[k - 1], along[k - 1]) for k in range(1, high)
    ]
    load0 = pltpu.make_async_copy(src.at[0, :, b], own0, local_sems.at[0])
    load1 = pltpu.make_async_copy(src.at[1, a], own1, local_sems.at[1])
    load0.start()
    load1.start()
    load0.wait()
    load1.wait()
    over0.wait_recv()
    mid0[...] = (own0[...].astype(F32) + recv0[...].astype(F32)).astype(BF16)
    up0 = [
        push(mid0.at[lax.rem(a + k, high)], last0.at[k - 1], along[k - 1]) for k in range(1, high)
    ]
    for copy in up1:
        copy.wait_recv()
    joined = own1[...].astype(F32)
    for k in range(1, high):
        joined = joined + recv1[k - 1].astype(F32)
    mid1[...] = joined.astype(BF16)
    over1 = push(mid1.at[1 - b], last1, across)
    for copy in up0:
        copy.wait_recv()
    result = own0[pl.ds(a, 1)][0].astype(F32) + recv0[pl.ds(a, 1)][0].astype(F32)
    for k in range(1, high):
        result = result + last0[k - 1].astype(F32)
    out[0] = result
    over1.wait_recv()
    result = own1[pl.ds(b, 1)][0].astype(F32)
    for k in range(1, high):
        result = result + recv1[k - 1, pl.ds(b, 1)][0].astype(F32)
    out[1] = result + last1[...].astype(F32)
    for copy in [over0, over1] + up0 + up1:
        copy.wait_send()
    riders.finish()


def sum_rows(partial_sums, grp, collective_id, name, riders=()):
    high = grp // 2
    tokens, width = partial_sums.shape
    rows = tokens // (2 * grp)
    parts = partial_sums.astype(BF16).reshape(2, high, 2, rows, width)
    (result,), arrived = carried_call(
        partial(sum_rows_kernel, high),
        [parts],
        [jax.ShapeDtypeStruct((2, rows, width), F32)],
        [ANY],
        [VMEM],
        [
            pltpu.VMEM((high, rows, width), BF16),
            pltpu.VMEM((high, rows, width), BF16),
            pltpu.VMEM((high - 1, rows, width), BF16),
            pltpu.VMEM((high - 1, 2, rows, width), BF16),
            pltpu.VMEM((2, rows, width), BF16),
            pltpu.VMEM((rows, width), BF16),
            pltpu.VMEM((high, rows, width), BF16),
            pltpu.VMEM((2, rows, width), BF16),
            DMA((2 * high,)),
            DMA((2 * high,)),
            DMA((2,)),
        ],
        comm_params(collective_id),
        name,
        riders,
    )
    return result, arrived


def pair_peer():
    s, g = lax.axis_index("seq"), lax.axis_index("grp")
    line = lax.axis_size("seq") // 2
    return s // line, (lax.rem(s + line, 2 * line), g)


def gather_pair_kernel(
    high, riders, src, beside, dst, beside_dst, send_sems, recv_sems, pair_sems, local_sems
):
    a, b, across, along = plane_peers(high)
    _, pair = pair_peer()
    greet([across, pair] + along + riders.peers())
    over_pair = send(src, dst.at[1, :, a, b], pair_sems.at[0], pair_sems.at[1], pair)
    riders.start()
    homes = [
        pltpu.make_async_copy(src, dst.at[0, :, a, b], local_sems.at[0]),
        pltpu.make_async_copy(beside, beside_dst.at[:, a, b], local_sems.at[1]),
    ]
    for copy in homes:
        copy.start()
    given = dst.at[1, :, a, b]
    planes = [
        PlaneGather(high, first, second, target, send_sems.at[i], recv_sems.at[i])
        for i, (first, second, target) in enumerate(
            (
                (src.at[0], src.at[1], dst.at[0]),
                (beside.at[0], beside.at[1], beside_dst),
                (given.at[0], given.at[1], dst.at[1]),
            )
        )
    ]
    planes[0].start()
    planes[1].start()
    planes[0].forward()
    over_pair.wait_recv()
    planes[2].start()
    planes[1].forward()
    planes[2].forward()
    for plane in planes:
        plane.finish()
    over_pair.wait_send()
    for copy in homes:
        copy.wait()
    riders.finish()


def gather_pair(array, beside, grp, collective_id, name, riders=()):
    high = grp // 2
    rows, width = array.shape[1:]
    both = jax.ShapeDtypeStruct((2,) + plane_shape(array, grp).shape, array.dtype)
    (result, beside), arrived = carried_call(
        partial(gather_pair_kernel, high),
        [array, beside],
        [both, plane_shape(beside, grp)],
        [ANY, ANY],
        [ANY, ANY],
        [DMA((3, 4 * high)), DMA((3, 4 * high)), DMA((2,)), DMA((2,))],
        comm_params(collective_id, 60),
        name,
        riders,
    )
    result, beside = result.reshape(4 * grp * rows, width), beside.reshape(2, grp * rows, width)
    return result, beside, arrived


class PairSum:
    def __init__(self, high, src, out, scratch):
        self.high, self.src, self.out = high, src, out
        self.recv0, self.mid0, self.last0, self.recv1, self.mid1, self.last1 = scratch[:6]
        self.own0, self.own1, self.given, self.taken = scratch[6:10]
        self.send_sems, self.recv_sems, self.pair_sems, self.local_sems = scratch[10:]
        self.place = plane_peers(high)
        self.pair = pair_peer()[1]
        self.slots = [iter(range(2 * high)), iter(range(2 * high))]
        self.sent, self.first, self.second = [[], []], [None, None], [None, None]

    @staticmethod
    def scratch(high, rows, width):
        return [
            pltpu.VMEM((2, high, rows, width), BF16),
            pltpu.VMEM((2, high, rows, width), BF16),
            pltpu.VMEM((2, high - 1, rows, width), BF16),
            pltpu.VMEM((2, high - 1, 2, rows, width), BF16),
            pltpu.VMEM((2, 2, rows, width), BF16),
            pltpu.VMEM((2, rows, width), BF16),
            pltpu.VMEM((2, high, rows, width), BF16),
            pltpu.VMEM((2, 2, rows, width), BF16),
            pltpu.VMEM((2, rows, width), BF16),
            pltpu.VMEM((2, rows, width), BF16),
            DMA((2, 2 * high)),
            DMA((2, 2 * high)),
            DMA((2,)),
            DMA((2, 2)),
        ]

    def push(self, i, what, where, peer):
        k = next(self.slots[i])
        copy = send(what, where, self.send_sems.at[i, k], self.recv_sems.at[i, k], peer)
        self.sent[i].append(copy)
        return copy

    def start(self, i):
        a, b, across, along = self.place
        part = self.src.at[1 - i]
        over0 = self.push(i, part.at[0, :, 1 - b], self.recv0.at[i], across)
        up1 = [
            self.push(i, part.at[1, lax.rem(a + k, self.high)], self.recv1.at[i, k - 1], along[k - 1])
            for k in range(1, self.high)
        ]
        loads = [
            pltpu.make_async_copy(part.at[0, :, b], self.own0.at[i], self.local_sems.at[i, 0]),
            pltpu.make_async_copy(part.at[1, a], self.own1.at[i], self.local_sems.at[i, 1]),
        ]
        for load in loads:
            load.start()
        self.first[i] = (over0, up1, loads)

    def middle(self, i):
        a, b, across, along = self.place
        over0, up1, loads = self.first[i]
        for load in loads:
            load.wait()
        over0.wait_recv()
        self.mid0[i] = (self.own0[i].astype(F32) + self.recv0[i].astype(F32)).astype(BF16)
        up0 = [
            self.push(
                i, self.mid0.at[i, lax.rem(a + k, self.high)], self.last0.at[i, k - 1], along[k - 1]
            )
            for k in range(1, self.high)
        ]
        for copy in up1:
            copy.wait_recv()
        joined = self.own1[i].astype(F32)
        for k in range(1, self.high):
            joined = joined + self.recv1[i, k - 1].astype(F32)
        self.mid1[i] = joined.astype(BF16)
        over1 = self.push(i, self.mid1.at[i, 1 - b], self.last1.at[i], across)
        self.second[i] = (up0, over1)

    def last(self, i):
        a, b, across, along = self.place
        up0, over1 = self.second[i]
        for copy in up0:
            copy.wait_recv()
        result0 = self.own0[i, pl.ds(a, 1)][0].astype(F32) + self.recv0[i, pl.ds(a, 1)][0].astype(F32)
        for k in range(1, self.high):
            result0 = result0 + self.last0[i, k - 1].astype(F32)
        over1.wait_recv()
        result1 = self.own1[i, pl.ds(b, 1)][0].astype(F32) + self.last1[i].astype(F32)
        for k in range(1, self.high):
            result1 = result1 + self.recv1[i, k - 1, pl.ds(b, 1)][0].astype(F32)
        if i == 0:
            self.given[0] = result0.astype(BF16)
            self.given[1] = result1.astype(BF16)
            self.over_pair = send(
                self.given, self.taken, self.pair_sems.at[0], self.pair_sems.at[1], self.pair
            )
        else:
            self.out[0] = result0
            self.out[1] = result1

    def finish(self):
        self.over_pair.wait_recv()
        self.out[...] += self.taken[...].astype(F32)
        self.over_pair.wait_send()
        for copy in self.sent[0] + self.sent[1]:
            copy.wait_send()


def sum_pair_kernel(high, count, riders, src, inner, *refs):
    blocks, (out, product, weights, sems, *scratch) = refs[:count], refs[count:]
    a, b, across, along = plane_peers(high)
    greet([across, pair_peer()[1]] + along + riders.peers())
    riders.start()
    whole = PairSum(high, src, out, scratch)
    whole.start(0)
    whole.middle(0)
    whole.start(1)
    mlp_out_kernel(blocks, inner, product, weights, sems)
    whole.last(0)
    whole.middle(1)
    whole.last(1)
    whole.finish()
    riders.finish()


def pair_parts(partial_sums, grp):
    tokens, width = partial_sums.shape
    return partial_sums.reshape(2, 2, grp // 2, 2, tokens // (4 * grp), width)


def sum_pair(partial_sums, blocks, inner, grp, collective_id, name, riders=()):
    parts = pair_parts(partial_sums, grp)
    high, _, rows, width = parts.shape[2:]
    (result, product), arrived = carried_call(
        partial(sum_pair_kernel, high, len(blocks)),
        [parts, inner, *blocks],
        [
            jax.ShapeDtypeStruct((2, rows, width), F32),
            jax.ShapeDtypeStruct(partial_sums.shape, BF16),
        ],
        [ANY, VMEM] + [ANY] * len(blocks),
        [VMEM, VMEM],
        [pltpu.VMEM((width, inner.shape[1]), BF16), DMA((len(blocks),))] + PairSum.scratch(high, rows, width),
        comm_params(collective_id, 48),
        name,
        riders,
    )
    return result, product, arrived


def turn_half(values):
    half = values.shape[-1] // 2
    return jnp.concatenate([-values[:, half:], values[:, :half]], axis=-1)


def fill_tables(frequency, cosine, sine):
    line = lax.axis_size("seq") // 2
    rows, dim = cosine.shape[0] // 2, cosine.shape[1]
    for part in range(2):
        first = (lax.rem(lax.axis_index("seq"), line) + part * line) * rows
        position = first + lax.broadcasted_iota(jnp.int32, (rows, dim), 0)
        angles = position.astype(F32) * frequency[...]
        cosine[part * rows : (part + 1) * rows] = jnp.cos(angles)
        sine[part * rows : (part + 1) * rows] = jnp.sin(angles)


def heads_kernel(queries, keys, x, w, frequency, query_gain, key_gain, raw, out, cosine, sine):
    step, dim = pl.program_id(0), cosine.shape[1]
    pl.when(step == 0)(lambda: fill_tables(frequency, cosine, sine))
    raw[...] = nn(x[...], w[...])
    for i in range(raw.shape[1] // dim):
        head, cut = step * (raw.shape[1] // dim) + i, slice(i * dim, (i + 1) * dim)

        @pl.when(head < queries + keys)
        def _():
            unit, _ = normalize(raw[:, cut])
            scaled = unit * jnp.where(head < queries, query_gain[...], key_gain[...])
            out[:, cut] = (scaled * cosine[...] + turn_half(scaled) * sine[...]).astype(BF16)

        @pl.when(head >= queries + keys)
        def _():
            out[:, cut] = raw[:, cut].astype(BF16)


def heads_forward(x, w, small, queries, keys):
    (tokens, depth), width, dim = x.shape, w.shape[1], small[0].shape[1]
    step = 2 * dim
    column = pl.BlockSpec((tokens, step), lambda h: (0, h))
    one = pl.BlockSpec((1, dim), lambda h: (0, 0))
    return pl.pallas_call(
        partial(heads_kernel, queries, keys),
        cost_estimate=NO_COST,
        name="heads_forward",
        grid=(width // step,),
        out_shape=[
            jax.ShapeDtypeStruct((tokens, width), F32),
            jax.ShapeDtypeStruct((tokens, width), BF16),
        ],
        in_specs=[
            pl.BlockSpec((tokens, depth), lambda h: (0, 0)),
            pl.BlockSpec((depth, step), lambda h: (0, h)),
            one,
            one,
            one,
        ],
        out_specs=[column, column],
        scratch_shapes=[pltpu.VMEM((tokens, dim), F32), pltpu.VMEM((tokens, dim), F32)],
        compiler_params=pltpu.CompilerParams(vmem_limit_bytes=60 * 2**20),
    )(x, w, *small)


def heads_back_kernel(
    queries, keys, raw, grad_q, grad_kv, frequency, query_gain, key_gain, out, gain_out, cosine, sine
):
    head = pl.program_id(0)
    pl.when(head == 0)(lambda: fill_tables(frequency, cosine, sine))

    def turned_back(given):
        unit, inverse = normalize(raw[...])
        turned = given * cosine[...] - turn_half(given * sine[...])
        gain_out[...] = jnp.broadcast_to(
            jnp.sum(turned * unit, axis=0, keepdims=True)[None], gain_out.shape
        )
        scaled = turned * jnp.where(head < queries, query_gain[...], key_gain[...])
        out[...] = norm_back(scaled, unit, inverse).astype(BF16)

    pl.when(head < queries)(lambda: turned_back(grad_q[...]))
    pl.when((head >= queries) & (head < queries + keys))(lambda: turned_back(grad_kv[...]))

    @pl.when(head >= queries + keys)
    def _():
        gain_out[...] = jnp.zeros_like(gain_out)
        out[...] = grad_kv[...].astype(BF16)


def heads_backward(raw, grad_q, grad_kv, small, queries, keys):
    (tokens, width), dim = raw.shape, small[0].shape[1]
    column = pl.BlockSpec((tokens, dim), lambda h: (0, h))
    one = pl.BlockSpec((1, dim), lambda h: (0, 0))
    return pl.pallas_call(
        partial(heads_back_kernel, queries, keys),
        cost_estimate=NO_COST,
        name="heads_backward",
        grid=(width // dim,),
        out_shape=[
            jax.ShapeDtypeStruct((tokens, width), BF16),
            jax.ShapeDtypeStruct((width // dim, 8, dim), F32),
        ],
        in_specs=[
            column,
            pl.BlockSpec((tokens, dim), lambda h: (0, jnp.minimum(h, queries - 1))),
            pl.BlockSpec((tokens, dim), lambda h: (0, jnp.maximum(h - queries, 0))),
            one,
            one,
            one,
        ],
        out_specs=[column, pl.BlockSpec((1, 8, dim), lambda h: (h, 0, 0))],
        scratch_shapes=[pltpu.VMEM((tokens, dim), F32), pltpu.VMEM((tokens, dim), F32)],
        compiler_params=pltpu.CompilerParams(vmem_limit_bytes=32 * 2**20),
    )(raw, grad_q, grad_kv, *small)


def half_line_peers(chips):
    s, g = lax.axis_index("seq"), lax.axis_index("grp")
    chip, core = s // 2, lax.rem(s, 2)
    place = lax.rem(chip, chips)
    others = [((chip - place + lax.rem(place + k, chips)) * 2 + core, g) for k in range(1, chips)]
    return place, core, (s + 1 - 2 * core, g), others


def remote(src, dst, send_sem, recv_sem, peer):
    return pltpu.make_async_remote_copy(
        src_ref=src,
        dst_ref=dst,
        send_sem=send_sem,
        recv_sem=recv_sem,
        device_id=peer,
        device_id_type=MESH,
    )


def allowed_pairs(query_block, key_block, length, rows, repeat, diagonal):
    key_pos = key_block * rows + lax.broadcasted_iota(jnp.int32, (rows, repeat * rows), 0)
    allowed = key_pos < length
    if diagonal:
        query_pos = lax.broadcasted_iota(jnp.int32, (rows, repeat * rows), 1)
        allowed = allowed & (key_pos <= query_block * rows + lax.rem(query_pos, rows))
    return allowed


def stacked(ref, part, rows, first, repeat, dim):
    return jnp.concatenate(
        [
            ref[part * rows : (part + 1) * rows, (first + r) * dim : (first + r + 1) * dim]
            for r in range(repeat)
        ],
        axis=0,
    )


def attend_kernel(
    shape,
    chips,
    high,
    riders,
    length,
    q,
    kv_home,
    beside,
    mixed,
    mixed_low,
    log_total,
    kv_all,
    beside_dst,
    plane_send,
    plane_recv,
    kv_buf,
    acc,
    sums,
    lane_send,
    lane_recv,
    cross_send,
    cross_recv,
    local_sems,
):
    rows, keys, repeat, dim = shape
    scale = 1.0 / math.sqrt(dim)
    place, core, cross, others = half_line_peers(chips)
    me = place * 2 + core
    a, b, across, along = plane_peers(high)
    greet([cross] + others + [across] + along + riders.peers())
    home = pltpu.make_async_copy(kv_home, kv_all.at[me], local_sems.at[0])
    home.start()
    beside_home = pltpu.make_async_copy(beside, beside_dst.at[:, a, b], local_sems.at[2])
    beside_home.start()
    plane = PlaneGather(high, beside.at[0], beside.at[1], beside_dst, plane_send, plane_recv)

    def over(i, src, owner):
        return remote(src, kv_all.at[owner], cross_send.at[i], cross_recv.at[i], cross)

    lanes = [
        remote(kv_home, kv_all.at[me], lane_send.at[k], lane_recv.at[k], peer)
        for k, peer in enumerate(others)
    ]
    crossed = [over(0, kv_home, me)]
    for copy in lanes + crossed:
        copy.start()
    plane.start()
    riders.start()
    acc[...] = jnp.zeros_like(acc)
    sums[...] = jnp.zeros_like(sums)

    def piece(owner, query_part, key_part, diagonal):
        query_block, key_block = me + query_part * 2 * chips, owner + key_part * 2 * chips
        allowed = allowed_pairs(query_block, key_block, length[0], rows, repeat, diagonal)
        here = slice(key_part * rows, (key_part + 1) * rows)
        for k in range(keys):
            unit = query_part * keys + k
            kk = kv_buf[here, k * dim : (k + 1) * dim]
            vv = kv_buf[here, (keys + k) * dim : (keys + k + 1) * dim]
            scores = nt(kk, stacked(q, query_part, rows, k * repeat, repeat, dim)) * scale
            weights = jnp.where(allowed, jnp.exp(scores), 0.0)
            sums[unit] += jnp.sum(weights, axis=0, keepdims=True)
            acc[unit] += tn(vv, weights.astype(BF16))

    def work(src, owner, own):
        load = pltpu.make_async_copy(src, kv_buf, local_sems.at[1])
        load.start()
        load.wait()
        piece(owner, 1, 0, False)
        if own:
            piece(owner, 0, 0, True)
            piece(owner, 1, 1, True)
        else:

            @pl.when(owner < me)
            def _():
                piece(owner, 0, 0, False)
                piece(owner, 1, 1, False)

    work(kv_home, me, True)
    for k in range(chips):
        near = lax.rem(place + chips - k, chips) * 2
        if k:
            owner = near + core
            lanes[k - 1].wait_recv()
            crossed.append(over(k, kv_all.at[owner], owner))
            crossed[k].start()
            work(kv_all.at[owner], owner, False)
        owner = near + 1 - core
        crossed[k].wait_recv()
        work(kv_all.at[owner], owner, False)
        if k == 0:
            plane.forward()
    for part in range(2):
        for k in range(keys):
            unit = part * keys + k
            log_total[unit] = jnp.log(sums[unit])
            result = (acc[unit] / sums[unit]).T
            for r in range(repeat):
                cut = result[r * rows : (r + 1) * rows]
                h = k * repeat + r
                mixed[part * rows : (part + 1) * rows, h * dim : (h + 1) * dim] = cut
                mixed_low[part * rows : (part + 1) * rows, h * dim : (h + 1) * dim] = cut.astype(BF16)
    home.wait()
    for copy in lanes + crossed:
        copy.wait_send()
    plane.finish()
    beside_home.wait()
    riders.finish()


def attend(length, q, kv_home, beside, seq, grp, keys, repeat, dim, collective_id, riders=()):
    tokens, kv_width = kv_home.shape
    rows, width = tokens // 2, keys * repeat * dim
    chips = seq // 4
    return carried_call(
        partial(attend_kernel, (rows, keys, repeat, dim), chips, grp // 2),
        [length, q, kv_home, beside],
        [
            jax.ShapeDtypeStruct((tokens, width), F32),
            jax.ShapeDtypeStruct((tokens, width), BF16),
            jax.ShapeDtypeStruct((2 * keys, 1, repeat * rows), F32),
            jax.ShapeDtypeStruct((2 * chips, tokens, kv_width), BF16),
            plane_shape(beside, grp),
        ],
        [pl.BlockSpec(memory_space=pltpu.SMEM), VMEM, ANY, ANY],
        [VMEM, VMEM, VMEM, ANY, ANY],
        [
            DMA((2 * grp,)),
            DMA((2 * grp,)),
            pltpu.VMEM((tokens, kv_width), BF16),
            pltpu.VMEM((2 * keys, dim, repeat * rows), F32),
            pltpu.VMEM((2 * keys, 1, repeat * rows), F32),
            DMA((chips,)),
            DMA((chips,)),
            DMA((chips,)),
            DMA((chips,)),
            DMA((3,)),
        ],
        comm_params(collective_id, 60),
        "attend",
        riders,
    )


def attend_back_kernel(
    shape,
    chips,
    high,
    riders,
    length,
    q,
    mixed,
    grad_mixed,
    log_total,
    kv_all,
    beside,
    grad_q,
    grad_kv,
    beside_out,
    kv_buf,
    acc,
    delta,
    mine,
    lane_out,
    lane_in,
    cross_out,
    cross_in,
    lane_send,
    lane_recv,
    cross_send,
    cross_recv,
    local_sem,
    *beside_scratch,
):
    rows, keys, repeat, dim = shape
    scale = 1.0 / math.sqrt(dim)
    place, core, cross, others = half_line_peers(chips)
    me = place * 2 + core
    _, _, across, along = plane_peers(high)
    greet([cross] + others + [across, pair_peer()[1]] + along + riders.peers())
    whole = PairSum(high, beside, beside_out, beside_scratch)
    whole.start(0)
    riders.start()
    acc[...] = jnp.zeros_like(acc)
    for part in range(2):
        for k in range(keys):
            product = stacked(mixed, part, rows, k * repeat, repeat, dim) * stacked(
                grad_mixed, part, rows, k * repeat, repeat, dim
            ).astype(F32)
            delta[part * keys + k] = jnp.sum(product.T, axis=0, keepdims=True)

    def piece(owner, query_part, key_part, diagonal, first):
        query_block, key_block = me + query_part * 2 * chips, owner + key_part * 2 * chips
        allowed = allowed_pairs(query_block, key_block, length[0], rows, repeat, diagonal)
        here = slice(key_part * rows, (key_part + 1) * rows)
        for k in range(keys):
            unit = query_part * keys + k
            key_cut, value_cut = slice(k * dim, (k + 1) * dim), slice((keys + k) * dim, (keys + k + 1) * dim)
            kk, vv = kv_buf[here, key_cut], kv_buf[here, value_cut]
            qq = stacked(q, query_part, rows, k * repeat, repeat, dim)
            gg = stacked(grad_mixed, query_part, rows, k * repeat, repeat, dim)
            weights = jnp.where(allowed, jnp.exp(nt(kk, qq) * scale - log_total[unit]), 0.0)
            grad_scores = (weights * (nt(vv, gg) - delta[unit])).astype(BF16)
            grad_k, grad_v = nn(grad_scores, qq) * scale, nn(weights.astype(BF16), gg)
            if first:
                mine[here, key_cut] = grad_k
                mine[here, value_cut] = grad_v
            else:
                mine[here, key_cut] += grad_k
                mine[here, value_cut] += grad_v
            acc[unit] += tn(grad_scores, kk)

    def work(owner, own):
        load = pltpu.make_async_copy(kv_all.at[owner], kv_buf, local_sem)
        load.start()
        load.wait()
        piece(owner, 1, 0, False, True)
        if own:
            piece(owner, 0, 0, True, False)
            piece(owner, 1, 1, True, True)
        else:

            @pl.when(owner < me)
            def _():
                piece(owner, 0, 0, False, False)
                piece(owner, 1, 1, False, True)

            @pl.when(owner > me)
            def _():
                mine[rows:, :] = jnp.zeros_like(mine[rows:, :])

    lanes, crossed = [], []
    for k in list(range(1, chips)) + [0]:
        near = lax.rem(place + k, chips) * 2
        work(near + 1 - core, False)
        if k == 1:
            whole.middle(0)
            whole.start(1)
        if k == 0:
            whole.middle(1)
        cross_out[k] = mine[...].astype(BF16)
        copy = remote(cross_out.at[k], cross_in.at[k], cross_send.at[k], cross_recv.at[k], cross)
        copy.start()
        crossed.append(copy)
        work(near + core, k == 0)
        if k == 1:
            whole.last(0)
        if k == 0:
            whole.last(1)
        copy.wait_recv()
        mine[...] += cross_in[k].astype(F32)
        if k:
            lane_out[k - 1] = mine[...].astype(BF16)
            copy = remote(
                lane_out.at[k - 1], lane_in.at[k - 1], lane_send.at[k - 1], lane_recv.at[k - 1], others[k - 1]
            )
            copy.start()
            lanes.append(copy)
    for k, copy in enumerate(lanes):
        copy.wait_recv()
        mine[...] += lane_in[k].astype(F32)
    grad_kv[...] = mine[...]
    for part in range(2):
        for k in range(keys):
            for r in range(repeat):
                h = k * repeat + r
                grad_q[part * rows : (part + 1) * rows, h * dim : (h + 1) * dim] = (
                    acc[part * keys + k, r * rows : (r + 1) * rows] * scale
                )
    for copy in lanes + crossed:
        copy.wait_send()
    whole.finish()
    riders.finish()


def attend_back(
    length, q, kv_all, mixed, grad_mixed, log_total, beside, grp, keys, repeat, dim, collective_id, riders=()
):
    owners, tokens, kv_width = kv_all.shape
    rows, width = tokens // 2, keys * repeat * dim
    chips = owners // 2
    parts = pair_parts(beside, grp)
    high, _, beside_rows, beside_width = parts.shape[2:]
    slots = pltpu.VMEM((chips, tokens, kv_width), BF16)
    return carried_call(
        partial(attend_back_kernel, (rows, keys, repeat, dim), chips, high),
        [length, q, mixed, grad_mixed, log_total, kv_all, parts],
        [
            jax.ShapeDtypeStruct((tokens, width), F32),
            jax.ShapeDtypeStruct((tokens, kv_width), F32),
            jax.ShapeDtypeStruct((2, beside_rows, beside_width), F32),
        ],
        [pl.BlockSpec(memory_space=pltpu.SMEM), VMEM, VMEM, VMEM, VMEM, ANY, ANY],
        [VMEM, VMEM, VMEM],
        [
            pltpu.VMEM((tokens, kv_width), BF16),
            pltpu.VMEM((2 * keys, repeat * rows, dim), F32),
            pltpu.VMEM((2 * keys, 1, repeat * rows), F32),
            pltpu.VMEM((tokens, kv_width), F32),
            slots,
            slots,
            slots,
            slots,
            DMA((chips,)),
            DMA((chips,)),
            DMA((chips,)),
            DMA((chips,)),
            DMA,
        ]
        + PairSum.scratch(high, beside_rows, beside_width),
        comm_params(collective_id, 48),
        "attend_back",
        riders,
    )


def attention_grads_kernel(rows, grad_raw, branch, mixed_low, out):
    width = grad_raw.shape[1]
    out[:, :width] = tn(rows[...], grad_raw[...]).astype(BF16)
    out[:, width:] = tn(branch[...], mixed_low[...]).astype(BF16)


def attention_grads(rows, grad_raw, branch, mixed_low):
    (tokens, depth), width, inner = rows.shape, grad_raw.shape[1], mixed_low.shape[1]
    step = 512
    column = pl.BlockSpec((tokens, step), lambda d: (0, d))
    return pl.pallas_call(
        attention_grads_kernel,
        cost_estimate=NO_COST,
        name="attention_grads",
        grid=(depth // step,),
        out_shape=jax.ShapeDtypeStruct((depth, width + inner), BF16),
        in_specs=[
            column,
            pl.BlockSpec((tokens, width), lambda d: (0, 0)),
            column,
            pl.BlockSpec((tokens, inner), lambda d: (0, 0)),
        ],
        out_specs=pl.BlockSpec((step, width + inner), lambda d: (d, 0)),
        compiler_params=pltpu.CompilerParams(vmem_limit_bytes=32 * 2**20),
    )(rows, grad_raw, branch, mixed_low)


def write_attention_kernel(sums, *outs):
    first = 0
    for out in outs[:-1]:
        last = first + out.shape[1]
        out[...] = sums[:, first:last].astype(F32)
        first = last
    outs[-1][...] = sums[:, first:].astype(F32).T


def write_attention(sums, widths):
    depth, columns = sums.shape
    shapes = [(depth, width) for width in widths] + [(columns - sum(widths), depth)]
    return pl.pallas_call(
        write_attention_kernel,
        cost_estimate=NO_COST,
        name="write_attention",
        in_specs=[VMEM],
        out_specs=[VMEM] * len(shapes),
        out_shape=[jax.ShapeDtypeStruct(shape, F32) for shape in shapes],
        compiler_params=pltpu.CompilerParams(vmem_limit_bytes=32 * 2**20),
    )(sums)


def load_weights(blocks, first, weights, sems):
    s = lax.axis_index("seq")
    line = lax.axis_size("seq") // 2
    chips = line // 2
    row, place, core = s // line, lax.rem(s, line) // 2, lax.rem(s, 2)
    depth, width = blocks[0].shape[0], weights.shape[1]
    copies = []
    for i, src in enumerate(blocks):
        which = row if i // chips % 2 == 0 else 1 - row
        back = lax.rem(place + chips - i % chips, chips)
        owner = which * line + back * 2 + (core if i < 2 * chips else 1 - core)
        copy = pltpu.make_async_copy(
            src.at[:, pl.ds(first, width)], weights.at[pl.ds(owner * depth, depth)], sems.at[i]
        )
        copy.start()
        copies.append(copy)
    for copy in copies:
        copy.wait()
    return depth


def weight_grads(x, grads, keep, give):
    chips, halves, depth, _ = keep.shape
    core = lax.rem(lax.axis_index("seq"), 2)

    def one(t, carry):
        cut = pl.ds(pl.multiple_of(t * 2 * depth, 2 * depth), 2 * depth)
        both = tn(x[:, cut], grads[...]).astype(BF16)
        chip, which = lax.rem(t, chips), t // chips

        @pl.when(core == 0)
        def _():
            keep[chip, which] = both[:depth]
            give[chip, which] = both[depth:]

        @pl.when(core == 1)
        def _():
            keep[chip, which] = both[depth:]
            give[chip, which] = both[:depth]

        return carry

    lax.fori_loop(0, halves * chips, one, 0)


def mlp_kernel(rows, cot_home, cot_away, *refs):
    *blocks, inner, grad_pre, keep, give, weights, cot, sems, cot_sems = refs
    block = cot_home.shape[1]
    row = lax.axis_index("seq") // (lax.axis_size("seq") // 2)

    def load(i, src):
        return pltpu.make_async_copy(src, cot.at[pl.ds(i * block, block)], cot_sems.at[i])

    for k, order in enumerate(
        (
            (cot_home.at[0], cot_away.at[0], cot_home.at[1], cot_away.at[1]),
            (cot_away.at[1], cot_home.at[1], cot_away.at[0], cot_home.at[0]),
        )
    ):

        @pl.when(row == k)
        def _():
            for i, src in enumerate(order):
                load(i, src).start()

    depth = load_weights(blocks, 0, weights, sems)
    for i in range(4):
        load(i, cot_home.at[0]).wait()
    units = inner.shape[1]
    step = 256 if units % 256 == 0 else 128
    tile = 512
    tiles = rows.shape[0] // tile

    def one(t, carry):
        here = pl.ds(pl.multiple_of(lax.rem(t, tiles) * tile, tile), tile)
        first = pl.multiple_of((t // tiles) * step, step)
        cols = pl.ds(first, step)
        x = rows[here, :]
        gate = nn(x, weights[:, cols])
        up = nn(x, weights[:, pl.ds(units + first, step)])
        grad = nn(cot[here, :], weights[:, pl.ds(2 * units + first, step)])
        sigmoid = jax.nn.sigmoid(gate)
        silu = gate * sigmoid
        inner[here, cols] = (silu * up).astype(BF16)
        grad_pre[here, cols] = (grad * up * sigmoid * (1.0 + gate * (1.0 - sigmoid))).astype(BF16)
        grad_pre[here, pl.ds(units + first, step)] = (grad * silu).astype(BF16)
        return carry

    lax.fori_loop(0, tiles * (units // step), one, 0)

    weight_grads(cot, inner, keep, give)


def grads_shape(width, columns):
    chips = lax.axis_size("seq") // 4
    return jax.ShapeDtypeStruct((chips, 2, width // chips // 4, columns), BF16)


def mlp(blocks, rows, cot_home, cot_away):
    (tokens, width), columns = rows.shape, blocks[0].shape[1]
    units = columns // 3
    return pl.pallas_call(
        mlp_kernel,
        cost_estimate=NO_COST,
        name="mlp",
        in_specs=[VMEM, ANY, ANY] + [ANY] * len(blocks),
        out_specs=[VMEM] * 4,
        out_shape=[
            jax.ShapeDtypeStruct((tokens, units), BF16),
            jax.ShapeDtypeStruct((tokens, 2 * units), BF16),
            grads_shape(width, units),
            grads_shape(width, units),
        ],
        scratch_shapes=[
            pltpu.VMEM((width, columns), BF16),
            pltpu.VMEM((tokens, width), BF16),
            DMA((len(blocks),)),
            DMA((4,)),
        ],
        compiler_params=pltpu.CompilerParams(vmem_limit_bytes=52 * 2**20),
    )(rows, cot_home, cot_away, *blocks)


def mlp_back_kernel(riders, rows, grad_pre, keep_down, give_down, *refs):
    *blocks, down, gate, up, grad_rows, keep, give, got, got_down, weights, sems, core_sems = refs
    core = peer_of("core")
    greet([core])
    over_down = send(give_down, got_down, core_sems.at[0, 0], core_sems.at[0, 1], core)
    load_weights(blocks, 0, weights, sems)
    weight_grads(rows, grad_pre, keep, give)
    over = send(give, got, core_sems.at[1, 0], core_sems.at[1, 1], core)
    tile = 512

    def one(t, carry):
        here = pl.ds(pl.multiple_of(t * tile, tile), tile)
        grad_rows[here, :] = nt(grad_pre[here, :], weights[...]).astype(BF16)
        return carry

    lax.fori_loop(0, rows.shape[0] // tile, one, 0)
    units = gate.shape[-1]
    over_down.wait()
    over.wait()

    def add(t, carry):
        at = (lax.rem(t, keep.shape[0]), t // keep.shape[0])
        down[at] = (keep_down[at].astype(F32) + got_down[at].astype(F32)).astype(BF16)
        both = (keep[at].astype(F32) + got[at].astype(F32)).astype(BF16)
        gate[at] = both[:, :units]
        up[at] = both[:, units:]
        return carry

    lax.fori_loop(0, 2 * keep.shape[0], add, 0)


def mlp_back(blocks, rows, grad_pre, keep_down, give_down, collective_id):
    (tokens, width), columns = rows.shape, grad_pre.shape[1]
    one, two = grads_shape(width, columns // 2), grads_shape(width, columns)
    results, _ = carried_call(
        mlp_back_kernel,
        [rows, grad_pre, keep_down, give_down, *blocks],
        [one, one, one, jax.ShapeDtypeStruct((tokens, width), BF16)],
        [VMEM, VMEM, VMEM, ANY] + [ANY] * len(blocks),
        [VMEM] * 4,
        [pltpu.VMEM(two.shape, BF16)] * 3
        + [
            pltpu.VMEM(one.shape, BF16),
            pltpu.VMEM((width, columns), BF16),
            DMA((len(blocks),)),
            DMA((2, 2)),
        ],
        comm_params(collective_id, 60),
        "mlp_back",
    )
    return results


def mlp_out_kernel(blocks, inner, out, weights, sems):
    load_weights(blocks, 2 * inner.shape[1], weights, sems)
    tile = 512

    def one(t, carry):
        here = pl.ds(pl.multiple_of(t * tile, tile), tile)
        out[here, :] = nt(inner[here, :], weights[...]).astype(BF16)
        return carry

    lax.fori_loop(0, inner.shape[0] // tile, one, 0)


def write_kernel(sums, taken, out):
    units = taken.shape[1]
    row = lax.axis_index("seq") // (lax.axis_size("seq") // 2)
    kept, other = sums[row].astype(F32), taken[...].astype(F32)
    out[:, :units] = jnp.where(row == 0, kept, other)
    out[:, units:] = jnp.where(row == 0, other, kept)


def write_down_kernel(sums, taken, out):
    units = taken.shape[1]
    row = lax.axis_index("seq") // (lax.axis_size("seq") // 2)
    kept, other = sums[row].astype(F32), taken[...].astype(F32)
    out[:units] = jnp.where(row == 0, kept, other).T
    out[units:] = jnp.where(row == 0, other, kept).T


def write(kernel, sums, taken, shape, name):
    return pl.pallas_call(
        kernel,
        cost_estimate=NO_COST,
        name=name,
        in_specs=[VMEM, VMEM],
        out_specs=VMEM,
        out_shape=jax.ShapeDtypeStruct(shape, F32),
        compiler_params=pltpu.CompilerParams(vmem_limit_bytes=32 * 2**20),
    )(sums, taken)


def shards(
    tokens,
    lengths,
    attn_gain,
    w_query,
    w_key,
    w_value,
    query_gain,
    key_gain,
    w_out,
    mlp_gain,
    w_gate,
    w_up,
    w_down,
    cotangent,
):
    seq, grp = lax.axis_size("seq"), lax.axis_size("grp")
    seq_index, grp_index = lax.axis_index("seq"), lax.axis_index("grp")
    local_rows, width = tokens.shape[1:]
    rows = local_rows * grp
    dim = query_gain.shape[0]
    queries, keys = w_query.shape[1] // dim, w_key.shape[1] // dim
    repeat = queries // keys
    hidden_units = w_gate.shape[1]
    chunk = attn_gain.shape[0]
    depth = width // seq

    line = seq // 2
    row = seq_index // line

    def to_give(values):
        return lax.dynamic_index_in_dim(values, 1 - row, 0, keepdims=False)

    def both_rows(values, taken):
        kept = lax.dynamic_index_in_dim(values, row, 0, keepdims=False)
        return jnp.stack([jnp.where(row == 0, kept, taken), jnp.where(row == 0, taken, kept)])

    length = lax.dynamic_slice(lengths, (row,), (1,))

    half_units = hidden_units // 2
    opposite = [(s, (s + line) % seq) for s in range(seq)]

    def half(which):
        cut = [
            lax.dynamic_slice_in_dim(w, which * half_units, half_units, 1)
            for w in (w_gate, w_up, w_down.T)
        ]
        return jnp.concatenate(cut, axis=1)

    chips = line // 2
    steps = range(1, chips)
    place = lax.rem(seq_index, line) // 2

    def chips_sum(parts, arrived):
        mine = lax.dynamic_index_in_dim(parts, place, 0, keepdims=False)
        return sum([x.astype(F32) for x in arrived], mine.astype(F32)).astype(BF16)

    def to_chips(parts):
        return [(k, parts, "chip") for k in steps]

    projections = jnp.concatenate([w_query, w_key, w_value], axis=1)
    full_qkv = lax.all_gather(projections, "seq", axis=0, tiled=True)
    lane = max(128, chunk)
    packed = jnp.pad(jnp.stack([attn_gain, mlp_gain]), ((0, 6), (0, lane - chunk)))
    spread_gains, (taken_tokens,) = spread(packed, seq, grp, 1, [("opposite", to_give(tokens))])
    spread_gains = spread_gains[:, :, :, :chunk].transpose(2, 1, 0, 3)
    gain_attn = spread_gains[0].reshape(-1)
    gain_mlp = spread_gains[1].reshape(-1)
    full_out = lax.all_gather(after(w_out.T, taken_tokens), "seq", axis=0, tiled=True)
    residual = both_rows(tokens, taken_tokens).astype(F32)
    attn_unit, attn_inverse = normalize(residual)
    attn_rows, _ = gather_rows((attn_unit * gain_attn).astype(BF16), grp, 2, "gather_inputs")
    kept_half, given_half = after((half(row), half(1 - row)), attn_rows)
    taken_half = lax.ppermute(given_half, "seq", opposite)
    token_pos = (seq_index * grp + grp_index) * local_rows + jnp.arange(local_rows, dtype=jnp.int32)
    valid_rows = (token_pos[None, :] < lengths[:, None]).astype(BF16)
    cot_home = cotangent * valid_rows[:, :, None]

    frequency = ROPE_BASE ** (-jnp.arange(dim // 2, dtype=F32) * 2.0 / dim)
    small = [jnp.tile(frequency, 2)[None], query_gain[None], key_gain[None]]
    raw, heads = heads_forward(attn_rows, full_qkv, small, queries, keys)
    q, kv_home = heads[:, : queries * dim], heads[:, queries * dim :]

    (mixed, mixed_low, log_total, kv_all, cot_gathered), _ = attend(
        length, q, kv_home, cot_home, seq, grp, keys, repeat, dim, 3
    )
    cot_gathered = cot_gathered.reshape(2, rows, width)
    summed, (taken_cotangent, *passed) = sum_rows(
        nt(mixed_low, full_out),
        grp,
        4,
        "sum_attention",
        [("opposite", cot_home)] + [(k, kept_half) for k in steps],
    )
    own_half = [kept_half] + passed
    early = jnp.where(row == 0, cot_home[0], taken_cotangent[1])
    late = jnp.where(row == 0, taken_cotangent[0], cot_home[1])
    cot_rows = jnp.stack([early, late]).astype(F32)
    hidden = residual + summed

    mlp_unit, mlp_inverse = normalize(hidden)
    first_blocks = own_half + [taken_half]
    mlp_rows, cot_away, arrived = gather_pair(
        (mlp_unit * gain_mlp).astype(BF16),
        taken_cotangent,
        grp,
        5,
        "gather_mlp",
        [(k, taken_half) for k in steps] + [("core", x) for x in first_blocks],
    )
    passed, core_blocks = arrived[: len(steps)], arrived[len(steps) :]
    core_swap = [(s, s ^ 1) for s in range(seq)]
    core_blocks += [lax.ppermute(x, "seq", core_swap) for x in passed]
    blocks_w = first_blocks + passed + core_blocks
    inner_low, grad_pre, keep_down, give_down = mlp(blocks_w, mlp_rows, cot_gathered, cot_away)
    down, gate, up, grad_mlp_part = mlp_back(blocks_w, mlp_rows, grad_pre, keep_down, give_down, 13)
    grad_mlp_in, out_part, arrived = sum_pair(
        grad_mlp_part,
        blocks_w,
        inner_low,
        grp,
        7,
        "sum_mlp_back",
        to_chips(down) + to_chips(gate),
    )
    down = chips_sum(down, arrived[: len(steps)])
    gate = chips_sum(gate, arrived[len(steps) :])
    grad_gain_mlp = jnp.sum(grad_mlp_in * mlp_unit, axis=(0, 1))
    grad_hidden = cot_rows + norm_back(grad_mlp_in * gain_mlp, mlp_unit, mlp_inverse)
    grad_branch, (taken_down, taken_gate, *arrived) = gather_rows(
        grad_hidden.astype(BF16),
        grp,
        8,
        "gather_branch",
        [("opposite", down, "row"), ("opposite", gate, "row")] + to_chips(up),
    )
    up = chips_sum(up, arrived)

    grad_mixed = nn(grad_branch, full_out).astype(BF16)
    (grad_q, grad_kv, summed), (taken_up,) = attend_back(
        length,
        q,
        kv_all,
        mixed,
        grad_mixed,
        log_total,
        out_part,
        grp,
        keys,
        repeat,
        dim,
        9,
        [("opposite", up, "row")],
    )
    output = (hidden + summed).astype(BF16)
    grad_raw, head_gain_parts = heads_backward(raw, grad_q, grad_kv, small, queries, keys)
    grad_w_attn = attention_grads(attn_rows, grad_raw, grad_branch, mixed_low)
    sum_attn = lax.psum_scatter(grad_w_attn, "seq", scatter_dimension=0, tiled=True)
    grad_attn_part = nt(after(grad_raw, grad_w_attn), full_qkv)
    grad_attn_in, (taken_output,) = sum_rows(
        grad_attn_part,
        grp,
        10,
        "sum_attention_back",
        [("opposite", to_give(output))],
    )
    output = both_rows(output, taken_output)
    wide_shape = (depth, hidden_units)
    taken_down, taken_gate, taken_up = after((taken_down, taken_gate, taken_up), grad_attn_in)
    out_down = write(write_down_kernel, down, taken_down, wide_shape[::-1], "write_down")
    out_gate = write(write_kernel, gate, taken_gate, wide_shape, "write_gate")
    out_up = write(write_kernel, up, taken_up, wide_shape, "write_up")
    grad_gain_attn = jnp.sum(grad_attn_in * attn_unit, axis=(0, 1))
    grad_tokens = grad_hidden + norm_back(grad_attn_in * gain_attn, attn_unit, attn_inverse)

    head_gain_grads = jnp.stack(
        [
            jnp.sum(head_gain_parts[:queries, 0], axis=0),
            jnp.sum(head_gain_parts[queries : queries + keys, 0], axis=0),
        ]
    )
    vector = jnp.concatenate([grad_gain_attn, grad_gain_mlp, head_gain_grads.reshape(-1)])
    padded = -(-vector.shape[0] // 1024) * 1024
    vector = jnp.pad(vector, (0, padded - vector.shape[0])).reshape(-1, 128)
    sums, (taken_grads,) = total(vector, seq, grp, 12, [("opposite", to_give(grad_tokens).astype(BF16))])
    sums = sums.reshape(-1)
    grad_tokens = both_rows(grad_tokens, taken_grads.astype(F32))
    place = (seq_index * grp + grp_index) * chunk
    out_attn_gain = lax.dynamic_slice(sums, (place,), (chunk,))
    out_mlp_gain = lax.dynamic_slice(sums, (width + place,), (chunk,))
    out_query_gain = sums[2 * width : 2 * width + dim]
    out_key_gain = sums[2 * width + dim : 2 * width + 2 * dim]

    out_query, out_key, out_value, out_out = write_attention(
        sum_attn, (queries * dim, keys * dim, keys * dim)
    )
    return (
        output,
        grad_tokens,
        out_attn_gain,
        out_query,
        out_key,
        out_value,
        out_query_gain,
        out_key_gain,
        out_out,
        out_mlp_gain,
        out_gate,
        out_up,
        out_down,
    )


def solution(mesh):
    rows = P(None, ("seq", "grp"), None)
    vector = P(("seq", "grp"))
    wide, tall = P("seq", "grp"), P("grp", "seq")
    return jax.shard_map(
        shards,
        mesh=mesh,
        in_specs=(
            rows,
            P(),
            vector,
            wide,
            wide,
            wide,
            P(),
            P(),
            tall,
            vector,
            wide,
            wide,
            tall,
            rows,
        ),
        out_specs=(
            rows,
            rows,
            vector,
            wide,
            wide,
            wide,
            P(),
            P(),
            tall,
            vector,
            wide,
            wide,
            tall,
        ),
        check_vma=False,
    )
```

time: 625 us -> 564 us (0.902)
  local copies, waits for them, and re-layouts: 43.8 us -> 21.9 us
  matrix products: 26.6 us -> 8.9 us
  waiting for transfers between devices: 30 us -> 17.1 us
    ppermute x3 -> x2, waiting for transfers between devices: 29.9 us -> 1.84 us  [the longest x1 1.84 us: shards(): core_blocks += [lax.ppermute(x, 'seq', core_swap) for x in passed]]
    reduce_scatter x4 -> x1, waiting for transfers between devices: 0.01 us -> 15.2 us  [shards(): lax.psum_scatter(grad_w_attn, 'seq', scatter_dimension=0, tiled=True)]
    dot_general x2 -> x0, matrix products: 9.77 us -> none  [tn(): lax.dot_general(a, b, (((0,), (0,)), ((), ())), preferred_element_type=F32)]
    dot_general x2 -> x1, matrix products: 9.46 us -> 1.28 us  [nn(): return jnp.dot(a, b, preferred_element_type=F32)]
    slice x4 -> x0, local copies, waits for them, and re-layouts: 8.13 us -> none  [the longest x1 3.32 us: from_halves(): low[:, i]]
    unnamed x85 -> x104, local copies, waits for them, and re-layouts: 22.5 us -> 14.6 us
    pallas_call x17 -> x19, Pallas kernels: 470 us -> 469 us  [the longest x11 420 us: carried_call(): pl.pallas_call(body, name=name, cost_estimate=NO_COST, out_shape=[jax.Sha...]
  transfers between devices with their start and end apart: 11 -> 5, of which waited for: 3 -> 2; matrix products, arithmetic and copies ran while one was open for 9% -> 5% of each run, Pallas kernels for 67% -> 38%
where the time goes in v3:
time: 564 us; the launch traced here: 555 us
  Pallas kernels  469 us (83%)
  local copies, waits for them, and re-layouts  21.9 us (4%)
  waiting for transfers between devices  17.1 us (3%)
  between operations  15 us (3%)
  other arithmetic  14.1 us (2%)
  matrix products  8.9 us (2%)
  starting transfers between devices  8.6 us (2%)
    pallas_call x11, Pallas kernels, carried_call(): pl.pallas_call(body, name=name, cost_estimate=NO_COST, out_shape=[jax.Sha...  420 us
    pallas_call x1, Pallas kernels, mlp(): pl.pallas_call(mlp_kernel, cost_estimate=NO_COST, name='mlp', in_specs=[V...  26 us
    reduce_scatter x1, waiting for transfers between devices, shards(): lax.psum_scatter(grad_w_attn, 'seq', scatter_dimension=0, tiled=True)  15.2 us
    unnamed x104, local copies, waits for them, and re-layouts  14.6 us
  transfers between devices with their start and end apart: 5, of which 2 were waited for; matrix products, arithmetic and copies ran while one was open for 5% of the time, Pallas kernels for 38%

profile of v3, /device:TPU:9, one launch (start us, length us, event | category | flops | bytes accessed | tf_op | source)
XLA Modules:
  0.0 554.8 jit_solution(12985255645966670887)
XLA Ops:
  7.3 2.0 pad_maximum_fusion.4
  10.4 28.0 %gather_gains.1 = (bf16[64,2048]{1,0:T(8,128)(2,1)S(1)}, f32[4,8,8,128]{3,2,1,0:T(8,128)S(1)}) custom-call(bf16[64,2048]{1,0:T(8,128)(2,1)S(1)} %dynamic-slice_bitcast_fusion.1.refs_0_, f32[8,128]{1,0:T(8,128)S(1)} %select_maximum_fusion.2.refs_1_), custom_call_target="tpu_custom_call" | custom-call | flops 1 | bytes 1 | tf_op jit(solution)/shard_map/gather_gains/pallas_call | solution.py:132
  39.1 16.8 %gather_inputs.1 = bf16[2,2,2,64,2048]{4,3,2,1,0:T(8,128)(2,1)S(1)} custom-call(bf16[2,64,2048]{2,1,0:T(8,128)(2,1)S(1)} %fusion.7.refs_0_), custom_call_target="tpu_custom_call" | custom-call | flops 1 | bytes 1 | tf_op jit(solution)/shard_map/gather_inputs/pallas_call | solution.py:132
  55.8 1.4 copy-done.8
  57.6 1.5 constant_dynamic-slice_fusion.1
  60.3 6.3 %collective-permute-start = (bf16[256,2304]{1,0:T(8,128)(2,1)}, bf16[256,2304]{1,0:T(8,128)(2,1)S(1)}, u32[]{:S(2)}, u32[]{:S(2)}) collective-permute-start(bf16[256,2304]{1,0:T(8,128)(2,1)} %pad_maximum_fusion.1), channel_id=1, source_target_pairs={{0,16},{4,20},{8,24},{12,28},{16,0},{20,4},{24,8},{28,12},{1,17},{... | collective-permute-start | bytes 3538952 | tf_op jit(solution)/shard_map/ppermute | solution.py:1406
  68.0 1.9 broadcast_multiply_fusion.refs_3_.refs_0_
  69.9 8.8 %heads_forward.1 = (f32[512,1024]{1,0:T(8,128)}, bf16[512,1024]{1,0:T(8,128)(2,1)}) custom-call(bf16[512,2048]{1,0:T(8,128)(2,1)} %bitcast.79, bf16[2048,1024]{1,0:T(8,128)(2,1)} %all-gather.3.cloned.1.call-done.w, f32[1,128]{1,0:T(1,128)} %broadcast_in_dim_tile.5.frequency, f32[1,128]{1,0:T(1,128)} %bitcast.85, f32[1,128]{1,0:T(1,128)} %bitcast.87), custom_call_target="tpu_custom_call" | custom-call | flops 1 | bytes 1 | tf_op jit(solution)/shard_map/heads_forward/pallas_call | solution.py:638
  78.7 2.2 fusion.23
  80.9 40.6 %attend.1 = (f32[512,512]{1,0:T(8,128)}, bf16[512,512]{1,0:T(8,128)(2,1)}, f32[4,1,512]{2,1,0:T(1,128)}, bf16[4,512,512]{2,1,0:T(8,128)(2,1)}, bf16[2,2,2,64,2048]{4,3,2,1,0:T(8,128)(2,1)}) custom-call(s32[1]{0:T(128)} %dynamic_slice.65.refs_0_.refs_1_, bf16[512,512]{1,0:T(8,128)(2,1)} %get-tuple-element.134.refs_1_.refs_2_, ...), custom_call_target="tpu_custom_call" | custom-call | flops 1 | bytes 1 | tf_op jit(solution)/shard_map/attend/pallas_call | solution.py:132
  121.6 3.1 convolution_convert_fusion.1
  124.7 44.7 %sum_attention.1 = (bf16[2,64,2048]{2,1,0:T(8,128)(2,1)S(1)}, bf16[256,2304]{1,0:T(8,128)(2,1)S(1)}, f32[2,64,2048]{2,1,0:T(8,128)S(1)}) custom-call(bf16[2,64,2048]{2,1,0:T(8,128)(2,1)S(1)} %copy-done.12, bf16[256,2304]{1,0:T(8,128)(2,1)S(1)} %pad_maximum_fusion.refs_1_.refs_0_.refs_4_, bf16[2,2,2,64,2048]{4,3,2,1,0:T(8,128)(2,1)S(1)} %bitcast.82), custom_call_target="tpu_custom_call" | custom-call | flops 1 | bytes 1 | tf_op jit(solution)/shard_map/sum_attention/pallas_call | solution.py:132
  169.7 1.4 multiply_convert_fusion.refs_4_
  172.1 65.0 %gather_mlp.1 = (bf16[256,2304]{1,0:T(8,128)(2,1)}, bf16[256,2304]{1,0:T(8,128)(2,1)}, bf16[256,2304]{1,0:T(8,128)(2,1)}, bf16[256,2304]{1,0:T(8,128)(2,1)}, bf1...) custom-call(bf16[256,2304]{1,0:T(8,128)(2,1)} %copy-done.3, bf16[256,2304]{1,0:T(8,128)(2,1)} %copy-done, ...), custom_call_target="tpu_custom_call" | custom-call | flops 1 | bytes 1 | tf_op jit(solution)/shard_map/gather_mlp/pallas_call | solution.py:132
  237.2 2.2 collective-permute-start.1
  240.2 1.8 collective-permute-done.1.refs_7_.refs_11_
  243.1 26.0 %mlp.1 = (bf16[1024,768]{1,0:T(8,128)(2,1)}, bf16[1024,1536]{1,0:T(8,128)(2,1)}, bf16[2,2,256,768]{3,2,1,0:T(8,128)(2,1)}, bf16[2,2,256,768]{3,2,1,0:T(8,128)(2,1)}) custom-call(bf16[1024,2048]{1,0:T(8,128)(2,1)} %bitcast.90, bf16[2,256,2048]{2,1,0:T(8,128)(2,1)} %bitcast.94, bf16[2,256,2048]{2,1,0:T(8,128)(2,1)} %bitcast.95, ...), custom_call_target="tpu_custom_call" | custom-call | flops 1 | bytes 1 | tf_op jit(solution)/shard_map/mlp/pallas_call | solution.py:1218
  269.1 26.5 %mlp_back.1 = (bf16[2,2,256,768]{3,2,1,0:T(8,128)(2,1)}, bf16[2,2,256,768]{3,2,1,0:T(8,128)(2,1)}, bf16[2,2,256,768]{3,2,1,0:T(8,128)(2,1)}, bf16[1024,2048]{1,0:T(8,128)(2,1)}) custom-call(bf16[1024,2048]{1,0:T(8,128)(2,1)} %bitcast.91, bf16[1024,1536]{1,0:T(8,128)(2,1)} %get-tuple-element.85.refs_1_, bf16[2,2,256,768]{3,2,1,0:T(8,128)(2,1)} %get-tuple-element.86.refs_2_, ...), custom_call_target="tpu_custom_call" | custom-call | flops 1 | bytes 1 | tf_op jit(solution)/shard_map/mlp_back/pallas_call | solution.py:132
  295.7 52.2 %sum_mlp_back.1 = (bf16[2,256,768]{2,1,0:T(8,128)(2,1)S(1)}, bf16[2,256,768]{2,1,0:T(8,128)(2,1)S(1)}, f32[2,64,2048]{2,1,0:T(8,128)S(1)}, bf16[1024,2048]{1,0:T(8,128)(2,1)}) custom-call(bf16[2,2,256,768]{3,2,1,0:T(8,128)(2,1)} %get-tuple-element.89.refs_0_, bf16[2,2,256,768]{3,2,1,0:T(8,128)(2,1)} %get-tuple-element.90.refs_1_, ...), custom_call_target="tpu_custom_call" | custom-call | flops 1 | bytes 1 | tf_op jit(solution)/shard_map/sum_mlp_back/pallas_call | solution.py:132
  348.2 1.6 copy-done.39
  351.8 36.1 %gather_branch.1 = (bf16[256,768]{1,0:T(8,128)(2,1)S(1)}, bf16[256,768]{1,0:T(8,128)(2,1)S(1)}, bf16[2,256,768]{2,1,0:T(8,128)(2,1)S(1)}, bf16[2,2,2,64,2048]{4,3,2,1,0:T(8,128)(2,1)S(1)}) custom-call(bf16[2,256,768]{2,1,0:T(8,128)(2,1)S(1)} %fusion.1.refs_0_.sums, bf16[2,256,768]{2,1,0:T(8,128)(2,1)S(1)} %fusion.refs_1_.sums, ...), custom_call_target="tpu_custom_call" | custom-call | flops 1 | bytes 1 | tf_op jit(solution)/shard_map/gather_branch/pallas_call | solution.py:132
  388.2 1.7 copy-done.49
  391.2 44.5 %attend_back.1 = (bf16[256,768]{1,0:T(8,128)(2,1)S(1)}, f32[512,512]{1,0:T(8,128)S(1)}, f32[512,512]{1,0:T(8,128)S(1)}, f32[2,64,2048]{2,1,0:T(8,128)S(1)}) custom-call(bf16[2,256,768]{2,1,0:T(8,128)(2,1)S(1)} %fusion.2.refs_0_.sums, s32[1]{0:T(128)} %dynamic_slice.65.refs_0_.refs_1_, bf16[512,512]{1,0:T(8,128)(2,1)S(1)} %copy-done.13, ...), custom_call_target="tpu_custom_call" | custom-call | flops 1 | bytes 1 | tf_op jit(solution)/shard_map/attend_back/pallas_call | solution.py:132
  437.4 4.5 heads_backward.1
  442.0 4.4 attention_grads.1
  446.4 2.7 copy-done.5
  449.1 1.7 add_convert_fusion
  450.8 4.6 convolution_convert_fusion
  455.4 25.0 %sum_attention_back.1 = (bf16[64,2048]{1,0:T(8,128)(2,1)S(1)}, f32[2,64,2048]{2,1,0:T(8,128)S(1)}) custom-call(bf16[64,2048]{1,0:T(8,128)(2,1)S(1)} %dynamic-slice_bitcast_fusion.refs_0_, bf16[2,2,2,64,2048]{4,3,2,1,0:T(8,128)(2,1)S(1)} %bitcast.81), custom_call_target="tpu_custom_call" | custom-call | flops 1 | bytes 1 | tf_op jit(solution)/shard_map/sum_attention_back/pallas_call | solution.py:132
  485.0 1.4 write_down.1
  486.4 40.7 %sum_gains.1 = (bf16[64,2048]{1,0:T(8,128)(2,1)S(1)}, f32[40,128]{1,0:T(8,128)S(1)}) custom-call(bf16[64,2048]{1,0:T(8,128)(2,1)S(1)} %fusion.16.refs_0_, f32[40,128]{1,0:T(8,128)S(1)} %fusion.21.refs_1_), custom_call_target="tpu_custom_call" | custom-call | flops 1 | bytes 1 | tf_op jit(solution)/shard_map/sum_gains/pallas_call | solution.py:132
  530.3 15.2 %reduce-scatter.2.cloned.1.call-done.sums = bf16[256,1536]{1,0:T(8,128)(2,1)} async-done(((bf16[2048,1536]{1,0:T(8,128)(2,1)}), bf16[256,1536]{1,0:T(8,128)(2,1)}) %reduce-scatter.2.cloned.1.call-update) | async-done | bytes 786448 | tf_op jit(solution)/shard_map/reduce_scatter | solution.py:1490
  (158 shorter events, 23.5 us)
Async XLA Ops:
  7.2 31.4 %copy-start.46 = (bf16[2,64,2048]{2,1,0:T(8,128)(2,1)S(1)}, bf16[2,64,2048]{2,1,0:T(8,128)(2,1)}, u32[]{:S(2)}) copy-start(bf16[2,64,2048]{2,1,0:T(8,128)(2,1)} %param.14) | copy-start | bytes 1572868
  7.2 3.1 copy-start.47
  7.2 3.1 copy-start.48
  7.2 62.7 %all-gather.3.cloned.1.call-start = ((), (), s32[]{:S(2)}) async-start(), calls=%async_computation.1 | async-start | bytes 4718592 | tf_op jit(solution)/shard_map/all_gather | solution.py:1394
  9.3 112.3 %all-gather.5.cloned.1.call-start = ((), (), s32[]{:S(2)}) async-start(), calls=%async_computation.2 | async-start | bytes 2359296 | tf_op jit(solution)/shard_map/all_gather | solution.py:1401
  38.4 507.1 %reduce-scatter.2.cloned.1.call-start = ((), (), s32[]{:S(2)}) async-start(), calls=%async_computation.3 | async-start | bytes 7077888 | tf_op jit(solution)/shard_map/reduce_scatter | solution.py:1490
  38.6 130.8 %copy-start.35 = (bf16[1,64,2048]{2,1,0:T(8,128)(2,1)}, bf16[1,64,2048]{2,1,0:T(8,128)(2,1)S(1)}, u32[]{:S(2)}) copy-start(bf16[1,64,2048]{2,1,0:T(8,128)(2,1)S(1)} %get-tuple-element.137) | copy-start | bytes 786436
  38.6 130.8 %copy-start.37 = (bf16[1,64,2048]{2,1,0:T(8,128)(2,1)}, bf16[1,64,2048]{2,1,0:T(8,128)(2,1)S(1)}, u32[]{:S(2)}) copy-start(bf16[1,64,2048]{2,1,0:T(8,128)(2,1)S(1)} %get-tuple-element.138) | copy-start | bytes 786436
  38.6 18.6 %copy-start.45 = (bf16[1536,256]{1,0:T(8,128)(2,1)S(1)}, bf16[1536,256]{1,0:T(8,128)(2,1)}, u32[]{:S(2)}) copy-start(bf16[1536,256]{1,0:T(8,128)(2,1)} %param.26) | copy-start | bytes 2359300
  59.1 7.5 %copy-start.50 = (s32[2]{0:T(128)S(1)}, s32[2]{0:T(128)}, u32[]{:S(2)}) copy-start(s32[2]{0:T(128)} %param.15) | copy-start | bytes 28
  60.3 64.4 %copy-start = (bf16[256,2304]{1,0:T(8,128)(2,1)}, bf16[256,2304]{1,0:T(8,128)(2,1)S(1)}, u32[]{:S(2)}) copy-start(bf16[256,2304]{1,0:T(8,128)(2,1)S(1)} %pad_maximum_fusion.refs_1_.refs_0_.refs_4_) | copy-start | bytes 3538948
  60.3 110.8 %collective-permute-start = (bf16[256,2304]{1,0:T(8,128)(2,1)}, bf16[256,2304]{1,0:T(8,128)(2,1)S(1)}, u32[]{:S(2)}, u32[]{:S(2)}) collective-permute-start(bf16[256,2304]{1,0:T(8,128)(2,1)} %pad_maximum_fusion.1), channel_id=1, source_target_pairs={{0,16},{4,20},{8,24},{12,28},{16,0},{20,4},{24,8},{28,12},{1,17},{... | collective-permute-start | bytes 3538952 | tf_op jit(solution)/shard_map/ppermute | solution.py:1406
  121.6 3.1 copy-start.12
  172.1 67.2 %copy-start.17 = (bf16[2,64,2048]{2,1,0:T(8,128)(2,1)S(1)}, bf16[2,64,2048]{2,1,0:T(8,128)(2,1)}, u32[]{:S(2)}) copy-start(bf16[2,64,2048]{2,1,0:T(8,128)(2,1)} %copy-done.16) | copy-start | bytes 1572868
  237.2 5.9 %copy-start.1 = (bf16[256,2304]{1,0:T(8,128)(2,1)S(1)}, bf16[256,2304]{1,0:T(8,128)(2,1)}, u32[]{:S(2)}) copy-start(bf16[256,2304]{1,0:T(8,128)(2,1)} %copy-done) | copy-start | bytes 3538948
  237.2 4.9 collective-permute-start.1
  269.1 26.6 %copy-start.2 = (bf16[256,2304]{1,0:T(8,128)(2,1)S(1)}, bf16[256,2304]{1,0:T(8,128)(2,1)}, u32[]{:S(2)}) copy-start(bf16[256,2304]{1,0:T(8,128)(2,1)} %copy-done) | copy-start | bytes 3538948
  269.1 26.6 %copy-start.4 = (bf16[256,2304]{1,0:T(8,128)(2,1)S(1)}, bf16[256,2304]{1,0:T(8,128)(2,1)}, u32[]{:S(2)}) copy-start(bf16[256,2304]{1,0:T(8,128)(2,1)} %copy-done.3) | copy-start | bytes 3538948
  269.1 26.6 %copy-start.7 = (bf16[256,2304]{1,0:T(8,128)(2,1)S(1)}, bf16[256,2304]{1,0:T(8,128)(2,1)}, u32[]{:S(2)}) copy-start(bf16[256,2304]{1,0:T(8,128)(2,1)} %copy-done.6) | copy-start | bytes 3538948
  295.7 52.2 %copy-start.40 = (bf16[2,2,256,768]{3,2,1,0:T(8,128)(2,1)S(1)}, bf16[2,2,256,768]{3,2,1,0:T(8,128)(2,1)}, u32[]{:S(2)}) copy-start(bf16[2,2,256,768]{3,2,1,0:T(8,128)(2,1)} %get-tuple-element.90.refs_1_) | copy-start | bytes 4718596
  388.0 3.2 copy-start.21
  388.0 3.2 copy-start.23
  391.2 46.2 %copy-start.15 = (f32[512,1024]{1,0:T(8,128)S(1)}, f32[512,1024]{1,0:T(8,128)}, u32[]{:S(2)}) copy-start(f32[512,1024]{1,0:T(8,128)} %get-tuple-element.103.raw) | copy-start | bytes 6291460
  391.2 46.2 %copy-start.28 = (f32[128]{0:T(128)S(1)}, f32[128]{0:T(128)}, u32[]{:S(2)}) copy-start(f32[128]{0:T(128)} %param.20) | copy-start | bytes 1540
  391.2 46.2 %copy-start.29 = (f32[128]{0:T(128)S(1)}, f32[128]{0:T(128)}, u32[]{:S(2)}) copy-start(f32[128]{0:T(128)} %param.21) | copy-start | bytes 1540
  391.2 46.2 %copy-start.30 = (f32[1,128]{1,0:T(1,128)S(1)}, f32[1,128]{1,0:T(1,128)}, u32[]{:S(2)}) copy-start(f32[1,128]{1,0:T(1,128)} %broadcast_in_dim_tile.5.frequency) | copy-start | bytes 1540
  437.4 4.5 copy-start.9
  437.4 4.5 copy-start.20
  455.3 25.0 %copy-start.24 = (bf16[256,768]{1,0:T(8,128)(2,1)S(1)}, bf16[256,768]{1,0:T(8,128)(2,1)}, u32[]{:S(2)}) copy-start(bf16[256,768]{1,0:T(8,128)(2,1)} %copy-done.23) | copy-start | bytes 1179652
  455.3 26.4 %copy-start.26 = (bf16[256,768]{1,0:T(8,128)(2,1)S(1)}, bf16[256,768]{1,0:T(8,128)(2,1)}, u32[]{:S(2)}) copy-start(bf16[256,768]{1,0:T(8,128)(2,1)} %copy-done.25) | copy-start | bytes 1179652
  480.4 2.8 copy-start.36
  480.4 2.8 copy-start.38
  (24 other events, 37.4 us)
Sparse Core Ops, SparseCore 0:
  10.2 49.6 all-gather.2
  61.5 58.3 all-gather.4
  449.2 96.2 reduce-scatter.1

commit v4 on v3

--- a/solution.py
+++ b/solution.py
@@ -398,7 +398,6 @@
     _, pair = pair_peer()
     greet([across, pair] + along + riders.peers())
     over_pair = send(src, dst.at[1, :, a, b], pair_sems.at[0], pair_sems.at[1], pair)
-    riders.start()
     homes = [
         pltpu.make_async_copy(src, dst.at[0, :, a, b], local_sems.at[0]),
         pltpu.make_async_copy(beside, beside_dst.at[:, a, b], local_sems.at[1]),
@@ -420,6 +419,7 @@
     planes[1].start()
     planes[0].forward()
     over_pair.wait_recv()
+    riders.start()
     planes[2].start()
     planes[1].forward()
     planes[2].forward()
@@ -451,8 +451,8 @@
 
 
 class PairSum:
-    def __init__(self, high, src, out, scratch):
-        self.high, self.src, self.out = high, src, out
+    def __init__(self, high, src, out, scratch, base=None):
+        self.high, self.src, self.out, self.base = high, src, out, base
         self.recv0, self.mid0, self.last0, self.recv1, self.mid1, self.last1 = scratch[:6]
         self.own0, self.own1, self.given, self.taken = scratch[6:10]
         self.send_sems, self.recv_sems, self.pair_sems, self.local_sems = scratch[10:]
@@ -486,17 +486,24 @@
         self.sent[i].append(copy)
         return copy
 
+    def block(self, i):
+        row = pair_peer()[0]
+        return row if i else 1 - row
+
     def start(self, i):
         a, b, across, along = self.place
-        part = self.src.at[1 - i]
-        over0 = self.push(i, part.at[0, :, 1 - b], self.recv0.at[i], across)
+        if self.base is None:
+            first, second = self.src.at[1 - i, 0], self.src.at[1 - i, 1]
+        else:
+            first, second = self.src.at[0, self.block(i)], self.src.at[1, self.block(i)]
+        over0 = self.push(i, first.at[:, 1 - b], self.recv0.at[i], across)
         up1 = [
-            self.push(i, part.at[1, lax.rem(a + k, self.high)], self.recv1.at[i, k - 1], along[k - 1])
+            self.push(i, second.at[lax.rem(a + k, self.high)], self.recv1.at[i, k - 1], along[k - 1])
             for k in range(1, self.high)
         ]
         loads = [
-            pltpu.make_async_copy(part.at[0, :, b], self.own0.at[i], self.local_sems.at[i, 0]),
-            pltpu.make_async_copy(part.at[1, a], self.own1.at[i], self.local_sems.at[i, 1]),
+            pltpu.make_async_copy(first.at[:, b], self.own0.at[i], self.local_sems.at[i, 0]),
+            pltpu.make_async_copy(second.at[a], self.own1.at[i], self.local_sems.at[i, 1]),
         ]
         for load in loads:
             load.start()
@@ -532,6 +539,8 @@
         result0 = self.own0[i, pl.ds(a, 1)][0].astype(F32) + self.recv0[i, pl.ds(a, 1)][0].astype(F32)
         for k in range(1, self.high):
             result0 = result0 + self.last0[i, k - 1].astype(F32)
+        if self.base is not None:
+            result0 = result0 + self.base[pl.ds(self.block(i), 1)][0]
         over1.wait_recv()
         result1 = self.own1[i, pl.ds(b, 1)][0].astype(F32) + self.last1[i].astype(F32)
         for k in range(1, self.high):
@@ -548,14 +557,14 @@
 
     def finish(self):
         self.over_pair.wait_recv()
-        self.out[...] += self.taken[...].astype(F32)
+        for k in range(2):
+            self.out[k] += self.taken[k if self.base is None else 1 - k].astype(F32)
         self.over_pair.wait_send()
         for copy in self.sent[0] + self.sent[1]:
             copy.wait_send()
 
 
-def sum_pair_kernel(high, count, riders, src, inner, *refs):
-    blocks, (out, product, weights, sems, *scratch) = refs[:count], refs[count:]
+def sum_pair_kernel(high, riders, src, inner, weights, out, product, *scratch):
     a, b, across, along = plane_peers(high)
     greet([across, pair_peer()[1]] + along + riders.peers())
     riders.start()
@@ -563,7 +572,14 @@
     whole.start(0)
     whole.middle(0)
     whole.start(1)
-    mlp_out_kernel(blocks, inner, product, weights, sems)
+    tile = 512
+
+    def one(t, carry):
+        here = pl.ds(pl.multiple_of(t * tile, tile), tile)
+        product[here, :] = nt(inner[here, :], weights[...]).astype(BF16)
+        return carry
+
+    lax.fori_loop(0, inner.shape[0] // tile, one, 0)
     whole.last(0)
     whole.middle(1)
     whole.last(1)
@@ -576,19 +592,19 @@
     return partial_sums.reshape(2, 2, grp // 2, 2, tokens // (4 * grp), width)
 
 
-def sum_pair(partial_sums, blocks, inner, grp, collective_id, name, riders=()):
+def sum_pair(partial_sums, inner, weights, grp, collective_id, name, riders=()):
     parts = pair_parts(partial_sums, grp)
     high, _, rows, width = parts.shape[2:]
     (result, product), arrived = carried_call(
-        partial(sum_pair_kernel, high, len(blocks)),
-        [parts, inner, *blocks],
+        partial(sum_pair_kernel, high),
+        [parts, inner, weights],
         [
             jax.ShapeDtypeStruct((2, rows, width), F32),
             jax.ShapeDtypeStruct(partial_sums.shape, BF16),
         ],
-        [ANY, VMEM] + [ANY] * len(blocks),
+        [ANY, VMEM, VMEM],
         [VMEM, VMEM],
-        [pltpu.VMEM((width, inner.shape[1]), BF16), DMA((len(blocks),))] + PairSum.scratch(high, rows, width),
+        PairSum.scratch(high, rows, width),
         comm_params(collective_id, 48),
         name,
         riders,
@@ -612,22 +628,29 @@
         sine[part * rows : (part + 1) * rows] = jnp.sin(angles)
 
 
-def heads_kernel(queries, keys, x, w, frequency, query_gain, key_gain, raw, out, cosine, sine):
+def heads_kernel(queries, keys, x, w, frequency, query_gain, key_gain, raw, q, kv, cosine, sine):
     step, dim = pl.program_id(0), cosine.shape[1]
     pl.when(step == 0)(lambda: fill_tables(frequency, cosine, sine))
     raw[...] = nn(x[...], w[...])
     for i in range(raw.shape[1] // dim):
         head, cut = step * (raw.shape[1] // dim) + i, slice(i * dim, (i + 1) * dim)
 
-        @pl.when(head < queries + keys)
+        def turned(gain):
+            unit, _ = normalize(raw[:, cut])
+            scaled = unit * gain[...]
+            return (scaled * cosine[...] + turn_half(scaled) * sine[...]).astype(BF16)
+
+        @pl.when(head < queries)
         def _():
-            unit, _ = normalize(raw[:, cut])
-            scaled = unit * jnp.where(head < queries, query_gain[...], key_gain[...])
-            out[:, cut] = (scaled * cosine[...] + turn_half(scaled) * sine[...]).astype(BF16)
+            q[:, cut] = turned(query_gain)
+
+        @pl.when((head >= queries) & (head < queries + keys))
+        def _():
+            kv[:, cut] = turned(key_gain)
 
         @pl.when(head >= queries + keys)
         def _():
-            out[:, cut] = raw[:, cut].astype(BF16)
+            kv[:, cut] = raw[:, cut].astype(BF16)
 
 
 def heads_forward(x, w, small, queries, keys):
@@ -642,7 +665,8 @@
         grid=(width // step,),
         out_shape=[
             jax.ShapeDtypeStruct((tokens, width), F32),
-            jax.ShapeDtypeStruct((tokens, width), BF16),
+            jax.ShapeDtypeStruct((tokens, queries * dim), BF16),
+            jax.ShapeDtypeStruct((tokens, 2 * keys * dim), BF16),
         ],
         in_specs=[
             pl.BlockSpec((tokens, depth), lambda h: (0, 0)),
@@ -651,7 +675,11 @@
             one,
             one,
         ],
-        out_specs=[column, column],
+        out_specs=[
+            column,
+            pl.BlockSpec((tokens, step), lambda h: (0, jnp.minimum(h, queries // 2 - 1))),
+            pl.BlockSpec((tokens, step), lambda h: (0, jnp.maximum(h - queries // 2, 0))),
+        ],
         scratch_shapes=[pltpu.VMEM((tokens, dim), F32), pltpu.VMEM((tokens, dim), F32)],
         compiler_params=pltpu.CompilerParams(vmem_limit_bytes=60 * 2**20),
     )(x, w, *small)
@@ -904,6 +932,7 @@
     log_total,
     kv_all,
     beside,
+    base,
     grad_q,
     grad_kv,
     beside_out,
@@ -928,7 +957,7 @@
     me = place * 2 + core
     _, _, across, along = plane_peers(high)
     greet([cross] + others + [across, pair_peer()[1]] + along + riders.peers())
-    whole = PairSum(high, beside, beside_out, beside_scratch)
+    whole = PairSum(high, beside, beside_out, beside_scratch, base)
     whole.start(0)
     riders.start()
     acc[...] = jnp.zeros_like(acc)
@@ -1024,7 +1053,7 @@
 
 
 def attend_back(
-    length, q, kv_all, mixed, grad_mixed, log_total, beside, grp, keys, repeat, dim, collective_id, riders=()
+    length, q, kv_all, mixed, grad_mixed, log_total, beside, base, grp, keys, repeat, dim, collective_id, riders=()
 ):
     owners, tokens, kv_width = kv_all.shape
     rows, width = tokens // 2, keys * repeat * dim
@@ -1034,13 +1063,13 @@
     slots = pltpu.VMEM((chips, tokens, kv_width), BF16)
     return carried_call(
         partial(attend_back_kernel, (rows, keys, repeat, dim), chips, high),
-        [length, q, mixed, grad_mixed, log_total, kv_all, parts],
+        [length, q, mixed, grad_mixed, log_total, kv_all, parts, base],
         [
             jax.ShapeDtypeStruct((tokens, width), F32),
             jax.ShapeDtypeStruct((tokens, kv_width), F32),
             jax.ShapeDtypeStruct((2, beside_rows, beside_width), F32),
         ],
-        [pl.BlockSpec(memory_space=pltpu.SMEM), VMEM, VMEM, VMEM, VMEM, ANY, ANY],
+        [pl.BlockSpec(memory_space=pltpu.SMEM), VMEM, VMEM, VMEM, VMEM, ANY, ANY, VMEM],
         [VMEM, VMEM, VMEM],
         [
             pltpu.VMEM((tokens, kv_width), BF16),
@@ -1114,28 +1143,16 @@
     )(sums)
 
 
-def load_weights(blocks, first, weights, sems):
+def owner_of(kind, core):
     s = lax.axis_index("seq")
     line = lax.axis_size("seq") // 2
-    chips = line // 2
-    row, place, core = s // line, lax.rem(s, line) // 2, lax.rem(s, 2)
-    depth, width = blocks[0].shape[0], weights.shape[1]
-    copies = []
-    for i, src in enumerate(blocks):
-        which = row if i // chips % 2 == 0 else 1 - row
-        back = lax.rem(place + chips - i % chips, chips)
-        owner = which * line + back * 2 + (core if i < 2 * chips else 1 - core)
-        copy = pltpu.make_async_copy(
-            src.at[:, pl.ds(first, width)], weights.at[pl.ds(owner * depth, depth)], sems.at[i]
-        )
-        copy.start()
-        copies.append(copy)
-    for copy in copies:
-        copy.wait()
-    return depth
-
-
-def weight_grads(x, grads, keep, give):
+    other, back = kind
+    half = 1 - s // line if other else s // line
+    place = lax.rem(lax.rem(s, line) // 2 + line // 2 - back, line // 2)
+    return half * line + place * 2 + core
+
+
+def weight_grads(x, grads, keep, give, first=0, last=None):
     chips, halves, depth, _ = keep.shape
     core = lax.rem(lax.axis_index("seq"), 2)
 
@@ -1156,11 +1173,33 @@
 
         return carry
 
-    lax.fori_loop(0, halves * chips, one, 0)
-
-
-def mlp_kernel(rows, cot_home, cot_away, *refs):
-    *blocks, inner, grad_pre, keep, give, weights, cot, sems, cot_sems = refs
+    lax.fori_loop(first, halves * chips if last is None else last, one, 0)
+
+
+def mlp_kernel(shared, alone, rows, cot_home, cot_away, *refs):
+    count = 2 * len(shared) + len(alone)
+    blocks, refs = refs[:count], refs[count:]
+    inner, out_weights, down, gate, up, grad_rows, refs = *refs[:6], refs[6:]
+    weights, cot, grad_pre, keep_down, give_down, got_down, keep, give, got, *refs = refs
+    *far_down, weight_sems, over_sems, cot_sems, core_sems, chip_sems = refs
+    core, mate = lax.rem(lax.axis_index("seq"), 2), peer_of("core")
+    depth, chips = blocks[0].shape[0], keep.shape[0]
+    greet([mate] + [peer_of(k) for k in range(1, chips)])
+
+    def place(kind, which):
+        return weights.at[pl.ds(pl.multiple_of(owner_of(kind, which) * depth, depth), depth)]
+
+    over = [
+        send(src, place(kind, core), over_sems.at[0, i], over_sems.at[1, i], mate)
+        for i, (kind, src) in enumerate(zip(alone, blocks[2 * len(shared) :]))
+    ]
+    kinds = [(kind, core) for kind in shared] + [(kind, 1 - core) for kind in shared]
+    kinds += [(kind, core) for kind in alone]
+    loads = []
+    for i, ((kind, which), src) in enumerate(zip(kinds, blocks)):
+        loads.append(pltpu.make_async_copy(src, place(kind, which), weight_sems.at[i]))
+        loads[i].start()
+
     block = cot_home.shape[1]
     row = lax.axis_index("seq") // (lax.axis_size("seq") // 2)
 
@@ -1179,9 +1218,13 @@
             for i, src in enumerate(order):
                 load(i, src).start()
 
-    depth = load_weights(blocks, 0, weights, sems)
+    for copy in loads:
+        copy.wait()
     for i in range(4):
         load(i, cot_home.at[0]).wait()
+    for copy in over:
+        copy.wait()
+
     units = inner.shape[1]
     step = 256 if units % 256 == 0 else 128
     tile = 512
@@ -1192,114 +1235,103 @@
         first = pl.multiple_of((t // tiles) * step, step)
         cols = pl.ds(first, step)
         x = rows[here, :]
-        gate = nn(x, weights[:, cols])
-        up = nn(x, weights[:, pl.ds(units + first, step)])
+        gate_pre = nn(x, weights[:, cols])
+        up_pre = nn(x, weights[:, pl.ds(units + first, step)])
         grad = nn(cot[here, :], weights[:, pl.ds(2 * units + first, step)])
-        sigmoid = jax.nn.sigmoid(gate)
-        silu = gate * sigmoid
-        inner[here, cols] = (silu * up).astype(BF16)
-        grad_pre[here, cols] = (grad * up * sigmoid * (1.0 + gate * (1.0 - sigmoid))).astype(BF16)
+        sigmoid = jax.nn.sigmoid(gate_pre)
+        silu = gate_pre * sigmoid
+        inner[here, cols] = (silu * up_pre).astype(BF16)
+        grad_gate = grad * up_pre * sigmoid * (1.0 + gate_pre * (1.0 - sigmoid))
+        grad_pre[here, cols] = grad_gate.astype(BF16)
         grad_pre[here, pl.ds(units + first, step)] = (grad * silu).astype(BF16)
         return carry
 
     lax.fori_loop(0, tiles * (units // step), one, 0)
-
-    weight_grads(cot, inner, keep, give)
-
-
-def grads_shape(width, columns):
-    chips = lax.axis_size("seq") // 4
-    return jax.ShapeDtypeStruct((chips, 2, width // chips // 4, columns), BF16)
-
-
-def mlp(blocks, rows, cot_home, cot_away):
-    (tokens, width), columns = rows.shape, blocks[0].shape[1]
-    units = columns // 3
-    return pl.pallas_call(
-        mlp_kernel,
-        cost_estimate=NO_COST,
-        name="mlp",
-        in_specs=[VMEM, ANY, ANY] + [ANY] * len(blocks),
-        out_specs=[VMEM] * 4,
-        out_shape=[
-            jax.ShapeDtypeStruct((tokens, units), BF16),
-            jax.ShapeDtypeStruct((tokens, 2 * units), BF16),
-            grads_shape(width, units),
-            grads_shape(width, units),
-        ],
-        scratch_shapes=[
-            pltpu.VMEM((width, columns), BF16),
-            pltpu.VMEM((tokens, width), BF16),
-            DMA((len(blocks),)),
-            DMA((4,)),
-        ],
-        compiler_params=pltpu.CompilerParams(vmem_limit_bytes=52 * 2**20),
-    )(rows, cot_home, cot_away, *blocks)
-
-
-def mlp_back_kernel(riders, rows, grad_pre, keep_down, give_down, *refs):
-    *blocks, down, gate, up, grad_rows, keep, give, got, got_down, weights, sems, core_sems = refs
-    core = peer_of("core")
-    greet([core])
-    over_down = send(give_down, got_down, core_sems.at[0, 0], core_sems.at[0, 1], core)
-    load_weights(blocks, 0, weights, sems)
-    weight_grads(rows, grad_pre, keep, give)
-    over = send(give, got, core_sems.at[1, 0], core_sems.at[1, 1], core)
-    tile = 512
-
-    def one(t, carry):
+    weight_grads(cot, inner, keep_down, give_down)
+    over_down = send(give_down, got_down, core_sems.at[0, 0], core_sems.at[0, 1], mate)
+    weight_grads(rows, grad_pre, keep, give, 0, chips)
+    over_down.wait()
+
+    def add_down(t, carry):
+        at = (lax.rem(t, chips), t // chips)
+        keep_down[at] = (keep_down[at].astype(F32) + got_down[at].astype(F32)).astype(BF16)
+        return carry
+
+    lax.fori_loop(0, 2 * chips, add_down, 0)
+    to_chips = [
+        send(
+            keep_down.at[part_of(k, "chip")],
+            far_down[k - 1],
+            chip_sems.at[0, k - 1],
+            chip_sems.at[1, k - 1],
+            peer_of(k),
+        )
+        for k in range(1, chips)
+    ]
+    weight_grads(rows, grad_pre, keep, give, chips, None)
+    over_pre = send(give, got, core_sems.at[1, 0], core_sems.at[1, 1], mate)
+
+    def two(t, carry):
         here = pl.ds(pl.multiple_of(t * tile, tile), tile)
-        grad_rows[here, :] = nt(grad_pre[here, :], weights[...]).astype(BF16)
+        grad_rows[here, :] = nt(grad_pre[here, :], weights[:, : 2 * units]).astype(BF16)
         return carry
 
-    lax.fori_loop(0, rows.shape[0] // tile, one, 0)
-    units = gate.shape[-1]
-    over_down.wait()
-    over.wait()
+    lax.fori_loop(0, tiles, two, 0)
+    out_weights[...] = weights[:, 2 * units :]
+    over_pre.wait()
 
     def add(t, carry):
-        at = (lax.rem(t, keep.shape[0]), t // keep.shape[0])
-        down[at] = (keep_down[at].astype(F32) + got_down[at].astype(F32)).astype(BF16)
+        at = (lax.rem(t, chips), t // chips)
         both = (keep[at].astype(F32) + got[at].astype(F32)).astype(BF16)
         gate[at] = both[:, :units]
         up[at] = both[:, units:]
         return carry
 
-    lax.fori_loop(0, 2 * keep.shape[0], add, 0)
-
-
-def mlp_back(blocks, rows, grad_pre, keep_down, give_down, collective_id):
-    (tokens, width), columns = rows.shape, grad_pre.shape[1]
-    one, two = grads_shape(width, columns // 2), grads_shape(width, columns)
+    lax.fori_loop(0, 2 * chips, add, 0)
+    total_down = keep_down[pl.ds(part_of(0, "chip"), 1)][0].astype(F32)
+    for k, copy in enumerate(to_chips):
+        copy.wait()
+        total_down = total_down + far_down[k][...].astype(F32)
+    down[...] = total_down.astype(BF16)
+
+
+def grads_shape(width, columns):
+    chips = lax.axis_size("seq") // 4
+    return jax.ShapeDtypeStruct((chips, 2, width // chips // 4, columns), BF16)
+
+
+def mlp(shared, alone, rows, cot_home, cot_away, collective_id):
+    blocks = [x for x, _ in shared.values()] + [x for _, x in shared.values()] + list(alone.values())
+    (tokens, width), columns = rows.shape, blocks[0].shape[1]
+    units = columns // 3
+    one, two = grads_shape(width, units), grads_shape(width, 2 * units)
+    far, others = jax.ShapeDtypeStruct(one.shape[1:], BF16), one.shape[0] - 1
     results, _ = carried_call(
-        mlp_back_kernel,
-        [rows, grad_pre, keep_down, give_down, *blocks],
-        [one, one, one, jax.ShapeDtypeStruct((tokens, width), BF16)],
-        [VMEM, VMEM, VMEM, ANY] + [ANY] * len(blocks),
-        [VMEM] * 4,
-        [pltpu.VMEM(two.shape, BF16)] * 3
-        + [
-            pltpu.VMEM(one.shape, BF16),
+        lambda riders, *refs: mlp_kernel(list(shared), list(alone), *refs),
+        [rows, cot_home, cot_away, *blocks],
+        [
+            jax.ShapeDtypeStruct((tokens, units), BF16),
+            jax.ShapeDtypeStruct((width, units), BF16),
+            far,
+            one,
+            one,
+            jax.ShapeDtypeStruct((tokens, width), BF16),
+        ],
+        [VMEM, ANY, ANY] + [ANY] * len(blocks),
+        [VMEM] * 6,
+        [
             pltpu.VMEM((width, columns), BF16),
-            DMA((len(blocks),)),
-            DMA((2, 2)),
-        ],
+            pltpu.VMEM((tokens, width), BF16),
+            pltpu.VMEM((tokens, 2 * units), BF16),
+        ]
+        + [pltpu.VMEM(one.shape, BF16)] * 3
+        + [pltpu.VMEM(two.shape, BF16)] * 3
+        + [pltpu.VMEM(far.shape, BF16)] * others
+        + [DMA((len(blocks),)), DMA((2, len(alone))), DMA((4,)), DMA((2, 2)), DMA((2, others))],
         comm_params(collective_id, 60),
-        "mlp_back",
+        "mlp",
     )
     return results
-
-
-def mlp_out_kernel(blocks, inner, out, weights, sems):
-    load_weights(blocks, 2 * inner.shape[1], weights, sems)
-    tile = 512
-
-    def one(t, carry):
-        here = pl.ds(pl.multiple_of(t * tile, tile), tile)
-        out[here, :] = nt(inner[here, :], weights[...]).astype(BF16)
-        return carry
-
-    lax.fori_loop(0, inner.shape[0] // tile, one, 0)
 
 
 def write_kernel(sums, taken, out):
@@ -1383,6 +1415,9 @@
     steps = range(1, chips)
     place = lax.rem(seq_index, line) // 2
 
+    def next_chip(k):
+        return [(s, s - s % line + (s % line + 2 * k) % line) for s in range(seq)]
+
     def chips_sum(parts, arrived):
         mine = lax.dynamic_index_in_dim(parts, place, 0, keepdims=False)
         return sum([x.astype(F32) for x in arrived], mine.astype(F32)).astype(BF16)
@@ -1410,61 +1445,56 @@
 
     frequency = ROPE_BASE ** (-jnp.arange(dim // 2, dtype=F32) * 2.0 / dim)
     small = [jnp.tile(frequency, 2)[None], query_gain[None], key_gain[None]]
-    raw, heads = heads_forward(attn_rows, full_qkv, small, queries, keys)
-    q, kv_home = heads[:, : queries * dim], heads[:, queries * dim :]
+    raw, q, kv_home = heads_forward(attn_rows, full_qkv, small, queries, keys)
 
     (mixed, mixed_low, log_total, kv_all, cot_gathered), _ = attend(
         length, q, kv_home, cot_home, seq, grp, keys, repeat, dim, 3
     )
     cot_gathered = cot_gathered.reshape(2, rows, width)
-    summed, (taken_cotangent, *passed) = sum_rows(
-        nt(mixed_low, full_out),
-        grp,
-        4,
-        "sum_attention",
-        [("opposite", cot_home)] + [(k, kept_half) for k in steps],
-    )
-    own_half = [kept_half] + passed
+    near = after(kept_half, mixed)
+    kept_passed = [lax.ppermute(near, "seq", next_chip(k)) for k in steps]
+    summed, (taken_cotangent,) = sum_rows(
+        nt(mixed_low, full_out), grp, 4, "sum_attention", [("opposite", cot_home)]
+    )
     early = jnp.where(row == 0, cot_home[0], taken_cotangent[1])
     late = jnp.where(row == 0, taken_cotangent[0], cot_home[1])
     cot_rows = jnp.stack([early, late]).astype(F32)
     hidden = residual + summed
 
     mlp_unit, mlp_inverse = normalize(hidden)
-    first_blocks = own_half + [taken_half]
-    mlp_rows, cot_away, arrived = gather_pair(
+    mlp_rows, cot_away, (core_kept, core_taken, *taken_passed) = gather_pair(
         (mlp_unit * gain_mlp).astype(BF16),
         taken_cotangent,
         grp,
         5,
         "gather_mlp",
-        [(k, taken_half) for k in steps] + [("core", x) for x in first_blocks],
-    )
-    passed, core_blocks = arrived[: len(steps)], arrived[len(steps) :]
-    core_swap = [(s, s ^ 1) for s in range(seq)]
-    core_blocks += [lax.ppermute(x, "seq", core_swap) for x in passed]
-    blocks_w = first_blocks + passed + core_blocks
-    inner_low, grad_pre, keep_down, give_down = mlp(blocks_w, mlp_rows, cot_gathered, cot_away)
-    down, gate, up, grad_mlp_part = mlp_back(blocks_w, mlp_rows, grad_pre, keep_down, give_down, 13)
+        [("core", kept_half), ("core", taken_half)] + [(k, taken_half) for k in steps],
+    )
+    shared = {(False, 0): (kept_half, core_kept), (True, 0): (taken_half, core_taken)}
+    alone = {(False, k): x for k, x in zip(steps, kept_passed)}
+    alone.update({(True, k): x for k, x in zip(steps, taken_passed)})
+    inner_low, down_weights, down, gate, up, grad_mlp_part = mlp(
+        shared, alone, mlp_rows, cot_gathered, cot_away, 13
+    )
     grad_mlp_in, out_part, arrived = sum_pair(
         grad_mlp_part,
-        blocks_w,
         inner_low,
+        down_weights,
         grp,
         7,
         "sum_mlp_back",
-        to_chips(down) + to_chips(gate),
-    )
-    down = chips_sum(down, arrived[: len(steps)])
-    gate = chips_sum(gate, arrived[len(steps) :])
+        [("opposite", down, "row")] + to_chips(gate),
+    )
+    taken_down, *arrived = arrived
+    gate = chips_sum(gate, arrived)
     grad_gain_mlp = jnp.sum(grad_mlp_in * mlp_unit, axis=(0, 1))
     grad_hidden = cot_rows + norm_back(grad_mlp_in * gain_mlp, mlp_unit, mlp_inverse)
-    grad_branch, (taken_down, taken_gate, *arrived) = gather_rows(
+    grad_branch, (taken_gate, *arrived) = gather_rows(
         grad_hidden.astype(BF16),
         grp,
         8,
         "gather_branch",
-        [("opposite", down, "row"), ("opposite", gate, "row")] + to_chips(up),
+        [("opposite", gate, "row")] + to_chips(up),
     )
     up = chips_sum(up, arrived)
 
@@ -1477,6 +1507,7 @@
         grad_mixed,
         log_total,
         out_part,
+        hidden,
         grp,
         keys,
         repeat,
@@ -1484,19 +1515,12 @@
         9,
         [("opposite", up, "row")],
     )
-    output = (hidden + summed).astype(BF16)
+    output = jnp.where(row == 0, summed, summed[::-1]).astype(BF16)
     grad_raw, head_gain_parts = heads_backward(raw, grad_q, grad_kv, small, queries, keys)
     grad_w_attn = attention_grads(attn_rows, grad_raw, grad_branch, mixed_low)
     sum_attn = lax.psum_scatter(grad_w_attn, "seq", scatter_dimension=0, tiled=True)
     grad_attn_part = nt(after(grad_raw, grad_w_attn), full_qkv)
-    grad_attn_in, (taken_output,) = sum_rows(
-        grad_attn_part,
-        grp,
-        10,
-        "sum_attention_back",
-        [("opposite", to_give(output))],
-    )
-    output = both_rows(output, taken_output)
+    grad_attn_in, _ = sum_rows(grad_attn_part, grp, 10, "sum_attention_back")
     wide_shape = (depth, hidden_units)
     taken_down, taken_gate, taken_up = after((taken_down, taken_gate, taken_up), grad_attn_in)
     out_down = write(write_down_kernel, down, taken_down, wide_shape[::-1], "write_down")
@@ -1514,7 +1538,9 @@
     vector = jnp.concatenate([grad_gain_attn, grad_gain_mlp, head_gain_grads.reshape(-1)])
     padded = -(-vector.shape[0] // 1024) * 1024
     vector = jnp.pad(vector, (0, padded - vector.shape[0])).reshape(-1, 128)
-    sums, (taken_grads,) = total(vector, seq, grp, 12, [("opposite", to_give(grad_tokens).astype(BF16))])
+    sums, (taken_grads,) = total(
+        vector, seq, grp, 12, [("opposite", to_give(grad_tokens).astype(BF16))]
+    )
     sums = sums.reshape(-1)
     grad_tokens = both_rows(grad_tokens, taken_grads.astype(F32))
     place = (seq_index * grp + grp_index) * chunk

time: 564 us -> 517 us (0.917)
  Pallas kernels: 469 us -> 436 us
    pallas_call x1 -> x0, Pallas kernels: 26 us -> none  [mlp(): pl.pallas_call(mlp_kernel, cost_estimate=NO_COST, name='mlp', in_specs=[V...]
    pallas_call x11, Pallas kernels: 420 us -> 412 us  [carried_call(): pl.pallas_call(body, name=name, cost_estimate=NO_COST, out_shape=[jax.Sha...]
    unnamed x104 -> x90, local copies, waits for them, and re-layouts: 14.6 us -> 14.2 us
  transfers between devices with their start and end apart: 5 -> 5, of which waited for: 2 -> 1; matrix products, arithmetic and copies ran while one was open for 5% -> 4% of each run, Pallas kernels for 38% -> 51%
where the time goes in v4:
time: 517 us; the launch traced here: 508 us
  Pallas kernels  436 us (84%)
  local copies, waits for them, and re-layouts  19 us (4%)
  between operations  14.7 us (3%)
  waiting for transfers between devices  11.9 us (2%)
  other arithmetic  11.1 us (2%)
  matrix products  9.23 us (2%)
  starting transfers between devices  6.43 us (1%)
    pallas_call x11, Pallas kernels, carried_call(): pl.pallas_call(body, name=name, cost_estimate=NO_COST, out_shape=[jax.Sha...  412 us
    unnamed x90, local copies, waits for them, and re-layouts  14.2 us
    reduce_scatter x1, waiting for transfers between devices, shards(): lax.psum_scatter(grad_w_attn, 'seq', scatter_dimension=0, tiled=True)  11.9 us
  transfers between devices with their start and end apart: 5, of which 1 were waited for; matrix products, arithmetic and copies ran while one was open for 4% of the time, Pallas kernels for 51%

profile of v4, /device:TPU:9, one launch (start us, length us, event | category | flops | bytes accessed | tf_op | source)
XLA Modules:
  0.0 507.9 jit_solution(15850906107820953163)
XLA Ops:
  7.3 2.0 pad_maximum_fusion.4
  10.4 28.0 %gather_gains.1 = (bf16[64,2048]{1,0:T(8,128)(2,1)S(1)}, f32[4,8,8,128]{3,2,1,0:T(8,128)S(1)}) custom-call(bf16[64,2048]{1,0:T(8,128)(2,1)S(1)} %dynamic-slice_bitcast_fusion.refs_0_, f32[8,128]{1,0:T(8,128)S(1)} %select_maximum_fusion.2.refs_1_), custom_call_target="tpu_custom_call" | custom-call | flops 1 | bytes 1 | tf_op jit(solution)/shard_map/gather_gains/pallas_call | solution.py:132
  39.1 16.8 %gather_inputs.1 = bf16[2,2,2,64,2048]{4,3,2,1,0:T(8,128)(2,1)S(1)} custom-call(bf16[2,64,2048]{2,1,0:T(8,128)(2,1)S(1)} %fusion.6.refs_0_), custom_call_target="tpu_custom_call" | custom-call | flops 1 | bytes 1 | tf_op jit(solution)/shard_map/gather_inputs/pallas_call | solution.py:132
  55.9 1.4 copy-done.1
  58.4 1.2 constant_dynamic-slice_fusion.1
  61.8 6.2 %collective-permute-start = (bf16[256,2304]{1,0:T(8,128)(2,1)}, bf16[256,2304]{1,0:T(8,128)(2,1)S(1)}, u32[]{:S(2)}, u32[]{:S(2)}) collective-permute-start(bf16[256,2304]{1,0:T(8,128)(2,1)} %pad_maximum_fusion.1), channel_id=1, source_target_pairs={{0,16},{4,20},{8,24},{12,28},{16,0},{20,4},{24,8},{28,12},{1,17},{... | collective-permute-start | bytes 3538952 | tf_op jit(solution)/shard_map/ppermute | solution.py:1441
  70.3 8.9 %heads_forward.1 = (f32[512,1024]{1,0:T(8,128)}, bf16[512,512]{1,0:T(8,128)(2,1)}, bf16[512,512]{1,0:T(8,128)(2,1)}) custom-call(bf16[512,2048]{1,0:T(8,128)(2,1)} %bitcast.63, bf16[2048,1024]{1,0:T(8,128)(2,1)} %all-gather.3.cloned.1.call-done.w, f32[1,128]{1,0:T(1,128)} %broadcast_in_dim_tile.5.frequency, f32[1,128]{1,0:T(1,128)} %bitcast.69, ...), custom_call_target="tpu_custom_call" | custom-call | flops 1 | bytes 1 | tf_op jit(solution)/shard_map/heads_forward/pallas_call | solution.py:661
  79.2 43.8 %attend.1 = (f32[512,512]{1,0:T(8,128)}, bf16[512,512]{1,0:T(8,128)(2,1)}, f32[4,1,512]{2,1,0:T(1,128)}, bf16[4,512,512]{2,1,0:T(8,128)(2,1)}, bf16[2,2,2,64,2048]{4,3,2,1,0:T(8,128)(2,1)}) custom-call(s32[1]{0:T(128)} %dynamic_slice.56.refs_0_.refs_1_, bf16[512,512]{1,0:T(8,128)(2,1)} %get-tuple-element.67.refs_1_.refs_2_, ...), custom_call_target="tpu_custom_call" | custom-call | flops 1 | bytes 1 | tf_op jit(solution)/shard_map/attend/pallas_call | solution.py:132
  123.2 3.1 convolution_convert_fusion.1
  126.3 41.6 %sum_attention.1 = (bf16[2,64,2048]{2,1,0:T(8,128)(2,1)S(1)}, f32[2,64,2048]{2,1,0:T(8,128)S(1)}) custom-call(bf16[2,64,2048]{2,1,0:T(8,128)(2,1)S(1)} %copy-done.3, bf16[2,2,2,64,2048]{4,3,2,1,0:T(8,128)(2,1)S(1)} %bitcast.65), custom_call_target="tpu_custom_call" | custom-call | flops 1 | bytes 1 | tf_op jit(solution)/shard_map/sum_attention/pallas_call | solution.py:132
  168.2 1.1 multiply_convert_fusion.refs_3_
  170.3 52.9 %gather_mlp.1 = (bf16[256,2304]{1,0:T(8,128)(2,1)}, bf16[256,2304]{1,0:T(8,128)(2,1)}, bf16[256,2304]{1,0:T(8,128)(2,1)}, bf16[2,2,2,2,64,2048]{5,4,3,2,1,0:T(8,128)(2,1)}, bf16[2,2,2,64,2048]{4,3,2,1,0:T(8,128)(2,1)}) custom-call(bf16[256,2304]{1,0:T(8,128)(2,1)} %pad_maximum_fusion.refs_0_.refs_3_, bf16[256,2304]{1,0:T(8,128)(2,1)} %copy-done.27, ...), custom_call_target="tpu_custom_call" | custom-call | flops 1 | bytes 1 | tf_op jit(solution)/shard_map/gather_mlp/pallas_call | solution.py:132
  223.3 53.2 %mlp.1 = (bf16[1024,768]{1,0:T(8,128)(2,1)}, bf16[2048,768]{1,0:T(8,128)(2,1)}, bf16[2,256,768]{2,1,0:T(8,128)(2,1)}, bf16[2,2,256,768]{3,2,1,0:T(8,128)(2,1)}, ...) custom-call(bf16[1024,2048]{1,0:T(8,128)(2,1)} %bitcast.75, bf16[2,256,2048]{2,1,0:T(8,128)(2,1)} %bitcast.77, ...), custom_call_target="tpu_custom_call" | custom-call | flops 1 | bytes 1 | tf_op jit(solution)/shard_map/mlp/pallas_call | solution.py:132
  276.5 1.4 copy-done.5
  277.9 1.1 copy-done.6
  279.0 1.4 copy-done.12
  280.4 43.3 %sum_mlp_back.1 = (bf16[256,768]{1,0:T(8,128)(2,1)S(1)}, bf16[2,256,768]{2,1,0:T(8,128)(2,1)S(1)}, f32[2,64,2048]{2,1,0:T(8,128)S(1)}, bf16[1024,2048]{1,0:T(8,128)(2,1)}) custom-call(bf16[2,256,768]{2,1,0:T(8,128)(2,1)S(1)} %copy-done.6, bf16[2,2,256,768]{3,2,1,0:T(8,128)(2,1)S(1)} %copy-done.5, bf16[2,2,2,2,64,2048]{5,4,3,2,1,0:T(8,128)(2,1)} %bitcast.76, ...), custom_call_target="tpu_custom_call" | custom-call | flops 1 | bytes 1 | tf_op jit(solution)/shard_map/sum_mlp_back/pallas_call | solution.py:132
  325.8 22.5 %gather_branch.1 = (bf16[256,768]{1,0:T(8,128)(2,1)S(1)}, bf16[2,256,768]{2,1,0:T(8,128)(2,1)S(1)}, bf16[2,2,2,64,2048]{4,3,2,1,0:T(8,128)(2,1)S(1)}) custom-call(bf16[2,256,768]{2,1,0:T(8,128)(2,1)S(1)} %fusion.refs_0_.sums, bf16[2,2,256,768]{3,2,1,0:T(8,128)(2,1)S(1)} %copy-done.4, bf16[2,64,2048]{2,1,0:T(8,128)(2,1)S(1)} %fusion.20.refs_2_), custom_call_target="tpu_custom_call" | custom-call | flops 1 | bytes 1 | tf_op jit(solution)/shard_map/gather_branch/pallas_call | solution.py:132
  348.5 1.3 convolution_convert_fusion.2.refs_4_
  349.9 47.8 %attend_back.1 = (bf16[256,768]{1,0:T(8,128)(2,1)S(1)}, f32[512,512]{1,0:T(8,128)S(1)}, f32[512,512]{1,0:T(8,128)S(1)}, f32[2,64,2048]{2,1,0:T(8,128)S(1)}) custom-call(bf16[2,256,768]{2,1,0:T(8,128)(2,1)S(1)} %fusion.1.refs_0_.sums, s32[1]{0:T(128)} %dynamic_slice.56.refs_0_.refs_1_, bf16[512,512]{1,0:T(8,128)(2,1)S(1)} %copy-done.9, ...), custom_call_target="tpu_custom_call" | custom-call | flops 1 | bytes 1 | tf_op jit(solution)/shard_map/attend_back/pallas_call | solution.py:132
  397.8 4.5 heads_backward.1
  402.4 4.5 attention_grads.1
  406.8 2.7 copy-done
  410.5 4.9 convolution_convert_fusion
  415.4 20.3 %sum_attention_back.1 = f32[2,64,2048]{2,1,0:T(8,128)S(1)} custom-call(bf16[2,2,2,64,2048]{4,3,2,1,0:T(8,128)(2,1)S(1)} %bitcast.66), custom_call_target="tpu_custom_call" | custom-call | flops 1 | bytes 1 | tf_op jit(solution)/shard_map/sum_attention_back/pallas_call | solution.py:132
  435.8 1.3 write_gate.1
  437.1 1.3 write_up.1
  440.2 1.4 write_down.1
  441.6 42.1 %sum_gains.1 = (bf16[64,2048]{1,0:T(8,128)(2,1)S(1)}, f32[40,128]{1,0:T(8,128)S(1)}) custom-call(bf16[64,2048]{1,0:T(8,128)(2,1)S(1)} %fusion.16.refs_0_, f32[40,128]{1,0:T(8,128)S(1)} %fusion.19.refs_1_), custom_call_target="tpu_custom_call" | custom-call | flops 1 | bytes 1 | tf_op jit(solution)/shard_map/sum_gains/pallas_call | solution.py:132
  487.0 11.9 %reduce-scatter.2.cloned.1.call-done.sums = bf16[256,1536]{1,0:T(8,128)(2,1)} async-done(((bf16[2048,1536]{1,0:T(8,128)(2,1)}), bf16[256,1536]{1,0:T(8,128)(2,1)}) %reduce-scatter.2.cloned.1.call-update) | async-done | bytes 786448 | tf_op jit(solution)/shard_map/reduce_scatter | solution.py:1521
  498.8 1.1 copy-done.16
  499.9 1.2 write_attention.1
  (138 shorter events, 16.9 us)
Async XLA Ops:
  7.2 31.4 %copy-start.38 = (bf16[2,64,2048]{2,1,0:T(8,128)(2,1)S(1)}, bf16[2,64,2048]{2,1,0:T(8,128)(2,1)}, u32[]{:S(2)}) copy-start(bf16[2,64,2048]{2,1,0:T(8,128)(2,1)} %param.14) | copy-start | bytes 1572868
  7.2 3.1 copy-start.40
  7.2 3.1 copy-start.41
  7.2 63.1 %all-gather.3.cloned.1.call-start = ((), (), s32[]{:S(2)}) async-start(), calls=%async_computation.1 | async-start | bytes 4718592 | tf_op jit(solution)/shard_map/all_gather | solution.py:1429
  9.3 113.9 %all-gather.5.cloned.1.call-start = ((), (), s32[]{:S(2)}) async-start(), calls=%async_computation.2 | async-start | bytes 2359296 | tf_op jit(solution)/shard_map/all_gather | solution.py:1436
  38.4 460.4 %reduce-scatter.2.cloned.1.call-start = ((), (), s32[]{:S(2)}) async-start(), calls=%async_computation.3 | async-start | bytes 7077888 | tf_op jit(solution)/shard_map/reduce_scatter | solution.py:1521
  38.6 129.3 %copy-start.28 = (bf16[1,64,2048]{2,1,0:T(8,128)(2,1)}, bf16[1,64,2048]{2,1,0:T(8,128)(2,1)S(1)}, u32[]{:S(2)}) copy-start(bf16[1,64,2048]{2,1,0:T(8,128)(2,1)S(1)} %get-tuple-element.123) | copy-start | bytes 786436
  38.6 129.3 %copy-start.30 = (bf16[1,64,2048]{2,1,0:T(8,128)(2,1)}, bf16[1,64,2048]{2,1,0:T(8,128)(2,1)S(1)}, u32[]{:S(2)}) copy-start(bf16[1,64,2048]{2,1,0:T(8,128)(2,1)S(1)} %get-tuple-element.124) | copy-start | bytes 786436
  38.7 18.6 %copy-start.36 = (bf16[1536,256]{1,0:T(8,128)(2,1)S(1)}, bf16[1536,256]{1,0:T(8,128)(2,1)}, u32[]{:S(2)}) copy-start(bf16[1536,256]{1,0:T(8,128)(2,1)} %param.26) | copy-start | bytes 2359300
  59.6 8.4 %copy-start.43 = (s32[2]{0:T(128)S(1)}, s32[2]{0:T(128)}, u32[]{:S(2)}) copy-start(s32[2]{0:T(128)} %param.15) | copy-start | bytes 28
  59.6 9.8 %copy-start.39 = (bf16[2,64,2048]{2,1,0:T(8,128)(2,1)S(1)}, bf16[2,64,2048]{2,1,0:T(8,128)(2,1)}, u32[]{:S(2)}) copy-start(bf16[2,64,2048]{2,1,0:T(8,128)(2,1)} %param.27) | copy-start | bytes 1572868
  61.8 107.5 %collective-permute-start = (bf16[256,2304]{1,0:T(8,128)(2,1)}, bf16[256,2304]{1,0:T(8,128)(2,1)S(1)}, u32[]{:S(2)}, u32[]{:S(2)}) collective-permute-start(bf16[256,2304]{1,0:T(8,128)(2,1)} %pad_maximum_fusion.1), channel_id=1, source_target_pairs={{0,16},{4,20},{8,24},{12,28},{16,0},{20,4},{24,8},{28,12},{1,17},{... | collective-permute-start | bytes 3538952 | tf_op jit(solution)/shard_map/ppermute | solution.py:1441
  123.1 100.2 %collective-permute-start.1 = (bf16[256,2304]{1,0:T(8,128)(2,1)}, bf16[256,2304]{1,0:T(8,128)(2,1)}, u32[]{:S(2)}, u32[]{:S(2)}) collective-permute-start(bf16[256,2304]{1,0:T(8,128)(2,1)} %pad_maximum_fusion.refs_0_.refs_3_), channel_id=1, source_target_pairs={{0,8},{4,12},{8,0},{12,4},{16,24},{20,28},{24,16},{28,20},{1,9},{5... | collective-permute-start | bytes 3538952 | tf_op jit(solution)/shard_map/ppermute | solution.py:1455
  123.2 3.1 copy-start.3
  168.2 155.5 %copy-start.24 = (f32[2,64,2048]{2,1,0:T(8,128)}, f32[2,64,2048]{2,1,0:T(8,128)S(1)}, u32[]{:S(2)}) copy-start(f32[2,64,2048]{2,1,0:T(8,128)S(1)} %get-tuple-element.118.refs_8_) | copy-start | bytes 3145732
  170.3 52.9 %copy-start.11 = (bf16[2,64,2048]{2,1,0:T(8,128)(2,1)S(1)}, bf16[2,64,2048]{2,1,0:T(8,128)(2,1)}, u32[]{:S(2)}) copy-start(bf16[2,64,2048]{2,1,0:T(8,128)(2,1)} %copy-done.10) | copy-start | bytes 1572868
  223.3 101.0 %copy-start.32 = (bf16[1,64,2048]{2,1,0:T(8,128)(2,1)}, bf16[1,64,2048]{2,1,0:T(8,128)(2,1)S(1)}, u32[]{:S(2)}) copy-start(bf16[1,64,2048]{2,1,0:T(8,128)(2,1)S(1)} %get-tuple-element.121) | copy-start | bytes 786436
  223.3 101.0 %copy-start.34 = (bf16[1,64,2048]{2,1,0:T(8,128)(2,1)}, bf16[1,64,2048]{2,1,0:T(8,128)(2,1)S(1)}, u32[]{:S(2)}) copy-start(bf16[1,64,2048]{2,1,0:T(8,128)(2,1)S(1)} %get-tuple-element.122) | copy-start | bytes 786436
  325.8 22.7 %copy-start.42 = (bf16[2048,512]{0,1:T(8,128)(2,1)S(1)}, bf16[2048,512]{0,1:T(8,128)(2,1)}, u32[]{:S(2)}) copy-start(bf16[2048,512]{0,1:T(8,128)(2,1)} %all-gather.5.cloned.1.call-done) | copy-start | bytes 6291460
  349.8 47.9 %copy-start.8 = (f32[512,1024]{1,0:T(8,128)S(1)}, f32[512,1024]{1,0:T(8,128)}, u32[]{:S(2)}) copy-start(f32[512,1024]{1,0:T(8,128)} %get-tuple-element.95.raw) | copy-start | bytes 6291460
  349.8 47.9 %copy-start.21 = (f32[128]{0:T(128)S(1)}, f32[128]{0:T(128)}, u32[]{:S(2)}) copy-start(f32[128]{0:T(128)} %param.20) | copy-start | bytes 1540
  349.9 47.9 %copy-start.22 = (f32[128]{0:T(128)S(1)}, f32[128]{0:T(128)}, u32[]{:S(2)}) copy-start(f32[128]{0:T(128)} %param.21) | copy-start | bytes 1540
  349.9 47.9 %copy-start.23 = (f32[1,128]{1,0:T(1,128)S(1)}, f32[1,128]{1,0:T(1,128)}, u32[]{:S(2)}) copy-start(f32[1,128]{1,0:T(1,128)} %broadcast_in_dim_tile.5.frequency) | copy-start | bytes 1540
  397.7 4.6 copy-start.14
  397.7 4.6 copy-start.18
  397.8 4.6 copy-start.2
  397.8 4.6 copy-start.17
  406.8 2.7 copy-start
  435.7 2.8 copy-start.29
  435.8 2.8 copy-start.31
  437.1 1.9 copy-start.35
  441.6 44.4 %copy-start.15 = (f32[2,64,2048]{2,1,0:T(8,128)S(1)}, f32[2,64,2048]{2,1,0:T(8,128)}, u32[]{:S(2)}) copy-start(f32[2,64,2048]{2,1,0:T(8,128)} %copy-done.14) | copy-start | bytes 3145732
  (17 other events, 22.5 us)
Sparse Core Ops, SparseCore 0:
  10.2 49.6 all-gather.2
  61.5 59.8 all-gather.4
  410.6 88.1 reduce-scatter.1

commit v5 on v4

--- a/solution.py
+++ b/solution.py
@@ -1180,7 +1180,7 @@
     count = 2 * len(shared) + len(alone)
     blocks, refs = refs[:count], refs[count:]
     inner, out_weights, down, gate, up, grad_rows, refs = *refs[:6], refs[6:]
-    weights, cot, grad_pre, keep_down, give_down, got_down, keep, give, got, *refs = refs
+    pre, weights, cot, grad_pre, keep_down, give_down, got_down, keep, give, got, *refs = refs
     *far_down, weight_sems, over_sems, cot_sems, core_sems, chip_sems = refs
     core, mate = lax.rem(lax.axis_index("seq"), 2), peer_of("core")
     depth, chips = blocks[0].shape[0], keep.shape[0]
@@ -1230,26 +1230,36 @@
     tile = 512
     tiles = rows.shape[0] // tile
 
-    def one(t, carry):
+    def cuts(t):
         here = pl.ds(pl.multiple_of(lax.rem(t, tiles) * tile, tile), tile)
-        first = pl.multiple_of((t // tiles) * step, step)
-        cols = pl.ds(first, step)
+        return here, pl.multiple_of((t // tiles) * step, step)
+
+    def forward(t, carry):
+        here, first = cuts(t)
+        cols, more = pl.ds(first, step), pl.ds(units + first, step)
         x = rows[here, :]
         gate_pre = nn(x, weights[:, cols])
-        up_pre = nn(x, weights[:, pl.ds(units + first, step)])
+        up_pre = nn(x, weights[:, more])
+        pre[here, cols] = gate_pre
+        pre[here, more] = up_pre
+        inner[here, cols] = (gate_pre * jax.nn.sigmoid(gate_pre) * up_pre).astype(BF16)
+        return carry
+
+    def backward(t, carry):
+        here, first = cuts(t)
+        cols, more = pl.ds(first, step), pl.ds(units + first, step)
+        gate_pre, up_pre = pre[here, cols], pre[here, more]
         grad = nn(cot[here, :], weights[:, pl.ds(2 * units + first, step)])
         sigmoid = jax.nn.sigmoid(gate_pre)
-        silu = gate_pre * sigmoid
-        inner[here, cols] = (silu * up_pre).astype(BF16)
         grad_gate = grad * up_pre * sigmoid * (1.0 + gate_pre * (1.0 - sigmoid))
         grad_pre[here, cols] = grad_gate.astype(BF16)
-        grad_pre[here, pl.ds(units + first, step)] = (grad * silu).astype(BF16)
+        grad_pre[here, more] = (grad * gate_pre * sigmoid).astype(BF16)
         return carry
 
-    lax.fori_loop(0, tiles * (units // step), one, 0)
+    lax.fori_loop(0, tiles * (units // step), forward, 0)
     weight_grads(cot, inner, keep_down, give_down)
     over_down = send(give_down, got_down, core_sems.at[0, 0], core_sems.at[0, 1], mate)
-    weight_grads(rows, grad_pre, keep, give, 0, chips)
+    lax.fori_loop(0, tiles * (units // step), backward, 0)
     over_down.wait()
 
     def add_down(t, carry):
@@ -1268,7 +1278,7 @@
         )
         for k in range(1, chips)
     ]
-    weight_grads(rows, grad_pre, keep, give, chips, None)
+    weight_grads(rows, grad_pre, keep, give)
     over_pre = send(give, got, core_sems.at[1, 0], core_sems.at[1, 1], mate)
 
     def two(t, carry):
@@ -1320,6 +1330,7 @@
         [VMEM, ANY, ANY] + [ANY] * len(blocks),
         [VMEM] * 6,
         [
+            pltpu.VMEM((tokens, 2 * units), F32),
             pltpu.VMEM((width, columns), BF16),
             pltpu.VMEM((tokens, width), BF16),
             pltpu.VMEM((tokens, 2 * units), BF16),

time: 517 us -> 515 us (level)
  transfers between devices with their start and end apart: 5 -> 5, of which waited for: 1 -> 1; matrix products, arithmetic and copies ran while one was open for 4% -> 4% of each run, Pallas kernels for 51% -> 50%
where the time goes in v5:
time: 515 us; the launch traced here: 506 us
  Pallas kernels  433 us (84%)
  local copies, waits for them, and re-layouts  19 us (4%)
  between operations  14.9 us (3%)
  waiting for transfers between devices  12 us (2%)
  other arithmetic  11.1 us (2%)
  matrix products  9.24 us (2%)
  starting transfers between devices  6.43 us (1%)
    pallas_call x11, Pallas kernels, carried_call(): pl.pallas_call(body, name=name, cost_estimate=NO_COST, out_shape=[jax.Sha...  410 us
    unnamed x90, local copies, waits for them, and re-layouts  14.2 us
    reduce_scatter x1, waiting for transfers between devices, shards(): lax.psum_scatter(grad_w_attn, 'seq', scatter_dimension=0, tiled=True)  11.9 us
  transfers between devices with their start and end apart: 5, of which 1 were waited for; matrix products, arithmetic and copies ran while one was open for 4% of the time, Pallas kernels for 50%

profile of v5, /device:TPU:9, one launch (start us, length us, event | category | flops | bytes accessed | tf_op | source)
XLA Modules:
  0.0 505.7 jit_solution(3494023403377174211)
XLA Ops:
  7.3 2.0 pad_maximum_fusion.4
  10.4 28.0 %gather_gains.1 = (bf16[64,2048]{1,0:T(8,128)(2,1)S(1)}, f32[4,8,8,128]{3,2,1,0:T(8,128)S(1)}) custom-call(bf16[64,2048]{1,0:T(8,128)(2,1)S(1)} %dynamic-slice_bitcast_fusion.refs_0_, f32[8,128]{1,0:T(8,128)S(1)} %select_maximum_fusion.2.refs_1_), custom_call_target="tpu_custom_call" | custom-call | flops 1 | bytes 1 | tf_op jit(solution)/shard_map/gather_gains/pallas_call | solution.py:132
  39.1 16.8 %gather_inputs.1 = bf16[2,2,2,64,2048]{4,3,2,1,0:T(8,128)(2,1)S(1)} custom-call(bf16[2,64,2048]{2,1,0:T(8,128)(2,1)S(1)} %fusion.6.refs_0_), custom_call_target="tpu_custom_call" | custom-call | flops 1 | bytes 1 | tf_op jit(solution)/shard_map/gather_inputs/pallas_call | solution.py:132
  55.9 1.4 copy-done.1
  58.4 1.2 constant_dynamic-slice_fusion.1
  61.8 6.2 %collective-permute-start = (bf16[256,2304]{1,0:T(8,128)(2,1)}, bf16[256,2304]{1,0:T(8,128)(2,1)S(1)}, u32[]{:S(2)}, u32[]{:S(2)}) collective-permute-start(bf16[256,2304]{1,0:T(8,128)(2,1)} %pad_maximum_fusion.1), channel_id=1, source_target_pairs={{0,16},{4,20},{8,24},{12,28},{16,0},{20,4},{24,8},{28,12},{1,17},{... | collective-permute-start | bytes 3538952 | tf_op jit(solution)/shard_map/ppermute | solution.py:1452
  70.3 8.9 %heads_forward.1 = (f32[512,1024]{1,0:T(8,128)}, bf16[512,512]{1,0:T(8,128)(2,1)}, bf16[512,512]{1,0:T(8,128)(2,1)}) custom-call(bf16[512,2048]{1,0:T(8,128)(2,1)} %bitcast.63, bf16[2048,1024]{1,0:T(8,128)(2,1)} %all-gather.3.cloned.1.call-done.w, f32[1,128]{1,0:T(1,128)} %broadcast_in_dim_tile.5.frequency, f32[1,128]{1,0:T(1,128)} %bitcast.69, ...), custom_call_target="tpu_custom_call" | custom-call | flops 1 | bytes 1 | tf_op jit(solution)/shard_map/heads_forward/pallas_call | solution.py:661
  79.2 43.8 %attend.1 = (f32[512,512]{1,0:T(8,128)}, bf16[512,512]{1,0:T(8,128)(2,1)}, f32[4,1,512]{2,1,0:T(1,128)}, bf16[4,512,512]{2,1,0:T(8,128)(2,1)}, bf16[2,2,2,64,2048]{4,3,2,1,0:T(8,128)(2,1)}) custom-call(s32[1]{0:T(128)} %dynamic_slice.56.refs_0_.refs_1_, bf16[512,512]{1,0:T(8,128)(2,1)} %get-tuple-element.67.refs_1_.refs_2_, ...), custom_call_target="tpu_custom_call" | custom-call | flops 1 | bytes 1 | tf_op jit(solution)/shard_map/attend/pallas_call | solution.py:132
  123.2 3.1 convolution_convert_fusion.1
  126.3 41.6 %sum_attention.1 = (bf16[2,64,2048]{2,1,0:T(8,128)(2,1)S(1)}, f32[2,64,2048]{2,1,0:T(8,128)S(1)}) custom-call(bf16[2,64,2048]{2,1,0:T(8,128)(2,1)S(1)} %copy-done.3, bf16[2,2,2,64,2048]{4,3,2,1,0:T(8,128)(2,1)S(1)} %bitcast.65), custom_call_target="tpu_custom_call" | custom-call | flops 1 | bytes 1 | tf_op jit(solution)/shard_map/sum_attention/pallas_call | solution.py:132
  168.1 1.1 multiply_convert_fusion.refs_3_
  170.3 52.9 %gather_mlp.1 = (bf16[256,2304]{1,0:T(8,128)(2,1)}, bf16[256,2304]{1,0:T(8,128)(2,1)}, bf16[256,2304]{1,0:T(8,128)(2,1)}, bf16[2,2,2,2,64,2048]{5,4,3,2,1,0:T(8,128)(2,1)}, bf16[2,2,2,64,2048]{4,3,2,1,0:T(8,128)(2,1)}) custom-call(bf16[256,2304]{1,0:T(8,128)(2,1)} %pad_maximum_fusion.refs_0_.refs_3_, bf16[256,2304]{1,0:T(8,128)(2,1)} %copy-done.27, ...), custom_call_target="tpu_custom_call" | custom-call | flops 1 | bytes 1 | tf_op jit(solution)/shard_map/gather_mlp/pallas_call | solution.py:132
  223.3 50.7 %mlp.1 = (bf16[1024,768]{1,0:T(8,128)(2,1)}, bf16[2048,768]{1,0:T(8,128)(2,1)}, bf16[2,256,768]{2,1,0:T(8,128)(2,1)}, bf16[2,2,256,768]{3,2,1,0:T(8,128)(2,1)}, ...) custom-call(bf16[1024,2048]{1,0:T(8,128)(2,1)} %bitcast.75, bf16[2,256,2048]{2,1,0:T(8,128)(2,1)} %bitcast.77, ...), custom_call_target="tpu_custom_call" | custom-call | flops 1 | bytes 1 | tf_op jit(solution)/shard_map/mlp/pallas_call | solution.py:132
  274.0 1.4 copy-done.5
  275.4 1.1 copy-done.6
  276.5 1.4 copy-done.12
  277.9 43.3 %sum_mlp_back.1 = (bf16[256,768]{1,0:T(8,128)(2,1)S(1)}, bf16[2,256,768]{2,1,0:T(8,128)(2,1)S(1)}, f32[2,64,2048]{2,1,0:T(8,128)S(1)}, bf16[1024,2048]{1,0:T(8,128)(2,1)}) custom-call(bf16[2,256,768]{2,1,0:T(8,128)(2,1)S(1)} %copy-done.6, bf16[2,2,256,768]{3,2,1,0:T(8,128)(2,1)S(1)} %copy-done.5, bf16[2,2,2,2,64,2048]{5,4,3,2,1,0:T(8,128)(2,1)} %bitcast.76, ...), custom_call_target="tpu_custom_call" | custom-call | flops 1 | bytes 1 | tf_op jit(solution)/shard_map/sum_mlp_back/pallas_call | solution.py:132
  323.4 22.3 %gather_branch.1 = (bf16[256,768]{1,0:T(8,128)(2,1)S(1)}, bf16[2,256,768]{2,1,0:T(8,128)(2,1)S(1)}, bf16[2,2,2,64,2048]{4,3,2,1,0:T(8,128)(2,1)S(1)}) custom-call(bf16[2,256,768]{2,1,0:T(8,128)(2,1)S(1)} %fusion.refs_0_.sums, bf16[2,2,256,768]{3,2,1,0:T(8,128)(2,1)S(1)} %copy-done.4, bf16[2,64,2048]{2,1,0:T(8,128)(2,1)S(1)} %fusion.20.refs_2_), custom_call_target="tpu_custom_call" | custom-call | flops 1 | bytes 1 | tf_op jit(solution)/shard_map/gather_branch/pallas_call | solution.py:132
  345.9 1.3 convolution_convert_fusion.2.refs_4_
  347.3 52.9 %attend_back.1 = (bf16[256,768]{1,0:T(8,128)(2,1)S(1)}, f32[512,512]{1,0:T(8,128)S(1)}, f32[512,512]{1,0:T(8,128)S(1)}, f32[2,64,2048]{2,1,0:T(8,128)S(1)}) custom-call(bf16[2,256,768]{2,1,0:T(8,128)(2,1)S(1)} %fusion.1.refs_0_.sums, s32[1]{0:T(128)} %dynamic_slice.56.refs_0_.refs_1_, bf16[512,512]{1,0:T(8,128)(2,1)S(1)} %copy-done.9, ...), custom_call_target="tpu_custom_call" | custom-call | flops 1 | bytes 1 | tf_op jit(solution)/shard_map/attend_back/pallas_call | solution.py:132
  400.3 4.5 heads_backward.1
  404.8 4.5 attention_grads.1
  409.3 2.7 copy-done
  413.0 4.9 convolution_convert_fusion
  417.9 17.4 %sum_attention_back.1 = f32[2,64,2048]{2,1,0:T(8,128)S(1)} custom-call(bf16[2,2,2,64,2048]{4,3,2,1,0:T(8,128)(2,1)S(1)} %bitcast.66), custom_call_target="tpu_custom_call" | custom-call | flops 1 | bytes 1 | tf_op jit(solution)/shard_map/sum_attention_back/pallas_call | solution.py:132
  435.3 1.3 write_gate.1
  436.7 1.3 write_up.1
  439.8 1.4 write_down.1
  441.2 40.1 %sum_gains.1 = (bf16[64,2048]{1,0:T(8,128)(2,1)S(1)}, f32[40,128]{1,0:T(8,128)S(1)}) custom-call(bf16[64,2048]{1,0:T(8,128)(2,1)S(1)} %fusion.16.refs_0_, f32[40,128]{1,0:T(8,128)S(1)} %fusion.19.refs_1_), custom_call_target="tpu_custom_call" | custom-call | flops 1 | bytes 1 | tf_op jit(solution)/shard_map/sum_gains/pallas_call | solution.py:132
  484.5 11.9 %reduce-scatter.2.cloned.1.call-done.sums = bf16[256,1536]{1,0:T(8,128)(2,1)} async-done(((bf16[2048,1536]{1,0:T(8,128)(2,1)}), bf16[256,1536]{1,0:T(8,128)(2,1)}) %reduce-scatter.2.cloned.1.call-update) | async-done | bytes 786448 | tf_op jit(solution)/shard_map/reduce_scatter | solution.py:1532
  496.4 1.1 copy-done.16
  497.5 1.2 write_attention.1
  (138 shorter events, 16.9 us)
Async XLA Ops:
  7.2 31.4 %copy-start.38 = (bf16[2,64,2048]{2,1,0:T(8,128)(2,1)S(1)}, bf16[2,64,2048]{2,1,0:T(8,128)(2,1)}, u32[]{:S(2)}) copy-start(bf16[2,64,2048]{2,1,0:T(8,128)(2,1)} %param.14) | copy-start | bytes 1572868
  7.2 3.1 copy-start.40
  7.2 3.1 copy-start.41
  7.2 63.1 %all-gather.3.cloned.1.call-start = ((), (), s32[]{:S(2)}) async-start(), calls=%async_computation.1 | async-start | bytes 4718592 | tf_op jit(solution)/shard_map/all_gather | solution.py:1440
  9.3 113.9 %all-gather.5.cloned.1.call-start = ((), (), s32[]{:S(2)}) async-start(), calls=%async_computation.2 | async-start | bytes 2359296 | tf_op jit(solution)/shard_map/all_gather | solution.py:1447
  38.4 458.0 %reduce-scatter.2.cloned.1.call-start = ((), (), s32[]{:S(2)}) async-start(), calls=%async_computation.3 | async-start | bytes 7077888 | tf_op jit(solution)/shard_map/reduce_scatter | solution.py:1532
  38.6 129.3 %copy-start.28 = (bf16[1,64,2048]{2,1,0:T(8,128)(2,1)}, bf16[1,64,2048]{2,1,0:T(8,128)(2,1)S(1)}, u32[]{:S(2)}) copy-start(bf16[1,64,2048]{2,1,0:T(8,128)(2,1)S(1)} %get-tuple-element.123) | copy-start | bytes 786436
  38.6 129.3 %copy-start.30 = (bf16[1,64,2048]{2,1,0:T(8,128)(2,1)}, bf16[1,64,2048]{2,1,0:T(8,128)(2,1)S(1)}, u32[]{:S(2)}) copy-start(bf16[1,64,2048]{2,1,0:T(8,128)(2,1)S(1)} %get-tuple-element.124) | copy-start | bytes 786436
  38.7 18.6 %copy-start.36 = (bf16[1536,256]{1,0:T(8,128)(2,1)S(1)}, bf16[1536,256]{1,0:T(8,128)(2,1)}, u32[]{:S(2)}) copy-start(bf16[1536,256]{1,0:T(8,128)(2,1)} %param.26) | copy-start | bytes 2359300
  59.6 8.4 %copy-start.43 = (s32[2]{0:T(128)S(1)}, s32[2]{0:T(128)}, u32[]{:S(2)}) copy-start(s32[2]{0:T(128)} %param.15) | copy-start | bytes 28
  59.6 9.8 %copy-start.39 = (bf16[2,64,2048]{2,1,0:T(8,128)(2,1)S(1)}, bf16[2,64,2048]{2,1,0:T(8,128)(2,1)}, u32[]{:S(2)}) copy-start(bf16[2,64,2048]{2,1,0:T(8,128)(2,1)} %param.27) | copy-start | bytes 1572868
  61.8 107.5 %collective-permute-start = (bf16[256,2304]{1,0:T(8,128)(2,1)}, bf16[256,2304]{1,0:T(8,128)(2,1)S(1)}, u32[]{:S(2)}, u32[]{:S(2)}) collective-permute-start(bf16[256,2304]{1,0:T(8,128)(2,1)} %pad_maximum_fusion.1), channel_id=1, source_target_pairs={{0,16},{4,20},{8,24},{12,28},{16,0},{20,4},{24,8},{28,12},{1,17},{... | collective-permute-start | bytes 3538952 | tf_op jit(solution)/shard_map/ppermute | solution.py:1452
  123.0 100.2 %collective-permute-start.1 = (bf16[256,2304]{1,0:T(8,128)(2,1)}, bf16[256,2304]{1,0:T(8,128)(2,1)}, u32[]{:S(2)}, u32[]{:S(2)}) collective-permute-start(bf16[256,2304]{1,0:T(8,128)(2,1)} %pad_maximum_fusion.refs_0_.refs_3_), channel_id=1, source_target_pairs={{0,8},{4,12},{8,0},{12,4},{16,24},{20,28},{24,16},{28,20},{1,9},{5... | collective-permute-start | bytes 3538952 | tf_op jit(solution)/shard_map/ppermute | solution.py:1466
  123.2 3.1 copy-start.3
  168.1 153.1 %copy-start.24 = (f32[2,64,2048]{2,1,0:T(8,128)}, f32[2,64,2048]{2,1,0:T(8,128)S(1)}, u32[]{:S(2)}) copy-start(f32[2,64,2048]{2,1,0:T(8,128)S(1)} %get-tuple-element.118.refs_8_) | copy-start | bytes 3145732
  170.3 52.9 %copy-start.11 = (bf16[2,64,2048]{2,1,0:T(8,128)(2,1)S(1)}, bf16[2,64,2048]{2,1,0:T(8,128)(2,1)}, u32[]{:S(2)}) copy-start(bf16[2,64,2048]{2,1,0:T(8,128)(2,1)} %copy-done.10) | copy-start | bytes 1572868
  223.3 98.5 %copy-start.32 = (bf16[1,64,2048]{2,1,0:T(8,128)(2,1)}, bf16[1,64,2048]{2,1,0:T(8,128)(2,1)S(1)}, u32[]{:S(2)}) copy-start(bf16[1,64,2048]{2,1,0:T(8,128)(2,1)S(1)} %get-tuple-element.121) | copy-start | bytes 786436
  223.3 98.5 %copy-start.34 = (bf16[1,64,2048]{2,1,0:T(8,128)(2,1)}, bf16[1,64,2048]{2,1,0:T(8,128)(2,1)S(1)}, u32[]{:S(2)}) copy-start(bf16[1,64,2048]{2,1,0:T(8,128)(2,1)S(1)} %get-tuple-element.122) | copy-start | bytes 786436
  323.4 22.6 %copy-start.42 = (bf16[2048,512]{0,1:T(8,128)(2,1)S(1)}, bf16[2048,512]{0,1:T(8,128)(2,1)}, u32[]{:S(2)}) copy-start(bf16[2048,512]{0,1:T(8,128)(2,1)} %all-gather.5.cloned.1.call-done) | copy-start | bytes 6291460
  347.2 53.0 %copy-start.8 = (f32[512,1024]{1,0:T(8,128)S(1)}, f32[512,1024]{1,0:T(8,128)}, u32[]{:S(2)}) copy-start(f32[512,1024]{1,0:T(8,128)} %get-tuple-element.95.raw) | copy-start | bytes 6291460
  347.3 53.0 %copy-start.21 = (f32[128]{0:T(128)S(1)}, f32[128]{0:T(128)}, u32[]{:S(2)}) copy-start(f32[128]{0:T(128)} %param.20) | copy-start | bytes 1540
  347.3 53.0 %copy-start.22 = (f32[128]{0:T(128)S(1)}, f32[128]{0:T(128)}, u32[]{:S(2)}) copy-start(f32[128]{0:T(128)} %param.21) | copy-start | bytes 1540
  347.3 53.0 %copy-start.23 = (f32[1,128]{1,0:T(1,128)S(1)}, f32[1,128]{1,0:T(1,128)}, u32[]{:S(2)}) copy-start(f32[1,128]{1,0:T(1,128)} %broadcast_in_dim_tile.5.frequency) | copy-start | bytes 1540
  400.2 4.6 copy-start.14
  400.2 4.6 copy-start.18
  400.3 4.6 copy-start.2
  400.3 4.6 copy-start.17
  409.3 2.7 copy-start
  435.3 2.8 copy-start.29
  435.3 2.8 copy-start.31
  436.7 1.9 copy-start.35
  441.2 42.4 %copy-start.15 = (f32[2,64,2048]{2,1,0:T(8,128)S(1)}, f32[2,64,2048]{2,1,0:T(8,128)}, u32[]{:S(2)}) copy-start(f32[2,64,2048]{2,1,0:T(8,128)} %copy-done.14) | copy-start | bytes 3145732
  (17 other events, 22.5 us)
Sparse Core Ops, SparseCore 0:
  10.2 49.6 all-gather.2
  61.5 59.8 all-gather.4
  413.1 83.2 reduce-scatter.1
